TPU v7x, 128 devices: a whole 4x4x4 slice. The times are simulated.
128 devices in a mesh: strip: 8 (over x, core), blk: 16 (over y, z).
Axes of the slice: x: 4, y: 4, z: 4, core: 2. Of those that a mesh axis runs over, the one named last changes fastest.
Arguments:
- krylov_start: float32 [4, 64, 2048], P(None, 'strip', 'blk'), may hold values from -5 to 6
- conductivity: float32 [4, 64, 2048], P(None, 'strip', 'blk'), may hold values from 0.1 to 1
- near_kernel: bfloat16 [6144, 3, 3, 128, 128], P(('strip', 'blk')), may hold values from -0.125 to 0.125
- near_pair: int32 [6144], P(('strip', 'blk')), may hold values from 0 to 71, as said below
- far_right: bfloat16 [128, 128, 32, 3, 128], P(('strip', 'blk')), may hold values from -1 to 1
- far_left: bfloat16 [128, 128, 32, 3, 128], P(('strip', 'blk')), may hold values from -1 to 1
- far_source_row: int32 [128, 128], P(('strip', 'blk')), may hold values from 0 to 7
- far_target_row: int32 [128, 128], P(('strip', 'blk')), may hold values from 0 to 7
Outputs:
- krylov_next: float32 [2, 4, 64, 2048], P(None, None, 'strip', 'blk')
- hessenberg: float32 [5], replicated
Inputs may be any that keep to these rules, and one draw needn't show every extreme that they name: `near_pair`: How many of them fall in one block row varies from row to row and device to device; a row holds at most 9. `far_source_row`: entry [g, d] belongs to the far pair owned by device g whose target block lies on device d. `far_target_row`: entry [g, d] is the target block row on device d of the far pair owned by g.
All inputs are finite; a program needn't handle non-finite values.
Results may differ from a plain program's by a relative error of at most 0.0022.
Values sent between devices are 32-bit elements; how exact they have to be, the bound alone decides.
No kernel may reach another device: no remote copies, remote signals or barrier semaphores. Data moves between devices by JAX's collectives and lax.ppermute only.
A program may use at most 64 MiB of HBM per device.

v0:
```python
import jax
import jax.numpy as jnp
from jax import lax
from jax.sharding import PartitionSpec as P

epsilon = 1e-06


def padded(shard, sides, width):
    for axis, dim in sides:
        devices, length = (lax.axis_size(axis), shard.shape[dim])
        up = [(i, (i + 1) % devices) for i in range(devices - 1)]
        down = [(j, i) for i, j in up]
        last = lax.slice_in_dim(shard, length - width, length, axis=dim)
        first = lax.slice_in_dim(shard, 0, width, axis=dim)
        before = lax.ppermute(last, axis, up)
        after = lax.ppermute(first, axis, down)
        shard = jnp.concatenate([before, shard, after], axis=dim)
    return shard


def local(
    krylov_start,
    conductivity,
    near_kernel,
    near_pair,
    far_right,
    far_left,
    far_source_row,
    far_target_row,
):
    row_blocks = krylov_start.shape[1]
    block_len = krylov_start.shape[2]
    entries = float(4 * row_blocks * block_len * lax.axis_size("strip") * lax.axis_size("blk"))
    row_ids = jnp.arange(row_blocks, dtype=jnp.int32)
    target_row = near_pair // 9
    neighbour = near_pair % 9
    source_index = (target_row + neighbour // 3) * 3 + neighbour % 3
    near_onehot = (target_row[:, None] == row_ids[None, :]).astype(jnp.float32)
    source_rows = far_source_row[0]
    far_targets = far_target_row[0]

    def apply_operator(vector):
        rimmed = padded(vector.reshape(4, row_blocks, 1, block_len), (("strip", 1), ("blk", 2)), 1)
        flattened = rimmed.reshape(4, (row_blocks + 2) * 3, block_len)
        near_source = jnp.take(flattened[0:3].astype(jnp.bfloat16), source_index, axis=1)
        products = jnp.einsum(
            "pabim,bpm->pai", near_kernel, near_source, preferred_element_type=jnp.float32
        )
        near_part = jnp.einsum(
            "pt,pai->ati", near_onehot, products, precision=lax.Precision.HIGHEST
        )
        displaced = vector[0:3].astype(jnp.bfloat16)
        far_source = jnp.take(displaced, source_rows, axis=1)
        coefficient = jnp.einsum(
            "drbm,bdm->dr", far_right[0], far_source, preferred_element_type=jnp.float32
        ).astype(jnp.bfloat16)
        pair_result = jnp.einsum(
            "drai,dr->dai", far_left[0], coefficient, preferred_element_type=jnp.float32
        )
        onehot = (far_targets[:, None] == row_ids[None, :]).astype(jnp.float32)
        far_part = lax.psum_scatter(
            jnp.einsum("dk,dai->daki", onehot, pair_result, precision=lax.Precision.HIGHEST),
            ("strip", "blk"),
            scatter_dimension=0,
            tiled=True,
        )[0]
        pressure = vector[3]
        rim_pressure = rimmed[3]
        north_side = rim_pressure[:-2, 1]
        south_side = rim_pressure[2:, 1]
        full_row = jnp.concatenate(
            [rim_pressure[1:-1, 0, -1:], pressure, rim_pressure[1:-1, 2, :1]], axis=1
        )
        west_side = full_row[:, :-2]
        east_side = full_row[:, 2:]
        flux_sum = conductivity[0] * (north_side - pressure) + conductivity[1] * (
            south_side - pressure
        )
        flux_sum = (
            flux_sum
            + conductivity[2] * (west_side - pressure)
            + conductivity[3] * (east_side - pressure)
        )
        elastic = vector[0:3] + near_part + far_part
        elastic = jnp.concatenate([elastic[0:1] - pressure[None], elastic[1:3]], axis=0)
        fluid = pressure + vector[0] - flux_sum
        return jnp.concatenate([elastic, fluid[None]], axis=0)

    def reduce_basis(image, basis):
        local_proj = jnp.stack([jnp.sum(vector * image) for vector in basis])
        proj_total = lax.psum(local_proj, ("strip", "blk"))
        coeffs = proj_total / entries
        remainder = image
        for position in range(len(basis)):
            remainder = remainder - coeffs[position] * basis[position]
        square_total = lax.psum(jnp.sum(remainder * remainder), ("strip", "blk"))
        norm_value = jnp.sqrt(square_total / entries + epsilon)
        return (remainder / norm_value, coeffs, norm_value)

    image = apply_operator(krylov_start)
    first_vector, first_coeffs, first_norm = reduce_basis(image, [krylov_start])
    image = apply_operator(first_vector)
    second_vector, second_coeffs, second_norm = reduce_basis(image, [krylov_start, first_vector])
    hessenberg = jnp.stack(
        [first_coeffs[0], first_norm, second_coeffs[0], second_coeffs[1], second_norm]
    )
    return (jnp.stack([first_vector, second_vector]), hessenberg)


def solution(mesh):
    in_specs = (
        P(None, "strip", "blk"),
        P(None, "strip", "blk"),
        P(("strip", "blk"), None, None, None, None),
        P(("strip", "blk")),
        P(("strip", "blk"), None, None, None, None),
        P(("strip", "blk"), None, None, None, None),
        P(("strip", "blk"), None),
        P(("strip", "blk"), None),
    )
    out_specs = (P(None, None, "strip", "blk"), P())
    return jax.shard_map(local, mesh=mesh, in_specs=in_specs, out_specs=out_specs, check_vma=False)
```

profile of v0, /device:TPU:1, one launch (start us, length us, event | category | flops | bytes accessed | tf_op | source)
XLA Modules:
  0.0 708.2 jit_solution(9139316706469975815)
XLA Ops:
  7.2 0.8 compare_and_fusion
  8.0 0.7 compare_select_fusion
  10.3 0.7 gather_fusion.1
  11.2 3.1 fusion.6
  15.1 1.4 multiply_bitcast_fusion.1
  16.5 4.5 collective-permute-start
  21.0 1.9 collective-permute-start.1
  23.0 2.9 collective-permute-done.1
  25.9 1.3 collective-permute-start.3
  27.2 4.2 collective-permute-start.2
  31.5 1.0 collective-permute-done.2
  33.3 9.3 %fusion.20 = f32[48,1,3,128,1]{3,1,4,2,0:T(1,128)S(1)} fusion(bf16[48,3,3,128,128]{4,3,2,1,0:T(8,128)(2,1)} %param.14, bf16[3,48,128,1,1]{2,0,1,3,4:T(4,128)(2,1)S(1)} %select_bitcast_fusion.3), kind=kOutput, calls=%fused_computation.36 | convolution fusion | flops 14155776 | bytes 14266368 | tf_op jit(solution)/shard_map/pabim,bpm->pai/dot_general | solution.py:47
  42.6 183.9 %reduce-scatter.7.cloned.1.call-done = f32[1,3,8,128]{3,2,1,0:T(8,128)} async-done(((f32[128,3,8,128]{3,2,1,0:T(8,128)}), f32[1,3,8,128]{3,2,1,0:T(8,128)}) %reduce-scatter.7.cloned.1.call-update) | async-done | bytes 12304
  226.5 0.9 fusion.11
  228.1 64.3 %psum.28 = f32[1]{0:T(128)} all-reduce(f32[1]{0:T(128)} %bitcast.31), channel_id=1, replica_groups=mesh['strip'=8,'blk'=16] {'strip','blk'}, use_global_device_ids=true, to_apply=%region_2.5 | all-reduce | flops 1 | bytes 8 | tf_op jit(solution)/shard_map/psum | solution.py:92
  293.7 62.5 %psum.29 = f32[]{:T(128)} all-reduce(f32[]{:T(128)} %multiply_reduce_fusion.3), channel_id=1, replica_groups=mesh['strip'=8,'blk'=16] {'strip','blk'}, use_global_device_ids=true, to_apply=%region_4.7 | all-reduce | flops 1 | bytes 8 | tf_op jit(solution)/shard_map/psum | solution.py:97
  356.9 0.7 gather_fusion.3
  357.9 3.1 fusion.4
  361.7 1.4 multiply_bitcast_fusion
  363.1 3.5 collective-permute-start.4
  366.6 1.9 collective-permute-start.5
  368.5 3.0 collective-permute-done.5
  371.5 1.3 collective-permute-start.7
  372.8 4.0 collective-permute-start.6
  376.8 1.0 collective-permute-done.6
  378.7 9.3 %fusion.17 = f32[48,1,3,128,1]{3,1,4,2,0:T(1,128)S(1)} fusion(bf16[48,3,3,128,128]{4,3,2,1,0:T(8,128)(2,1)} %param.14, bf16[3,48,128,1,1]{2,0,1,3,4:T(4,128)(2,1)S(1)} %select_bitcast_fusion.2), kind=kOutput, calls=%fused_computation.33 | convolution fusion | flops 14155776 | bytes 14266368 | tf_op jit(solution)/shard_map/pabim,bpm->pai/dot_general | solution.py:47
  388.0 179.1 %reduce-scatter.9.cloned.1.call-done = f32[1,3,8,128]{3,2,1,0:T(8,128)} async-done(((f32[128,3,8,128]{3,2,1,0:T(8,128)}), f32[1,3,8,128]{3,2,1,0:T(8,128)}) %reduce-scatter.9.cloned.1.call-update) | async-done | bytes 12304
  567.1 0.9 fusion.9
  568.7 1.4 pad_maximum_fusion.11
  570.1 64.2 %psum.30 = f32[2]{0:T(128)S(1)} all-reduce(f32[2]{0:T(128)S(1)} %pad_maximum_fusion.11), channel_id=1, replica_groups=mesh['strip'=8,'blk'=16] {'strip','blk'}, use_global_device_ids=true, to_apply=%region_8.11 | all-reduce | flops 2 | bytes 16 | tf_op jit(solution)/shard_map/psum | solution.py:92
  635.0 1.9 multiply_reduce_fusion
  637.0 62.5 %psum.31 = f32[]{:T(128)} all-reduce(f32[]{:T(128)} %get-tuple-element.6), channel_id=1, replica_groups=mesh['strip'=8,'blk'=16] {'strip','blk'}, use_global_device_ids=true, to_apply=%region_10.13 | all-reduce | flops 1 | bytes 8 | tf_op jit(solution)/shard_map/psum | solution.py:97
  (65 shorter events, 9.2 us)
Async XLA Ops:
  7.2 7.2 %copy-start = (bf16[1,128,32,3,128]{4,2,3,1,0:T(8,128)(2,1)S(1)}, bf16[1,128,32,3,128]{4,2,3,1,0:T(8,128)(2,1)}, u32[]{:S(2)}) copy-start(bf16[1,128,32,3,128]{4,2,3,1,0:T(8,128)(2,1)} %param.17) | copy-start | bytes 9437188
  7.2 219.3 %reduce-scatter.7.cloned.1.call-start = ((), (), s32[]{:S(2)}) async-start(), calls=%async_computation.2 | async-start | bytes 1585152
  14.3 2.2 copy-start.1
  14.3 8.6 %copy-start.3 = (s32[48]{0:T(128)S(1)}, s32[48]{0:T(128)}, u32[]{:S(2)}) copy-start(s32[48]{0:T(128)} %param.15) | copy-start | bytes 580
  16.4 550.6 %reduce-scatter.9.cloned.1.call-start = ((), (), s32[]{:S(2)}) async-start(), calls=%async_computation.3 | async-start | bytes 1585152
  16.5 6.5 collective-permute-start
  21.0 4.9 collective-permute-start.1
  25.9 5.5 collective-permute-start.3
  27.2 5.2 collective-permute-start.2
  33.3 194.0 %copy-start.2 = (f32[4,8,128]{2,1,0:T(8,128)S(1)}, f32[4,8,128]{2,1,0:T(8,128)}, u32[]{:S(2)}) copy-start(f32[4,8,128]{2,1,0:T(8,128)} %param.13) | copy-start | bytes 49156
  363.1 5.5 collective-permute-start.4
  366.6 4.9 collective-permute-start.5
  371.5 5.3 collective-permute-start.7
  372.8 5.0 collective-permute-start.6
Sparse Core Ops, SparseCore 0:
  16.6 209.8 reduce-scatter.6
  363.2 203.8 reduce-scatter.8
where the time goes:
time: 709 us; the launch traced here: 708 us
  waiting for transfers between devices  371 us (52%)
  blocking collectives  254 us (36%)
  matrix products  27.7 us (4%)
  starting transfers between devices  22.7 us (3%)
  between operations  16.5 us (2%)
  other arithmetic  12.4 us (2%)
    unnamed x4, waiting for transfers between devices  363 us
    psum x2, blocking collectives, reduce_basis(): proj_total = lax.psum(local_proj, ('strip', 'blk'))  129 us
    psum x2, blocking collectives, reduce_basis(): square_total = lax.psum(jnp.sum(remainder * remainder), ('strip', 'blk'))  125 us
    dot_general x2, matrix products, apply_operator(): jnp.einsum('pabim,bpm->pai', near_kernel, near_source, preferred_element_...  18.5 us
    ppermute x4, starting transfers between devices, padded(): before = lax.ppermute(last, axis, up)  16.2 us
  transfers between devices with their start and end apart: 10, of which 6 were waited for; matrix products, arithmetic and copies ran while one was open for 3% of the time, Pallas kernels for 0%

commit v1 on v0

v1 whole, which is shorter than its diff:
```python
import functools

import jax
import jax.numpy as jnp
from jax import lax
from jax.experimental import pallas as pl
from jax.experimental.pallas import tpu as pltpu
from jax.sharding import PartitionSpec as P

EPSILON = 1e-06
STRIPS, BLKS, DEVICES = 8, 16, 128
ROWS, LEN, RANK, PAIRS = 8, 128, 32, 48
ENTRIES = float(4 * STRIPS * ROWS * BLKS * LEN)
HALO = 32
NEAR_CHUNK = 4
NEAR_CHUNKS = PAIRS // NEAR_CHUNK
FAR_CHUNK = 8
FAR_CHUNKS = DEVICES // FAR_CHUNK
FAR_COPIES = 4
FAR_PER_COPY = DEVICES // FAR_COPIES
BF16, F32 = jnp.bfloat16, jnp.float32
TRANS_B = (((1,), (1,)), ((), ()))
PLAIN = (((1,), (0,)), ((), ()))
VMEM = pl.BlockSpec(memory_space=pltpu.VMEM)
SMEM = pl.BlockSpec(memory_space=pltpu.SMEM)
ANY = pl.BlockSpec(memory_space=pl.ANY)


def two_sum(a, b):
    s = a + b
    t = s - a
    return s, (a - (s - t)) + (b - t)


def halves(a):
    c = a * 4097.0
    hi = c - (c - a)
    return hi, a - hi


def two_prod(a, b):
    p = a * b
    ah, al = halves(a)
    bh, bl = halves(b)
    return p, ((ah * bh - p) + ah * bl + al * bh) + al * bl


def pair_add(x, y):
    s, e = two_sum(x[0], y[0])
    return two_sum(s, e + (x[1] + y[1]))


def pair_mul(x, y):
    p, e = two_prod(x[0], y[0])
    return two_sum(p, e + (x[0] * y[1] + x[1] * y[0]))


def neg(x):
    return -x[0], -x[1]


def scaled(x, power_of_two):
    return x[0] * power_of_two, x[1] * power_of_two


def dot_row(pairs):
    sub = lax.broadcasted_iota(jnp.int32, (8, LEN), 0)
    high = jnp.zeros((8, LEN), F32)
    low = jnp.zeros((8, LEN), F32)
    for k, (a, b) in enumerate(pairs):
        s, e = two_prod(a[0], b[0])
        for c in range(1, 4):
            s, e = pair_add((s, e), two_prod(a[c], b[c]))
        for step in (4, 2, 1):
            s, e = pair_add((s, e), (pltpu.roll(s, step, 0), pltpu.roll(e, step, 0)))
        high = jnp.where(sub == k, s, high)
        low = jnp.where(sub == k, e, low)
    pad = jnp.zeros((LEN - 16, LEN), F32)
    turned = jnp.concatenate([high, low, pad], axis=0).T
    s, e = column_sums(turned)
    return s + pltpu.roll(e, 16, 1)


def column_sums(x):
    parts = [(x[8 * i : 8 * i + 8], jnp.zeros((8, LEN), F32)) for i in range(16)]
    while len(parts) > 1:
        parts = [pair_add(parts[i], parts[i + 1]) for i in range(0, len(parts), 2)]
    s, e = parts[0]
    for step in (4, 2, 1):
        s, e = pair_add((s, e), (pltpu.roll(s, step, 0), pltpu.roll(e, step, 0)))
    return s[0:1], e[0:1]


def totals(rows, count):
    s, e = column_sums(rows)
    low = e + pltpu.roll(s, LEN - 8, 1) + pltpu.roll(s, LEN - 16, 1)
    s, low = two_sum(s, low)
    return [(s[0:1, k : k + 1], low[0:1, k : k + 1]) for k in range(count)]


def over_entries(x):
    return scaled(x, 1.0 / ENTRIES)


def place():
    strip, blk = lax.axis_index("strip"), lax.axis_index("blk")
    return strip, blk


def send_halo(payload, vector):
    strip, blk = place()
    for ds, row in ((-1, 0), (1, ROWS - 1)):
        for db in (-1, 0, 1):
            s, j = strip + ds, blk + db
            inside = (s >= 0) & (s < STRIPS) & (j >= 0) & (j < BLKS)

            @pl.when(inside)
            def _():
                payload[s * BLKS + j, 4:8, :] = vector[:, row, :]


def gather_halo(around, vector, left, right, received):
    strip, blk = place()
    for column, own in ((0, left), (1, vector), (2, right)):
        j = blk + column - 1
        column_in = (j >= 0) & (j < BLKS)
        jj = jnp.clip(j, 0, BLKS - 1)
        base = 10 * column
        block = own[...]
        around[:, base + 1 : base + 9, :] = jnp.where(column_in, block, 0.0) if column != 1 else block
        for row, s in ((0, strip - 1), (9, strip + 1)):
            row_in = column_in & (s >= 0) & (s < STRIPS)
            source = jnp.clip(s, 0, STRIPS - 1) * BLKS + jj
            around[:, base + row, :] = jnp.where(row_in, received[source, 4:8, :], 0.0)
    around[:, 30:32, :] = jnp.zeros((4, 2, LEN), F32)


def near(around, near_pair, kernel_hbm, kernels, sems):
    sub = lax.broadcasted_iota(jnp.int32, (8, LEN), 0)

    def chunk(n, total):
        near_copy(kernel_hbm, kernels, sems, n).wait()
        for i in range(NEAR_CHUNK):
            p = n * NEAR_CHUNK + i
            code = near_pair[p]
            t = code // 9
            k = code - 9 * t
            up = k // 3
            source = (k - 3 * up) * 10 + t + up
            for b in range(3):
                row = around[b, pl.ds(source, 1), :]
                left = jnp.where(sub == t, row, 0.0).astype(BF16)
                matrix = kernels[p, :, b].reshape(3 * LEN, LEN)
                total = total + lax.dot_general(left, matrix, TRANS_B, preferred_element_type=F32)
        return total

    return lax.fori_loop(0, NEAR_CHUNKS, chunk, jnp.zeros((8, 3 * LEN), F32))


def near_copy(kernel_hbm, kernels, sems, n):
    part = pl.ds(n * NEAR_CHUNK, NEAR_CHUNK)
    return pltpu.make_async_copy(kernel_hbm.at[part], kernels.at[part], sems.at[n])


def far_copy(hbm, buffer, sems, n):
    part = pl.ds(n * FAR_PER_COPY, FAR_PER_COPY)
    return pltpu.make_async_copy(hbm.at[part], buffer.at[part], sems.at[n])


def split3(x):
    a = x.astype(BF16)
    rest = x - a.astype(F32)
    b = rest.astype(BF16)
    c = (rest - b.astype(F32)).astype(BF16)
    return a, b, c


def far(payload, vector, source_row, right_hbm, left_hbm, right, left, right_sems, left_sems, gathered, parts):
    for d in range(DEVICES):
        gathered[:, d, :] = vector[0:3, source_row[d], :]
    sub = lax.broadcasted_iota(jnp.int32, (FAR_CHUNK, FAR_CHUNK * RANK), 0)
    lane = lax.broadcasted_iota(jnp.int32, (FAR_CHUNK, FAR_CHUNK * RANK), 1)
    own = lane // RANK == sub

    def stacked(x):
        if parts == 1:
            return x.astype(BF16)
        return jnp.concatenate([piece.astype(F32) for piece in split3(x)], axis=0).astype(BF16)

    def summed(x):
        if parts == 1:
            return x
        return x[0:8] + (x[8:16] + x[16:24])

    per_copy = FAR_PER_COPY // FAR_CHUNK

    def chunk(n, carry):
        @pl.when(lax.rem(n, per_copy) == 0)
        def _():
            far_copy(right_hbm, right, right_sems, n // per_copy).wait()
            far_copy(left_hbm, left, left_sems, n // per_copy).wait()

        d = pl.ds(pl.multiple_of(n * FAR_CHUNK, FAR_CHUNK), FAR_CHUNK)
        c = jnp.zeros((8 * parts, FAR_CHUNK * RANK), F32)
        for b in range(3):
            matrix = right[d, b].reshape(FAR_CHUNK * RANK, LEN)
            c = c + lax.dot_general(stacked(gathered[b, d, :]), matrix, TRANS_B, preferred_element_type=F32)
        c = stacked(jnp.where(own, summed(c), 0.0))
        for a in range(3):
            matrix = left[d, a].reshape(FAR_CHUNK * RANK, LEN)
            payload[d, a, :] = summed(lax.dot_general(c, matrix, PLAIN, preferred_element_type=F32))
        return carry

    lax.fori_loop(0, FAR_CHUNKS, chunk, 0, unroll=2)


def far_sum(received, target):
    sub = lax.broadcasted_iota(jnp.int32, (8, LEN), 0).astype(F32)

    def some(n, totals):
        out = list(totals)
        for i in range(8):
            g = n * 8 + i
            hit = target(g) == sub
            for a in range(3):
                k = 3 * (i % 2) + a
                out[k] = out[k] + jnp.where(hit, received[g, a : a + 1, :], 0.0)
        return tuple(out)

    z = lax.fori_loop(0, DEVICES // 8, some, (jnp.zeros((8, LEN), F32),) * 6)
    return [z[a] + z[3 + a] for a in range(3)]


def flux(around, conductivity):
    pressure = around[3, 11:19, :]
    lane = lax.broadcasted_iota(jnp.int32, (8, LEN), 1)
    west = pltpu.roll(jnp.where(lane == LEN - 1, around[3, 1:9, :], pressure), 1, 1)
    east = pltpu.roll(jnp.where(lane == 0, around[3, 21:29, :], pressure), LEN - 1, 1)
    total = conductivity[0] * (around[3, 10:18, :] - pressure) + conductivity[1] * (around[3, 12:20, :] - pressure)
    return total + conductivity[2] * (west - pressure) + conductivity[3] * (east - pressure)


def image_of(vector, near_part, far_part, flux_sum):
    out = [vector[a] + near_part[:, a * LEN : (a + 1) * LEN] + far_part[a] for a in range(3)]
    out[0] = out[0] - vector[3]
    return out + [vector[3] + vector[0] - flux_sum]


def far_scratch():
    return [
        pltpu.VMEM((DEVICES, 3, RANK, LEN), BF16),
        pltpu.VMEM((DEVICES, 3, RANK, LEN), BF16),
        pltpu.SemaphoreType.DMA((FAR_COPIES,)),
        pltpu.SemaphoreType.DMA((FAR_COPIES,)),
        pltpu.VMEM((3, DEVICES, LEN), F32),
    ]


def near_scratch():
    return [
        pltpu.VMEM((PAIRS, 3, 3, LEN, LEN), BF16),
        pltpu.SemaphoreType.DMA((NEAR_CHUNKS,)),
    ]


def start_far(right_hbm, left_hbm, right, left, right_sems, left_sems):
    for n in range(FAR_COPIES):
        far_copy(right_hbm, right, right_sems, n).start()
        far_copy(left_hbm, left, left_sems, n).start()


def start_near(kernel_hbm, kernels, sems):
    for n in range(NEAR_CHUNKS):
        near_copy(kernel_hbm, kernels, sems, n).start()


def first_far(source_row, target_row, vector, right_hbm, left_hbm, payload, right, left, right_sems, left_sems, gathered):
    start_far(right_hbm, left_hbm, right, left, right_sems, left_sems)
    payload[:, 4:8, :] = jnp.zeros((DEVICES, 4, LEN), F32)
    send_halo(payload, vector)
    for d in range(DEVICES):
        payload[d, 3:4, :] = jnp.full((1, LEN), target_row[d], jnp.int32).astype(F32)
    far(payload, vector, source_row, right_hbm, left_hbm, right, left, right_sems, left_sems, gathered, 1)


def middle(
    near_pair, source_row, vector, conductivity, left_side, right_side, received, kernel_hbm, right_hbm, left_hbm,
    image, far_part, around, payload,
    rounded, kernels, near_sems, right, left, right_sems, left_sems, gathered,
):
    start_near(kernel_hbm, kernels, near_sems)
    start_far(right_hbm, left_hbm, right, left, right_sems, left_sems)
    gather_halo(around, vector, left_side, right_side, received)
    rounded[...] = around[0:3].astype(BF16).astype(F32)
    payload[:, 4:8, :] = jnp.zeros((DEVICES, 4, LEN), F32)
    arrived = far_sum(received, lambda g: received[g, 3:4, :])
    for a in range(3):
        far_part[a] = arrived[a]
    flux_sum = flux(around, conductivity)
    near_part = near(rounded, near_pair, kernel_hbm, kernels, near_sems)
    own = [vector[c] for c in range(4)]
    result = image_of(own, near_part, arrived, flux_sum)
    for c in range(4):
        image[c] = result[c]
    send_halo(payload, image)
    row = dot_row([(own, own), (own, result), (result, result)])
    payload[:, 3, :] = jnp.broadcast_to(row, (DEVICES, LEN))
    far(payload, image, source_row, right_hbm, left_hbm, right, left, right_sems, left_sems, gathered, 3)


def last(
    near_pair, vector, image, conductivity, left_side, right_side, target, received, far_one, around_one, kernel_hbm,
    first, image_two, scalars, rows,
    around, rounded, kernels, near_sems,
):
    start_near(kernel_hbm, kernels, near_sems)
    gather_halo(around, image, left_side, right_side, received)
    vv, vi, ii = totals(received[:, 3, :], 3)
    h = over_entries(vi)
    h0 = h[0]
    h0_pair = (h0, jnp.zeros_like(h0))
    square = pair_add(ii, pair_add(scaled(neg(pair_mul(h0_pair, vi)), 2.0), pair_mul(pair_mul(h0_pair, h0_pair), vv)))
    beta1 = jnp.sqrt(jnp.maximum(square[0], 0.0) / ENTRIES + EPSILON)
    h0_wide = jnp.broadcast_to(h0, (8, LEN))
    beta_wide = jnp.broadcast_to(beta1, (8, LEN))
    for c in range(4):
        for r in range(0, HALO, 8):
            around[c, r : r + 8, :] = (around[c, r : r + 8, :] - h0_wide * around_one[c, r : r + 8, :]) / beta_wide
    rounded[...] = around[0:3].astype(BF16).astype(F32)
    own = [around[c, 11:19, :] for c in range(4)]
    for c in range(4):
        first[c] = own[c]
    arrived = far_sum(received, lambda g: target[g, 3:4, :])
    far_part = [(arrived[a] - h0_wide * far_one[a]) / beta_wide for a in range(3)]
    flux_sum = flux(around, conductivity)
    near_part = near(rounded, near_pair, kernel_hbm, kernels, near_sems)
    result = image_of(own, near_part, far_part, flux_sum)
    for c in range(4):
        image_two[c] = result[c]
    start = [vector[c] for c in range(4)]
    row = dot_row([(start, result), (own, result), (result, result), (start, start), (start, own), (own, own)])
    rows[...] = jnp.broadcast_to(row, (DEVICES, LEN))
    lane = lax.broadcasted_iota(jnp.int32, (1, LEN), 1)
    scalars[...] = jnp.where(lane == 0, h0, beta1)


def finish(vector, first, image, scalars, rows, krylov, hessenberg):
    si, fi, ii, ss, sf, ff = totals(rows[...], 6)
    g0, g1 = over_entries(si)[0], over_entries(fi)[0]
    zero = jnp.zeros_like(g0)
    p0, p1 = (g0, zero), (g1, zero)
    square = pair_add(ii, scaled(neg(pair_add(pair_mul(p0, si), pair_mul(p1, fi))), 2.0))
    cross = scaled(pair_mul(pair_mul(p0, p1), sf), 2.0)
    square = pair_add(square, pair_add(cross, pair_add(pair_mul(pair_mul(p0, p0), ss), pair_mul(pair_mul(p1, p1), ff))))
    beta2 = jnp.sqrt(jnp.maximum(square[0], 0.0) / ENTRIES + EPSILON)
    g0_wide, g1_wide, beta_wide = (jnp.broadcast_to(x, (8, LEN)) for x in (g0, g1, beta2))
    for c in range(4):
        krylov[0, c] = first[c]
        krylov[1, c] = (image[c] - g0_wide * vector[c] - g1_wide * first[c]) / beta_wide
    lane = lax.broadcasted_iota(jnp.int32, (1, LEN), 1)
    out = jnp.where(lane < 2, scalars[...], jnp.where(lane == 2, g0, jnp.where(lane == 3, g1, beta2)))
    hessenberg[...] = out


def shape(*dims):
    return jax.ShapeDtypeStruct(dims, F32)


def params(mib):
    return pltpu.CompilerParams(vmem_limit_bytes=mib * 1024 * 1024)


def exchange(x):
    return lax.all_to_all(x, ("strip", "blk"), 0, 0, tiled=True)


def sides(vector):
    up = [(i, (i + 1) % BLKS) for i in range(BLKS)]
    down = [(j, i) for i, j in up]
    return lax.ppermute(vector, "blk", up), lax.ppermute(vector, "blk", down)


def local(vector, conductivity, near_kernel, near_pair, far_right, far_left, far_source_row, far_target_row):
    right = jnp.transpose(far_right[0], (0, 2, 1, 3))
    left = jnp.transpose(far_left[0], (0, 2, 1, 3))
    source_row, target_row = far_source_row[0], far_target_row[0]
    block, halo, slots = shape(4, ROWS, LEN), shape(4, HALO, LEN), shape(DEVICES, 8, LEN)

    left_side, right_side = sides(vector)
    payload = pl.pallas_call(
        first_far,
        out_shape=slots,
        in_specs=[SMEM, SMEM, VMEM, ANY, ANY],
        out_specs=VMEM,
        scratch_shapes=far_scratch(),
        compiler_params=params(24),
        name="first_far",
    )(source_row, target_row, vector, right, left)
    received_one = exchange(payload)
    image, far_part, around, payload = pl.pallas_call(
        middle,
        out_shape=(block, shape(3, ROWS, LEN), halo, slots),
        in_specs=[SMEM, SMEM, VMEM, VMEM, VMEM, VMEM, VMEM, ANY, ANY, ANY],
        out_specs=(VMEM,) * 4,
        scratch_shapes=[pltpu.VMEM((3, HALO, LEN), F32)] + near_scratch() + far_scratch(),
        compiler_params=params(40),
        name="middle",
    )(near_pair, source_row, vector, conductivity, left_side, right_side, received_one, near_kernel, right, left)
    left_side, right_side = sides(image)
    received_two = exchange(payload)
    first, image_two, scalars, rows = pl.pallas_call(
        last,
        out_shape=(block, block, shape(1, LEN), shape(DEVICES, LEN)),
        in_specs=[SMEM] + [VMEM] * 9 + [ANY],
        out_specs=(VMEM,) * 4,
        scratch_shapes=[pltpu.VMEM((4, HALO, LEN), F32), pltpu.VMEM((3, HALO, LEN), F32)] + near_scratch(),
        compiler_params=params(32),
        name="last",
    )(
        near_pair, vector, image, conductivity, left_side, right_side, received_one, received_two, far_part, around,
        near_kernel,
    )
    rows = exchange(rows)
    krylov, hessenberg = pl.pallas_call(
        finish,
        out_shape=(shape(2, 4, ROWS, LEN), shape(1, LEN)),
        in_specs=[VMEM] * 5,
        out_specs=(VMEM, VMEM),
        name="finish",
    )(vector, first, image_two, scalars, rows)
    return krylov, hessenberg[0, 0:5]


def solution(mesh):
    in_specs = (
        P(None, "strip", "blk"),
        P(None, "strip", "blk"),
        P(("strip", "blk"), None, None, None, None),
        P(("strip", "blk")),
        P(("strip", "blk"), None, None, None, None),
        P(("strip", "blk"), None, None, None, None),
        P(("strip", "blk"), None),
        P(("strip", "blk"), None),
    )
    out_specs = (P(None, None, "strip", "blk"), P())
    return jax.shard_map(local, mesh=mesh, in_specs=in_specs, out_specs=out_specs, check_vma=False)
```

time: 709 us -> 112 us (0.16)
  waiting for transfers between devices: 371 us -> 16.1 us
  blocking collectives: 254 us -> 14.3 us
  Pallas kernels: 0 us -> 36.7 us
  matrix products: 27.7 us -> 0 us
  between operations: 16.5 us -> 0.78 us
  other arithmetic: 12.4 us -> 0 us
  local copies, waits for them, and re-layouts: 4.48 us -> 15.5 us
    unnamed x4 -> x0, waiting for transfers between devices: 363 us -> none
    psum x4 -> x0, blocking collectives: 254 us -> none  [the longest x2 129 us: reduce_basis(): proj_total = lax.psum(local_proj, ('strip', 'blk'))]
    pallas_call x0 -> x4, Pallas kernels: none -> 36.7 us  [the longest x1 15.4 us: local(): pl.pallas_call(middle, out_shape=(block, shape(3, ROWS, LEN), halo, slots...]
    dot_general x8 -> x0, matrix products: 27.7 us -> none  [the longest x2 18.5 us: apply_operator(): jnp.einsum('pabim,bpm->pai', near_kernel, near_source, preferred_element_...]
    all_to_all x0 -> x2, starting transfers between devices: none -> 16.1 us  [exchange(): return lax.all_to_all(x, ('strip', 'blk'), 0, 0, tiled=True)]
    unnamed x8 -> x34, local copies, waits for them, and re-layouts: 0.04 us -> 14.3 us
    all_to_all x0 -> x1, blocking collectives: none -> 14.3 us  [exchange(): return lax.all_to_all(x, ('strip', 'blk'), 0, 0, tiled=True)]
    ppermute x8 -> x4, starting transfers between devices: 22.6 us -> 11.4 us  [sides(): return (lax.ppermute(vector, 'blk', up), lax.ppermute(vector, 'blk', down))]
  transfers between devices with their start and end apart: 10 -> 6, of which waited for: 6 -> 6; matrix products, arithmetic and copies ran while one was open for 3% -> 0% of each run, Pallas kernels for 0% -> 0%
where the time goes in v1:
time: 112 us; the launch traced here: 111 us
  Pallas kernels  36.7 us (33%)
  starting transfers between devices  27.6 us (25%)
  waiting for transfers between devices  16.1 us (14%)
  local copies, waits for them, and re-layouts  15.5 us (14%)
  blocking collectives  14.3 us (13%)
    all_to_all x2, starting transfers between devices, exchange(): return lax.all_to_all(x, ('strip', 'blk'), 0, 0, tiled=True)  16.1 us
    pallas_call x1, Pallas kernels, local(): pl.pallas_call(middle, out_shape=(block, shape(3, ROWS, LEN), halo, slots...  15.4 us
    unnamed x34, local copies, waits for them, and re-layouts  14.3 us
    all_to_all x1, blocking collectives, exchange(): return lax.all_to_all(x, ('strip', 'blk'), 0, 0, tiled=True)  14.3 us
    ppermute x4, waiting for transfers between devices, sides(): return (lax.ppermute(vector, 'blk', up), lax.ppermute(vector, 'blk', down))  13.2 us
    pallas_call x1, Pallas kernels, local(): pl.pallas_call(last, out_shape=(block, block, shape(1, LEN), shape(DEVICE...  11.7 us
    ppermute x4, starting transfers between devices, sides(): return (lax.ppermute(vector, 'blk', up), lax.ppermute(vector, 'blk', down))  11.4 us
    pallas_call x1, Pallas kernels, local(): pl.pallas_call(first_far, out_shape=slots, in_specs=[SMEM, SMEM, VMEM, AN...  7.28 us
  transfers between devices with their start and end apart: 6, of which 6 were waited for; matrix products, arithmetic and copies ran while one was open for 0% of the time, Pallas kernels for 0%

profile of v1, /device:TPU:1, one launch (start us, length us, event | category | flops | bytes accessed | tf_op | source)
XLA Modules:
  0.0 111.0 jit_solution(12885329051234309766)
XLA Ops:
  0.6 1.9 %copy-done.1 = bf16[1,128,32,3,128]{4,2,3,1,0:T(8,128)(2,1)S(1)} copy-done((bf16[1,128,32,3,128]{4,2,3,1,0:T(8,128)(2,1)S(1)}, bf16[1,128,32,3,128]{4,2,3,1,0:T(8,128)(2,1)}, u32[]{:S(2)}) %copy-start.1) | copy-done | bytes 3145752
  2.5 1.9 %copy-done.3 = bf16[1,128,32,3,128]{4,2,3,1,0:T(8,128)(2,1)S(1)} copy-done((bf16[1,128,32,3,128]{4,2,3,1,0:T(8,128)(2,1)S(1)}, bf16[1,128,32,3,128]{4,2,3,1,0:T(8,128)(2,1)}, u32[]{:S(2)}) %copy-start.3) | copy-done | bytes 3145752
  4.4 0.7 copy-done.7
  5.1 0.7 copy-done.12
  5.8 0.7 copy-done.15
  6.5 7.3 %first_far.1 = f32[128,8,128]{2,1,0:T(8,128)S(1)} custom-call(s32[128]{0:T(128)S(1)} %bitcast.19, s32[128]{0:T(128)S(1)} %bitcast.21, f32[4,8,128]{2,1,0:T(8,128)S(1)} %copy-done.7, bf16[128,3,32,128]{3,2,1,0:T(8,128)(2,1)S(1)} %bitcast.14, bf16[128,3,32,128]{3,2,1,0:T(8,128)(2,1)S(1)} %bitcast.16), custom_call_target="tpu_custom_call" | custom-call | tf_op jit(solution)/shard_map/first_far/pallas_call | solution.py:390
  13.8 0.8 copy-done.5
  14.6 12.0 %all-to-all-start = ((f32[128,8,128]{2,1,0:T(8,128)}), f32[128,8,128]{2,1,0:T(8,128)}, u32[]{:S(2)}, u32[]{:S(2)}) async-start(f32[128,8,128]{2,1,0:T(8,128)} %copy-done.5), calls=%async_computation | async-start | bytes 1048576 | tf_op jit(solution)/shard_map/all_to_all | solution.py:374
  26.5 5.6 %collective-permute-start.1 = (f32[4,8,128]{2,1,0:T(8,128)S(1)}, f32[4,8,128]{2,1,0:T(8,128)S(1)}, u32[]{:S(2)}, u32[]{:S(2)}) collective-permute-start(f32[4,8,128]{2,1,0:T(8,128)S(1)} %copy-done.8), channel_id=1, source_target_pairs={{1,0},{2,1},{3,2},{4,3},{5,4},{6,5},{7,6},{8,7},{9,8},{10,9},{11,1... | collective-permute-start | bytes 49160 | tf_op jit(solution)/shard_map/ppermute | solution.py:380
  32.2 0.0 collective-permute-start
  32.2 0.9 collective-permute-done.1.right_side
  33.0 5.7 %collective-permute-done.left_side = f32[4,8,128]{2,1,0:T(8,128)S(1)} collective-permute-done((f32[4,8,128]{2,1,0:T(8,128)S(1)}, f32[4,8,128]{2,1,0:T(8,128)S(1)}, u32[]{:S(2)}, u32[]{:S(2)}) %collective-permute-start) | collective-permute-done | bytes 16416 | tf_op jit(solution)/shard_map/ppermute | solution.py:380
  38.7 1.4 %all-to-all-done.received.target = f32[128,8,128]{2,1,0:T(8,128)} async-done(((f32[128,8,128]{2,1,0:T(8,128)}), f32[128,8,128]{2,1,0:T(8,128)}, u32[]{:S(2)}, u32[]{:S(2)}) %all-to-all-start) | async-done | bytes 524320 | tf_op jit(solution)/shard_map/all_to_all | solution.py:374
  40.0 0.0 copy-done.9
  40.1 0.0 copy-start.4
  40.1 1.9 %copy-done.4 = bf16[1,128,32,3,128]{4,2,3,1,0:T(8,128)(2,1)S(1)} copy-done((bf16[1,128,32,3,128]{4,2,3,1,0:T(8,128)(2,1)S(1)}, bf16[1,128,32,3,128]{4,2,3,1,0:T(8,128)(2,1)}, u32[]{:S(2)}) %copy-start.4) | copy-done | bytes 3145752
  42.0 15.4 %middle.1 = (f32[4,8,128]{2,1,0:T(8,128)S(1)}, f32[3,8,128]{2,1,0:T(8,128)S(1)}, f32[4,32,128]{2,1,0:T(8,128)S(1)}, f32[128,8,128]{2,1,0:T(8,128)S(1)}) custom-call(s32[48]{0:T(128)S(1)} %copy-done.14, s32[128]{0:T(128)S(1)} %bitcast.20, f32[4,8,128]{2,1,0:T(8,128)S(1)} %copy-done.8, f32[4,8,128]{2,1,0:T(8,128)S(1)} %copy-done.9, ...), custom_call_target="tpu_custom_call" | custom-call | tf_op jit(solution)/shard_map/middle/pallas_call | solution.py:400
  57.4 0.0 copy-start.6
  57.4 0.8 copy-done.6
  58.2 4.2 %all-to-all-start.1 = ((f32[128,8,128]{2,1,0:T(8,128)}), f32[128,8,128]{2,1,0:T(8,128)S(1)}, u32[]{:S(2)}, u32[]{:S(2)}) async-start(f32[128,8,128]{2,1,0:T(8,128)} %copy-done.6), calls=%async_computation.1 | async-start | bytes 1048576 | tf_op jit(solution)/shard_map/all_to_all | solution.py:374
  62.4 5.8 %collective-permute-start.3 = (f32[4,8,128]{2,1,0:T(8,128)S(1)}, f32[4,8,128]{2,1,0:T(8,128)S(1)}, u32[]{:S(2)}, u32[]{:S(2)}) collective-permute-start(f32[4,8,128]{2,1,0:T(8,128)S(1)} %get-tuple-element.12.image), channel_id=1, source_target_pairs={{1,0},{2,1},{3,2},{4,3},{5,4},{6,5},{7,6},{8,7},{9,8},{10,9},{11,1... | collective-permute-start | bytes 49160 | tf_op jit(solution)/shard_map/ppermute | solution.py:380
  68.2 0.0 collective-permute-start.2
  68.2 0.9 collective-permute-done.3.right_side
  69.0 5.8 %collective-permute-done.2.left_side = f32[4,8,128]{2,1,0:T(8,128)S(1)} collective-permute-done((f32[4,8,128]{2,1,0:T(8,128)S(1)}, f32[4,8,128]{2,1,0:T(8,128)S(1)}, u32[]{:S(2)}, u32[]{:S(2)}) %collective-permute-start.2) | collective-permute-done | bytes 16416 | tf_op jit(solution)/shard_map/ppermute | solution.py:380
  74.9 1.5 %all-to-all-done.1.received = f32[128,8,128]{2,1,0:T(8,128)S(1)} async-done(((f32[128,8,128]{2,1,0:T(8,128)}), f32[128,8,128]{2,1,0:T(8,128)S(1)}, u32[]{:S(2)}, u32[]{:S(2)}) %all-to-all-start.1) | async-done | bytes 524320 | tf_op jit(solution)/shard_map/all_to_all | solution.py:374
  76.4 5.0 %copy-done = bf16[48,3,3,128,128]{4,3,2,1,0:T(8,128)(2,1)S(1)} copy-done((bf16[48,3,3,128,128]{4,3,2,1,0:T(8,128)(2,1)S(1)}, bf16[48,3,3,128,128]{4,3,2,1,0:T(8,128)(2,1)}, u32[]{:S(2)}) %copy-start) | copy-done | bytes 14155800
  81.4 11.7 %last.1 = (f32[4,8,128]{2,1,0:T(8,128)S(1)}, f32[4,8,128]{2,1,0:T(8,128)S(1)}, f32[1,128]{1,0:T(1,128)S(1)}, f32[128,128]{1,0:T(8,128)S(1)}) custom-call(s32[48]{0:T(128)S(1)} %copy-done.14, f32[4,8,128]{2,1,0:T(8,128)S(1)} %copy-done.8, f32[4,8,128]{2,1,0:T(8,128)S(1)} %get-tuple-element.12.image, f32[4,8,128]{2,1,0:T(8,128)S(1)} %copy-done.9, ...), custom_call_target="tpu_custom_call" | custom-call | tf_op jit(solution)/shard_map/last/pallas_call | solution.py:411
  93.1 0.0 copy-start.16
  93.1 14.3 %all_to_all.21 = f32[128,1,128]{2,1,0:T(1,128)} all-to-all(f32[128,1,128]{2,1,0:T(1,128)S(1)} %bitcast.18), channel_id=1, replica_groups=mesh['strip'=8,'blk'=16] {'strip','blk'}, dimensions={0} | all-to-all | bytes 131072 | tf_op jit(solution)/shard_map/all_to_all | solution.py:374
  107.4 0.0 copy-done.11
  107.4 2.4 %finish.1 = (f32[2,4,8,128]{3,2,1,0:T(8,128)}, f32[1,128]{1,0:T(1,128)}) custom-call(f32[4,8,128]{2,1,0:T(8,128)} %vector.7, f32[4,8,128]{2,1,0:T(8,128)} %copy-done.10, f32[4,8,128]{2,1,0:T(8,128)} %copy-done.11, f32[1,128]{1,0:T(1,128)} %copy-done.16, f32[128,128]{1,0:T(8,128)} %bitcast.22), custom_call_target="tpu_custom_call" | custom-call | tf_op jit(solution)/shard_map/finish/pallas_call | solution.py:424
  109.8 1.2 %slice_bitcast_fusion = f32[5]{0:T(128)} fusion(f32[1,128]{1,0:T(1,128)} %get-tuple-element.21), kind=kLoop, calls=%fused_computation | loop fusion | bytes 40 | tf_op jit(solution)/shard_map/squeeze | solution.py:431
  (20 shorter events, 0.0 us)
Async XLA Ops:
  0.6 1.9 %copy-start.1 = (bf16[1,128,32,3,128]{4,2,3,1,0:T(8,128)(2,1)S(1)}, bf16[1,128,32,3,128]{4,2,3,1,0:T(8,128)(2,1)}, u32[]{:S(2)}) copy-start(bf16[1,128,32,3,128]{4,2,3,1,0:T(8,128)(2,1)} %param.12) | copy-start | bytes 9437188
  2.5 1.9 %copy-start.3 = (bf16[1,128,32,3,128]{4,2,3,1,0:T(8,128)(2,1)S(1)}, bf16[1,128,32,3,128]{4,2,3,1,0:T(8,128)(2,1)}, u32[]{:S(2)}) copy-start(bf16[1,128,32,3,128]{4,2,3,1,0:T(8,128)(2,1)} %param.13) | copy-start | bytes 9437188
  4.4 0.7 copy-start.7
  5.1 0.7 copy-start.12
  5.8 0.7 copy-start.15
  6.4 20.1 %copy-start.8 = (f32[4,8,128]{2,1,0:T(8,128)S(1)}, f32[4,8,128]{2,1,0:T(8,128)}, u32[]{:S(2)}) copy-start(f32[4,8,128]{2,1,0:T(8,128)} %vector.7) | copy-start | bytes 49156
  6.4 33.6 %copy-start.2 = (bf16[1,128,32,3,128]{4,2,3,1,0:T(8,128)(2,1)S(1)}, bf16[1,128,32,3,128]{4,2,3,1,0:T(8,128)(2,1)}, u32[]{:S(2)}) copy-start(bf16[1,128,32,3,128]{4,2,3,1,0:T(8,128)(2,1)} %param.12) | copy-start | bytes 9437188
  6.4 33.6 %copy-start.9 = (f32[4,8,128]{2,1,0:T(8,128)S(1)}, f32[4,8,128]{2,1,0:T(8,128)}, u32[]{:S(2)}) copy-start(f32[4,8,128]{2,1,0:T(8,128)} %conductivity.3) | copy-start | bytes 49156
  6.4 33.6 %copy-start.13 = (s32[1,128]{1,0:T(1,128)S(1)}, s32[1,128]{1,0:T(1,128)}, u32[]{:S(2)}) copy-start(s32[1,128]{1,0:T(1,128)} %param.14) | copy-start | bytes 1540
  6.5 33.6 %copy-start.14 = (s32[48]{0:T(128)S(1)}, s32[48]{0:T(128)}, u32[]{:S(2)}) copy-start(s32[48]{0:T(128)} %near_pair.3) | copy-start | bytes 580
  13.7 0.8 copy-start.5
  14.6 25.5 %all-to-all-start = ((f32[128,8,128]{2,1,0:T(8,128)}), f32[128,8,128]{2,1,0:T(8,128)}, u32[]{:S(2)}, u32[]{:S(2)}) async-start(f32[128,8,128]{2,1,0:T(8,128)} %copy-done.5), calls=%async_computation | async-start | bytes 1048576 | tf_op jit(solution)/shard_map/all_to_all | solution.py:374
  26.5 6.5 %collective-permute-start.1 = (f32[4,8,128]{2,1,0:T(8,128)S(1)}, f32[4,8,128]{2,1,0:T(8,128)S(1)}, u32[]{:S(2)}, u32[]{:S(2)}) collective-permute-start(f32[4,8,128]{2,1,0:T(8,128)S(1)} %copy-done.8), channel_id=1, source_target_pairs={{1,0},{2,1},{3,2},{4,3},{5,4},{6,5},{7,6},{8,7},{9,8},{10,9},{11,1... | collective-permute-start | bytes 49160 | tf_op jit(solution)/shard_map/ppermute | solution.py:380
  32.2 6.5 %collective-permute-start = (f32[4,8,128]{2,1,0:T(8,128)S(1)}, f32[4,8,128]{2,1,0:T(8,128)S(1)}, u32[]{:S(2)}, u32[]{:S(2)}) collective-permute-start(f32[4,8,128]{2,1,0:T(8,128)S(1)} %copy-done.8), channel_id=1, source_target_pairs={{0,1},{1,2},{2,3},{3,4},{4,5},{5,6},{6,7},{7,8},{8,9},{9,10},{10,1... | collective-permute-start | bytes 49160 | tf_op jit(solution)/shard_map/ppermute | solution.py:380
  40.1 1.9 %copy-start.4 = (bf16[1,128,32,3,128]{4,2,3,1,0:T(8,128)(2,1)S(1)}, bf16[1,128,32,3,128]{4,2,3,1,0:T(8,128)(2,1)}, u32[]{:S(2)}) copy-start(bf16[1,128,32,3,128]{4,2,3,1,0:T(8,128)(2,1)} %param.13) | copy-start | bytes 9437188
  57.4 0.8 copy-start.6
  58.2 18.2 %all-to-all-start.1 = ((f32[128,8,128]{2,1,0:T(8,128)}), f32[128,8,128]{2,1,0:T(8,128)S(1)}, u32[]{:S(2)}, u32[]{:S(2)}) async-start(f32[128,8,128]{2,1,0:T(8,128)} %copy-done.6), calls=%async_computation.1 | async-start | bytes 1048576 | tf_op jit(solution)/shard_map/all_to_all | solution.py:374
  62.4 6.6 %collective-permute-start.3 = (f32[4,8,128]{2,1,0:T(8,128)S(1)}, f32[4,8,128]{2,1,0:T(8,128)S(1)}, u32[]{:S(2)}, u32[]{:S(2)}) collective-permute-start(f32[4,8,128]{2,1,0:T(8,128)S(1)} %get-tuple-element.12.image), channel_id=1, source_target_pairs={{1,0},{2,1},{3,2},{4,3},{5,4},{6,5},{7,6},{8,7},{9,8},{10,9},{11,1... | collective-permute-start | bytes 49160 | tf_op jit(solution)/shard_map/ppermute | solution.py:380
  68.2 6.7 %collective-permute-start.2 = (f32[4,8,128]{2,1,0:T(8,128)S(1)}, f32[4,8,128]{2,1,0:T(8,128)S(1)}, u32[]{:S(2)}, u32[]{:S(2)}) collective-permute-start(f32[4,8,128]{2,1,0:T(8,128)S(1)} %get-tuple-element.12.image), channel_id=1, source_target_pairs={{0,1},{1,2},{2,3},{3,4},{4,5},{5,6},{6,7},{7,8},{8,9},{9,10},{10,1... | collective-permute-start | bytes 49160 | tf_op jit(solution)/shard_map/ppermute | solution.py:380
  76.4 5.0 %copy-start = (bf16[48,3,3,128,128]{4,3,2,1,0:T(8,128)(2,1)S(1)}, bf16[48,3,3,128,128]{4,3,2,1,0:T(8,128)(2,1)}, u32[]{:S(2)}) copy-start(bf16[48,3,3,128,128]{4,3,2,1,0:T(8,128)(2,1)} %kernel_hbm.3) | copy-start | bytes 42467332
  93.1 14.3 %copy-start.10 = (f32[4,8,128]{2,1,0:T(8,128)}, f32[4,8,128]{2,1,0:T(8,128)S(1)}, u32[]{:S(2)}) copy-start(f32[4,8,128]{2,1,0:T(8,128)S(1)} %get-tuple-element.16.first) | copy-start | bytes 49156
  93.1 14.3 %copy-start.11 = (f32[4,8,128]{2,1,0:T(8,128)}, f32[4,8,128]{2,1,0:T(8,128)S(1)}, u32[]{:S(2)}) copy-start(f32[4,8,128]{2,1,0:T(8,128)S(1)} %get-tuple-element.17.image) | copy-start | bytes 49156
  93.1 14.3 %copy-start.16 = (f32[1,128]{1,0:T(1,128)}, f32[1,128]{1,0:T(1,128)S(1)}, u32[]{:S(2)}) copy-start(f32[1,128]{1,0:T(1,128)S(1)} %get-tuple-element.18.scalars) | copy-start | bytes 1540

commit v2 on v1

v2 whole, which is shorter than its diff:
```python
import functools

import jax
import jax.numpy as jnp
from jax import lax
from jax.experimental import pallas as pl
from jax.experimental.pallas import tpu as pltpu
from jax.sharding import PartitionSpec as P

EPSILON = 1e-06
STRIPS, BLKS, DEVICES = 8, 16, 128
ROWS, LEN, RANK, PAIRS = 8, 128, 32, 48
ENTRIES = float(4 * STRIPS * ROWS * BLKS * LEN)
HALO = 32
NEAR_CHUNK = 8
NEAR_CHUNKS = PAIRS // NEAR_CHUNK
FAR_CHUNK = 16
FAR_CHUNKS = DEVICES // FAR_CHUNK
FAR_PER_COPY = 2
FAR_COPIES = FAR_CHUNKS // FAR_PER_COPY
BF16, F32 = jnp.bfloat16, jnp.float32
TRANS_B = (((1,), (1,)), ((), ()))
PLAIN = (((1,), (0,)), ((), ()))
VMEM = pl.BlockSpec(memory_space=pltpu.VMEM)
SMEM = pl.BlockSpec(memory_space=pltpu.SMEM)
ANY = pl.BlockSpec(memory_space=pl.ANY)
HBM = pl.BlockSpec(memory_space=pltpu.HBM)


def two_sum(a, b):
    s = a + b
    t = s - a
    return s, (a - (s - t)) + (b - t)


def halves(a):
    c = a * 4097.0
    hi = c - (c - a)
    return hi, a - hi


def two_prod(a, b):
    p = a * b
    ah, al = halves(a)
    bh, bl = halves(b)
    return p, ((ah * bh - p) + ah * bl + al * bh) + al * bl


def pair_add(x, y):
    s, e = two_sum(x[0], y[0])
    return two_sum(s, e + (x[1] + y[1]))


def pair_mul(x, y):
    p, e = two_prod(x[0], y[0])
    return two_sum(p, e + (x[0] * y[1] + x[1] * y[0]))


def neg(x):
    return -x[0], -x[1]


def scaled(x, power_of_two):
    return x[0] * power_of_two, x[1] * power_of_two


def dot_row(pairs):
    sub = lax.broadcasted_iota(jnp.int32, (8, LEN), 0)
    high = jnp.zeros((8, LEN), F32)
    low = jnp.zeros((8, LEN), F32)
    for k, (a, b) in enumerate(pairs):
        s, e = two_prod(a[0], b[0])
        for c in range(1, 4):
            s, e = pair_add((s, e), two_prod(a[c], b[c]))
        for step in (4, 2, 1):
            s, e = pair_add((s, e), (pltpu.roll(s, step, 0), pltpu.roll(e, step, 0)))
        high = jnp.where(sub == k, s, high)
        low = jnp.where(sub == k, e, low)
    pad = jnp.zeros((LEN - 16, LEN), F32)
    turned = jnp.concatenate([high, low, pad], axis=0).T
    s, e = column_sums(turned)
    return s + pltpu.roll(e, 16, 1)


def column_sums(x):
    parts = [(x[8 * i : 8 * i + 8], jnp.zeros((8, LEN), F32)) for i in range(16)]
    while len(parts) > 1:
        parts = [pair_add(parts[i], parts[i + 1]) for i in range(0, len(parts), 2)]
    s, e = parts[0]
    for step in (4, 2, 1):
        s, e = pair_add((s, e), (pltpu.roll(s, step, 0), pltpu.roll(e, step, 0)))
    return s[0:1], e[0:1]


def totals(rows, count):
    s, e = column_sums(rows)
    low = e + pltpu.roll(s, LEN - 8, 1) + pltpu.roll(s, LEN - 16, 1)
    s, low = two_sum(s, low)
    return [(s[0:1, k : k + 1], low[0:1, k : k + 1]) for k in range(count)]


def over_entries(x):
    return scaled(x, 1.0 / ENTRIES)


def place():
    strip, blk = lax.axis_index("strip"), lax.axis_index("blk")
    return strip, blk


def near(around, near_pair, kernel_hbm, kernels, sems):
    sub = lax.broadcasted_iota(jnp.int32, (8, LEN), 0)

    def chunk(n, total):
        near_copy(kernel_hbm, kernels, sems, n).wait()
        rows, matrices = [], []
        for i in range(NEAR_CHUNK):
            p = n * NEAR_CHUNK + i
            code = near_pair[p]
            t = code // 9
            k = code - 9 * t
            up = k // 3
            source = (k - 3 * up) * 10 + t + up
            for b in range(3):
                rows.append(jnp.where(sub == t, around[b, pl.ds(source, 1), :], 0.0))
                matrices.append(kernels[p, :, b].reshape(3 * LEN, LEN))
        left = jnp.concatenate(split3(jnp.concatenate(rows, axis=1)), axis=0)
        matrix = jnp.concatenate(matrices, axis=1)
        return total + lax.dot_general(left, matrix, TRANS_B, preferred_element_type=F32)

    total = lax.fori_loop(0, NEAR_CHUNKS, chunk, jnp.zeros((24, 3 * LEN), F32))
    return total[0:8], total[0:8] + (total[8:16] + total[16:24])


def near_copy(kernel_hbm, kernels, sems, n):
    part = pl.ds(n * NEAR_CHUNK, NEAR_CHUNK)
    return pltpu.make_async_copy(kernel_hbm.at[part], kernels.at[part], sems.at[n])


def far_copy(hbm, buffer, sems, n):
    part = pl.ds(n * FAR_CHUNK * FAR_PER_COPY, FAR_CHUNK * FAR_PER_COPY)
    return pltpu.make_async_copy(hbm.at[part], buffer.at[part], sems.at[n])


def split3(x):
    a = x.astype(BF16)
    rest = x - a.astype(F32)
    b = rest.astype(BF16)
    c = (rest - b.astype(F32)).astype(BF16)
    return a, b, c


def far(payload, vector, source_row, right_hbm, left_hbm, right, left, right_sems, left_sems, gathered, coefficients, parts):
    row = lax.broadcasted_iota(jnp.int32, (LEN, LEN), 0)
    from_row = jnp.where(row == source_row, 1.0, 0.0).T.astype(BF16)
    pieces = [[x.astype(BF16)] if parts == 1 else split3(x) for x in (vector[b] for b in range(3))]
    below = jnp.zeros((LEN - ROWS, LEN), F32)
    sources = [jnp.concatenate([pieces[b][k].astype(F32), below], axis=0).astype(BF16) for k in range(parts) for b in range(3)]
    sources = jnp.concatenate(sources, axis=1)
    gathered[...] = lax.dot_general(from_row, sources, PLAIN, preferred_element_type=F32).astype(BF16)
    rows = FAR_CHUNK * RANK
    sub = lax.broadcasted_iota(jnp.int32, (FAR_CHUNK, rows), 0)
    lane = lax.broadcasted_iota(jnp.int32, (FAR_CHUNK, rows), 1)
    own = lane // RANK == sub

    def summed(x):
        if parts == 1:
            return x
        return x[0:FAR_CHUNK] + (x[FAR_CHUNK : 2 * FAR_CHUNK] + x[2 * FAR_CHUNK :])

    for n in range(FAR_CHUNKS):
        if n % FAR_PER_COPY == 0:
            far_copy(right_hbm, right, right_sems, n // FAR_PER_COPY).wait()
        d = pl.ds(n * FAR_CHUNK, FAR_CHUNK)
        source = jnp.concatenate([gathered[d, 3 * LEN * k : 3 * LEN * (k + 1)] for k in range(parts)], axis=0)
        matrix = jnp.concatenate([right[d, b].reshape(rows, LEN) for b in range(3)], axis=1)
        c = summed(lax.dot_general(source, matrix, TRANS_B, preferred_element_type=F32))
        c = jnp.where(own, c, 0.0)
        coefficients[n] = c.astype(BF16) if parts == 1 else jnp.concatenate(split3(c), axis=0)
    for n in range(FAR_CHUNKS):
        if n % FAR_PER_COPY == 0:
            far_copy(left_hbm, left, left_sems, n // FAR_PER_COPY).wait()
        d = pl.ds(n * FAR_CHUNK, FAR_CHUNK)
        matrix = jnp.concatenate([left[d, a].reshape(rows, LEN) for a in range(3)], axis=1)
        result = summed(lax.dot_general(coefficients[n], matrix, PLAIN, preferred_element_type=F32))
        for a in range(3):
            payload[d, a, :] = result[:, a * LEN : (a + 1) * LEN]


def far_sum(received, target):
    sub = lax.broadcasted_iota(jnp.int32, (8, LEN), 0).astype(F32)

    def some(n, totals):
        out = list(totals)
        for i in range(8):
            g = n * 8 + i
            hit = target(g) == sub
            for a in range(3):
                k = 3 * (i % 2) + a
                out[k] = out[k] + jnp.where(hit, received[g, a : a + 1, :], 0.0)
        return tuple(out)

    z = lax.fori_loop(0, DEVICES // 8, some, (jnp.zeros((8, LEN), F32),) * 6)
    return [z[a] + z[3 + a] for a in range(3)]


def flux(around, conductivity):
    pressure = around[3, 11:19, :]
    lane = lax.broadcasted_iota(jnp.int32, (8, LEN), 1)
    west = pltpu.roll(jnp.where(lane == LEN - 1, around[3, 1:9, :], pressure), 1, 1)
    east = pltpu.roll(jnp.where(lane == 0, around[3, 21:29, :], pressure), LEN - 1, 1)
    total = conductivity[0] * (around[3, 10:18, :] - pressure) + conductivity[1] * (around[3, 12:20, :] - pressure)
    return total + conductivity[2] * (west - pressure) + conductivity[3] * (east - pressure)


def image_of(vector, local, far_part):
    out = [vector[a] + local[a] + far_part[a] for a in range(3)]
    out[0] = out[0] - vector[3]
    return out + [vector[3] + vector[0] - local[3]]


def far_scratch(parts, rows):
    return [
        pltpu.VMEM((DEVICES, 3, RANK, LEN), BF16),
        pltpu.VMEM((DEVICES, 3, RANK, LEN), BF16),
        pltpu.SemaphoreType.DMA((FAR_COPIES,)),
        pltpu.SemaphoreType.DMA((FAR_COPIES,)),
        pltpu.VMEM((DEVICES, parts * 3 * LEN), BF16),
        pltpu.VMEM((FAR_CHUNKS, parts * FAR_CHUNK, FAR_CHUNK * RANK), BF16),
        pltpu.VMEM((rows, 1, LEN), jnp.int32),
        pltpu.SemaphoreType.DMA((rows,)),
    ]


def near_scratch():
    return [
        pltpu.VMEM((PAIRS, 3, 3, LEN, LEN), BF16),
        pltpu.SemaphoreType.DMA((NEAR_CHUNKS,)),
    ]


def start_far(right_hbm, left_hbm, right, left, right_sems, left_sems):
    for n in range(FAR_COPIES):
        far_copy(right_hbm, right, right_sems, n).start()
    for n in range(FAR_COPIES):
        far_copy(left_hbm, left, left_sems, n).start()


def row_copies(sources, rows, sems):
    return [pltpu.make_async_copy(source, rows.at[i], sems.at[i]) for i, source in enumerate(sources)]


def start_near(kernel_hbm, kernels, sems):
    for n in range(NEAR_CHUNKS):
        near_copy(kernel_hbm, kernels, sems, n).start()


def first_far(
    source_hbm, target_hbm, vector, after_0, after_1, right_hbm, left_hbm, payload,
    right, left, right_sems, left_sems, gathered, coefficients, rows, row_sems,
):
    copies = row_copies((source_hbm, target_hbm), rows, row_sems)
    for copy in copies:
        copy.start()
    start_far(right_hbm, left_hbm, right, left, right_sems, left_sems)
    for copy in copies:
        copy.wait()
    payload[:, 3, :] = jnp.broadcast_to(rows[1].astype(F32), (DEVICES, LEN)).T
    far(payload, vector, rows[0], right_hbm, left_hbm, right, left, right_sems, left_sems, gathered, coefficients, 1)


def second_far(
    source_hbm, vector, row, after_0, after_1, right_hbm, left_hbm, payload,
    right, left, right_sems, left_sems, gathered, coefficients, rows, row_sems,
):
    (copy,) = row_copies((source_hbm,), rows, row_sems)
    copy.start()
    start_far(right_hbm, left_hbm, right, left, right_sems, left_sems)
    payload[:, 3, :] = jnp.broadcast_to(row[...], (DEVICES, LEN))
    copy.wait()
    far(payload, vector, rows[0], right_hbm, left_hbm, right, left, right_sems, left_sems, gathered, coefficients, 3)


def edges(vector, swap_a, swap_b, out):
    strip, _ = place()
    even = lax.rem(strip, 2) == 0
    above = jnp.where(even, swap_b[:, ROWS - 1, :], swap_a[:, ROWS - 1, :])
    below = jnp.where(even, swap_a[:, 0, :], swap_b[:, 0, :])
    out[0:4] = vector[...]
    out[4, 0:4, :] = jnp.where(strip > 0, above, 0.0)
    out[4, 4:8, :] = jnp.where(strip < STRIPS - 1, below, 0.0)


def local_part(near_pair, conductivity, own, left, right, kernel_hbm, rounded, full, around, kernels, sems):
    start_near(kernel_hbm, kernels, sems)
    _, blk = place()
    for column, blocks, inside in ((0, left, blk > 0), (1, own, None), (2, right, blk < BLKS - 1)):
        keep = (lambda x: x) if inside is None else (lambda x, inside=inside: jnp.where(inside, x, 0.0))
        base = 10 * column
        around[:, base + 1 : base + 9, :] = keep(blocks[0:4])
        around[:, base, :] = keep(blocks[4, 0:4, :])
        around[:, base + 9, :] = keep(blocks[4, 4:8, :])
    flux_sum = flux(around, conductivity)
    rounded[3] = flux_sum
    full[3] = flux_sum
    near_rounded, near_full = near(around, near_pair, kernel_hbm, kernels, sems)
    for a in range(3):
        rounded[a] = near_rounded[:, a * LEN : (a + 1) * LEN]
        full[a] = near_full[:, a * LEN : (a + 1) * LEN]


def first_image(vector, local, received, image, far_part, row):
    arrived = far_sum(received, lambda g: received[g, 3:4, :])
    for a in range(3):
        far_part[a] = arrived[a]
    own = [vector[c] for c in range(4)]
    result = image_of(own, local, arrived)
    for c in range(4):
        image[c] = result[c]
    row[...] = dot_row([(own, own), (own, result), (result, result)])


def second_image(vector, image, local_one, local_two, target, received, far_one, first, image_two, scalars, rows):
    vv, vi, ii = totals(received[:, 3, :], 3)
    h = over_entries(vi)
    h0 = h[0]
    h0_pair = (h0, jnp.zeros_like(h0))
    square = pair_add(ii, pair_add(scaled(neg(pair_mul(h0_pair, vi)), 2.0), pair_mul(pair_mul(h0_pair, h0_pair), vv)))
    beta1 = jnp.sqrt(jnp.maximum(square[0], 0.0) / ENTRIES + EPSILON)
    h0_wide = jnp.broadcast_to(h0, (8, LEN))
    beta_wide = jnp.broadcast_to(beta1, (8, LEN))

    def of_first(of_image, of_vector):
        return (of_image - h0_wide * of_vector) / beta_wide

    start = [vector[c] for c in range(4)]
    own = [of_first(image[c], start[c]) for c in range(4)]
    for c in range(4):
        first[c] = own[c]
    arrived = far_sum(received, lambda g: target[g, 3:4, :])
    far_part = [of_first(arrived[a], far_one[a]) for a in range(3)]
    local = [of_first(local_two[c], local_one[c]) for c in range(4)]
    result = image_of(own, local, far_part)
    for c in range(4):
        image_two[c] = result[c]
    row = dot_row([(start, result), (own, result), (result, result), (start, start), (start, own), (own, own)])
    rows[...] = jnp.broadcast_to(row, (DEVICES, LEN))
    lane = lax.broadcasted_iota(jnp.int32, (1, LEN), 1)
    scalars[...] = jnp.where(lane == 0, h0, beta1)


def finish(vector, first, image, scalars, rows, krylov, hessenberg):
    si, fi, ii, ss, sf, ff = totals(rows[...], 6)
    g0, g1 = over_entries(si)[0], over_entries(fi)[0]
    zero = jnp.zeros_like(g0)
    p0, p1 = (g0, zero), (g1, zero)
    square = pair_add(ii, scaled(neg(pair_add(pair_mul(p0, si), pair_mul(p1, fi))), 2.0))
    cross = scaled(pair_mul(pair_mul(p0, p1), sf), 2.0)
    square = pair_add(square, pair_add(cross, pair_add(pair_mul(pair_mul(p0, p0), ss), pair_mul(pair_mul(p1, p1), ff))))
    beta2 = jnp.sqrt(jnp.maximum(square[0], 0.0) / ENTRIES + EPSILON)
    g0_wide, g1_wide, beta_wide = (jnp.broadcast_to(x, (8, LEN)) for x in (g0, g1, beta2))
    for c in range(4):
        krylov[0, c] = first[c]
        krylov[1, c] = (image[c] - g0_wide * vector[c] - g1_wide * first[c]) / beta_wide
    for i, value in enumerate((scalars[0, 0], scalars[0, 1], g0[0, 0], g1[0, 0], beta2[0, 0])):
        hessenberg[i] = value


def shape(*dims):
    return jax.ShapeDtypeStruct(dims, F32)


def limit(mib):
    return pltpu.CompilerParams(vmem_limit_bytes=mib * 1024 * 1024)


def in_hbm(x):
    return pltpu.with_memory_space_constraint(x, pltpu.HBM)


def exchange(x):
    return lax.all_to_all(x, ("strip", "blk"), 0, 0, tiled=True)


def swaps(x, axis, size):
    even = [(i, i ^ 1) for i in range(size)]
    odd = [(i, (i + 1) % size if i % 2 else (i - 1) % size) for i in range(size)]
    return lax.ppermute(x, axis, even), lax.ppermute(x, axis, odd)


def sides(x):
    up = [(i, (i + 1) % BLKS) for i in range(BLKS)]
    down = [(j, i) for i, j in up]
    return lax.ppermute(x, "blk", up), lax.ppermute(x, "blk", down)


def with_halo(vector):
    swap_a, swap_b = swaps(vector, "strip", STRIPS)
    own = pl.pallas_call(edges, out_shape=shape(5, ROWS, LEN), in_specs=[VMEM] * 3, out_specs=VMEM, compiler_params=limit(4), name="edges")(
        vector, swap_a, swap_b
    )
    return (own, *sides(own))


def local(vector, conductivity, near_kernel, near_pair, far_right, far_left, far_source_row, far_target_row):
    right = in_hbm(jnp.transpose(far_right[0], (0, 2, 1, 3)))
    left = in_hbm(jnp.transpose(far_left[0], (0, 2, 1, 3)))
    near_kernel = in_hbm(near_kernel)
    source_row, target_row = in_hbm(far_source_row), in_hbm(far_target_row)
    block, slots, line = shape(4, ROWS, LEN), shape(DEVICES, 4, LEN), shape(1, LEN)

    local_call = functools.partial(
        pl.pallas_call,
        local_part,
        out_shape=(block, block),
        in_specs=[SMEM, VMEM, VMEM, VMEM, VMEM, HBM],
        out_specs=(VMEM, VMEM),
        scratch_shapes=[pltpu.VMEM((4, HALO, LEN), F32)] + near_scratch(),
        compiler_params=limit(20),
        cost_estimate=pl.CostEstimate(flops=4 * 10**8, bytes_accessed=2 * 10**7, transcendentals=0),
        name="local_part",
    )

    blocks = with_halo(vector)
    start = blocks[0]
    payload = pl.pallas_call(
        first_far,
        out_shape=slots,
        in_specs=[HBM, HBM, VMEM, ANY, ANY, HBM, HBM],
        out_specs=VMEM,
        scratch_shapes=far_scratch(1, 2),
        compiler_params=limit(12),
        name="first_far",
    )(source_row, target_row, blocks[0], blocks[1], blocks[2], right, left)
    received_one = exchange(payload)
    rounded_one, local_one = local_call()(near_pair, conductivity, *blocks, near_kernel)
    image, far_one, row = pl.pallas_call(
        first_image,
        out_shape=(block, shape(3, ROWS, LEN), line),
        in_specs=[VMEM] * 3,
        out_specs=(VMEM,) * 3,
        compiler_params=limit(4),
        name="first_image",
    )(start, rounded_one, received_one)
    blocks = with_halo(image)
    payload = pl.pallas_call(
        second_far,
        out_shape=slots,
        in_specs=[HBM, VMEM, VMEM, ANY, ANY, HBM, HBM],
        out_specs=VMEM,
        scratch_shapes=far_scratch(3, 1),
        compiler_params=limit(12),
        name="second_far",
    )(source_row, image, row, blocks[1], blocks[2], right, left)
    received_two = exchange(payload)
    _, local_two = local_call()(near_pair, conductivity, *blocks, near_kernel)
    first, image_two, scalars, rows = pl.pallas_call(
        second_image,
        out_shape=(block, block, line, shape(DEVICES, LEN)),
        in_specs=[VMEM] * 7,
        out_specs=(VMEM,) * 4,
        compiler_params=limit(4),
        name="second_image",
    )(start, image, local_one, local_two, received_one, received_two, far_one)
    rows = exchange(rows)
    krylov, hessenberg = pl.pallas_call(
        finish,
        out_shape=(shape(2, 4, ROWS, LEN), shape(5)),
        in_specs=[VMEM] * 5,
        out_specs=(VMEM, SMEM),
        compiler_params=limit(4),
        name="finish",
    )(start, first, image_two, scalars, rows)
    return krylov, hessenberg


def solution(mesh):
    in_specs = (
        P(None, "strip", "blk"),
        P(None, "strip", "blk"),
        P(("strip", "blk"), None, None, None, None),
        P(("strip", "blk")),
        P(("strip", "blk"), None, None, None, None),
        P(("strip", "blk"), None, None, None, None),
        P(("strip", "blk"), None),
        P(("strip", "blk"), None),
    )
    out_specs = (P(None, None, "strip", "blk"), P())
    return jax.shard_map(local, mesh=mesh, in_specs=in_specs, out_specs=out_specs, check_vma=False)
```

time: 112 us -> 94.4 us (0.84)
  local copies, waits for them, and re-layouts: 15.5 us -> 0.72 us
  Pallas kernels: 36.7 us -> 28.7 us
  waiting for transfers between devices: 16.1 us -> 24 us
  starting transfers between devices: 27.6 us -> 24.4 us
  blocking collectives: 14.3 us -> 15.5 us
    unnamed x34 -> x6, local copies, waits for them, and re-layouts: 14.3 us -> 0.72 us
    pallas_call x4 -> x9, Pallas kernels: 36.7 us -> 28.7 us  [the longest x1 7.57 us: local(): _, local_two = local_call()(near_pair, conductivity, *blocks, near_kernel)]
    all_to_all x2, waiting for transfers between devices: 2.89 us -> 8.18 us  [exchange(): return lax.all_to_all(x, ('strip', 'blk'), 0, 0, tiled=True)]
    all_to_all x2, starting transfers between devices: 16.1 us -> 12.1 us  [exchange(): return lax.all_to_all(x, ('strip', 'blk'), 0, 0, tiled=True)]
    ppermute x4 -> x8, waiting for transfers between devices: 13.2 us -> 15.9 us  [the longest x4 11.9 us: sides(): return (lax.ppermute(x, 'blk', up), lax.ppermute(x, 'blk', down))]
    all_to_all x1, blocking collectives: 14.3 us -> 15.5 us  [exchange(): return lax.all_to_all(x, ('strip', 'blk'), 0, 0, tiled=True)]
    squeeze x1 -> x0, local copies, waits for them, and re-layouts: 1.18 us -> none  [local(): return (krylov, hessenberg[0, 0:5])]
    ppermute x4 -> x8, starting transfers between devices: 11.4 us -> 12.4 us  [the longest x4 8.28 us: sides(): return (lax.ppermute(x, 'blk', up), lax.ppermute(x, 'blk', down))]
  transfers between devices with their start and end apart: 6 -> 10, of which waited for: 6 -> 8; matrix products, arithmetic and copies ran while one was open for 0% -> 0% of each run, Pallas kernels for 0% -> 15%
where the time goes in v2:
time: 94.4 us; the launch traced here: 94.1 us
  Pallas kernels  28.7 us (30%)
  starting transfers between devices  24.4 us (26%)
  waiting for transfers between devices  24 us (25%)
  blocking collectives  15.5 us (16%)
    all_to_all x1, blocking collectives, exchange(): return lax.all_to_all(x, ('strip', 'blk'), 0, 0, tiled=True)  15.5 us
    all_to_all x2, starting transfers between devices, exchange(): return lax.all_to_all(x, ('strip', 'blk'), 0, 0, tiled=True)  12.1 us
    ppermute x4, waiting for transfers between devices, sides(): return (lax.ppermute(x, 'blk', up), lax.ppermute(x, 'blk', down))  11.9 us
    ppermute x4, starting transfers between devices, sides(): return (lax.ppermute(x, 'blk', up), lax.ppermute(x, 'blk', down))  8.28 us
    all_to_all x2, waiting for transfers between devices, exchange(): return lax.all_to_all(x, ('strip', 'blk'), 0, 0, tiled=True)  8.18 us
    pallas_call x1, Pallas kernels, local(): _, local_two = local_call()(near_pair, conductivity, *blocks, near_kernel)  7.57 us
    pallas_call x1, Pallas kernels, local(): local_call()(near_pair, conductivity, *blocks, near_kernel)  6.97 us
    pallas_call x1, Pallas kernels, local(): pl.pallas_call(second_far, out_shape=slots, in_specs=[HBM, VMEM, VMEM, AN...  5.58 us
  transfers between devices with their start and end apart: 10, of which 8 were waited for; matrix products, arithmetic and copies ran while one was open for 0% of the time, Pallas kernels for 15%

profile of v2, /device:TPU:1, one launch (start us, length us, event | category | flops | bytes accessed | tf_op | source)
XLA Modules:
  0.0 94.1 jit_solution(15217764267655670160)
XLA Ops:
  0.6 1.5 %collective-permute-start = (f32[4,8,128]{2,1,0:T(8,128)}, f32[4,8,128]{2,1,0:T(8,128)S(1)}, u32[]{:S(2)}, u32[]{:S(2)}) collective-permute-start(f32[4,8,128]{2,1,0:T(8,128)} %vector.1), channel_id=1, source_target_pairs={{0,16},{16,0},{32,48},{48,32},{64,80},{80,64},{96,112},{112,96},{1... | collective-permute-start | bytes 49160 | tf_op jit(solution)/shard_map/ppermute | solution.py:388
  2.1 1.3 %collective-permute-start.1 = (f32[4,8,128]{2,1,0:T(8,128)}, f32[4,8,128]{2,1,0:T(8,128)S(1)}, u32[]{:S(2)}, u32[]{:S(2)}) collective-permute-start(f32[4,8,128]{2,1,0:T(8,128)} %vector.1), channel_id=1, source_target_pairs={{0,112},{16,32},{32,16},{48,64},{64,48},{80,96},{96,80},{112,0},{1... | collective-permute-start | bytes 49160 | tf_op jit(solution)/shard_map/ppermute | solution.py:388
  3.4 0.0 collective-permute-done.swap_a
  3.4 2.1 %collective-permute-done.1.swap_b = f32[4,8,128]{2,1,0:T(8,128)S(1)} collective-permute-done((f32[4,8,128]{2,1,0:T(8,128)}, f32[4,8,128]{2,1,0:T(8,128)S(1)}, u32[]{:S(2)}, u32[]{:S(2)}) %collective-permute-start.1) | collective-permute-done | bytes 16416 | tf_op jit(solution)/shard_map/ppermute | solution.py:388
  5.5 0.0 copy-start.1
  5.5 0.7 copy-done.1
  6.2 6.4 %collective-permute-start.3 = (f32[5,8,128]{2,1,0:T(8,128)S(1)}, f32[5,8,128]{2,1,0:T(8,128)S(1)}, u32[]{:S(2)}, u32[]{:S(2)}) collective-permute-start(f32[5,8,128]{2,1,0:T(8,128)S(1)} %edges.2.own.vector), channel_id=1, source_target_pairs={{1,0},{2,1},{3,2},{4,3},{5,4},{6,5},{7,6},{8,7},{9,8},{10,9},{11,1... | collective-permute-start | bytes 61448 | tf_op jit(solution)/shard_map/ppermute | solution.py:394
  12.6 0.0 collective-permute-start.2
  12.6 0.9 collective-permute-done.3.right.after_1
  13.5 5.0 %collective-permute-done.2.left.after_0 = f32[5,8,128]{2,1,0:T(8,128)S(1)} collective-permute-done((f32[5,8,128]{2,1,0:T(8,128)S(1)}, f32[5,8,128]{2,1,0:T(8,128)S(1)}, u32[]{:S(2)}, u32[]{:S(2)}) %collective-permute-start.2) | collective-permute-done | bytes 20512 | tf_op jit(solution)/shard_map/ppermute | solution.py:394
  18.6 5.4 %first_far.1 = f32[128,4,128]{2,1,0:T(4,128)} custom-call(s32[1,128]{1,0:T(1,128)} %source_hbm.3, s32[1,128]{1,0:T(1,128)} %target_hbm.1, f32[5,8,128]{2,1,0:T(8,128)S(1)} %edges.2.own.vector, f32[5,8,128]{2,1,0:T(8,128)S(1)} %collective-permute-done.2.left.after_0, f32[5,8,128]{2,1,0:T(8,128)S(1)} %collective-permute-done.3.right.after_1, ...), custom_call_target="tpu_custom_call" | custom-call | tf_op jit(solution)/shard_map/first_far/pallas_call | solution.py:426
  23.9 6.2 %all-to-all-start = ((f32[128,4,128]{2,1,0:T(4,128)}), f32[128,4,128]{2,1,0:T(4,128)S(1)}, u32[]{:S(2)}, u32[]{:S(2)}) async-start(f32[128,4,128]{2,1,0:T(4,128)} %first_far.1), calls=%async_computation | async-start | bytes 524288 | tf_op jit(solution)/shard_map/all_to_all | solution.py:382
  30.1 0.0 copy-done
  30.1 0.0 copy-done.2
  30.1 7.0 %local_part.2 = (f32[4,8,128]{2,1,0:T(8,128)S(1)}, f32[4,8,128]{2,1,0:T(8,128)S(1)}) custom-call(s32[48]{0:T(128)S(1)} %copy-done.2, f32[4,8,128]{2,1,0:T(8,128)S(1)} %copy-done, f32[5,8,128]{2,1,0:T(8,128)S(1)} %edges.2.own.vector, f32[5,8,128]{2,1,0:T(8,128)S(1)} %collective-permute-done.2.left.after_0, ...), custom_call_target="tpu_custom_call" | custom-call | flops 400000000 | bytes 20000000 | tf_op jit(solution)/shard_map/local_part/pallas_call | solution.py:436
  37.1 4.4 %all-to-all-done.received.target = f32[128,4,128]{2,1,0:T(4,128)S(1)} async-done(((f32[128,4,128]{2,1,0:T(4,128)}), f32[128,4,128]{2,1,0:T(4,128)S(1)}, u32[]{:S(2)}, u32[]{:S(2)}) %all-to-all-start) | async-done | bytes 262176 | tf_op jit(solution)/shard_map/all_to_all | solution.py:382
  41.5 0.5 first_image.1
  41.9 0.9 collective-permute-start.5
  42.9 0.4 collective-permute-start.4
  43.3 1.9 %collective-permute-done.5.swap_b = f32[4,8,128]{2,1,0:T(8,128)S(1)} collective-permute-done((f32[4,8,128]{2,1,0:T(8,128)S(1)}, f32[4,8,128]{2,1,0:T(8,128)S(1)}, u32[]{:S(2)}, u32[]{:S(2)}) %collective-permute-start.5) | collective-permute-done | bytes 16416 | tf_op jit(solution)/shard_map/ppermute | solution.py:388
  45.1 0.0 collective-permute-done.4.swap_a
  45.1 1.9 %collective-permute-start.7 = (f32[5,8,128]{2,1,0:T(8,128)S(1)}, f32[5,8,128]{2,1,0:T(8,128)S(1)}, u32[]{:S(2)}, u32[]{:S(2)}) collective-permute-start(f32[5,8,128]{2,1,0:T(8,128)S(1)} %edges.3.own), channel_id=1, source_target_pairs={{1,0},{2,1},{3,2},{4,3},{5,4},{6,5},{7,6},{8,7},{9,8},{10,9},{11,1... | collective-permute-start | bytes 61448 | tf_op jit(solution)/shard_map/ppermute | solution.py:394
  47.1 0.0 collective-permute-start.6
  47.1 0.9 collective-permute-done.7.right.after_1
  48.0 5.0 %collective-permute-done.6.left.after_0 = f32[5,8,128]{2,1,0:T(8,128)S(1)} collective-permute-done((f32[5,8,128]{2,1,0:T(8,128)S(1)}, f32[5,8,128]{2,1,0:T(8,128)S(1)}, u32[]{:S(2)}, u32[]{:S(2)}) %collective-permute-start.6) | collective-permute-done | bytes 20512 | tf_op jit(solution)/shard_map/ppermute | solution.py:394
  53.0 5.6 %second_far.1 = f32[128,4,128]{2,1,0:T(4,128)} custom-call(s32[1,128]{1,0:T(1,128)} %source_hbm.3, f32[4,8,128]{2,1,0:T(8,128)S(1)} %get-tuple-element.13.vector.image, f32[1,128]{1,0:T(1,128)S(1)} %get-tuple-element.16.row, f32[5,8,128]{2,1,0:T(8,128)S(1)} %collective-permute-done.6.left.after_0, f32[5,8,128]{2,1,0:T(8,128)S(1)} %collective-permute-done.7.right.after_1, ...), custom_call_target="tpu_custom_call" | custom-call | tf_op jit(solution)/shard_map/second_far/pallas_call | solution.py:446
  58.6 5.9 %all-to-all-start.1 = ((f32[128,4,128]{2,1,0:T(4,128)}), f32[128,4,128]{2,1,0:T(4,128)S(1)}, u32[]{:S(2)}, u32[]{:S(2)}) async-start(f32[128,4,128]{2,1,0:T(4,128)} %second_far.1), calls=%async_computation.1 | async-start | bytes 524288 | tf_op jit(solution)/shard_map/all_to_all | solution.py:382
  64.5 7.6 %local_part.3 = (f32[4,8,128]{2,1,0:T(8,128)}, f32[4,8,128]{2,1,0:T(8,128)S(1)}) custom-call(s32[48]{0:T(128)S(1)} %copy-done.2, f32[4,8,128]{2,1,0:T(8,128)S(1)} %copy-done, f32[5,8,128]{2,1,0:T(8,128)S(1)} %edges.3.own, f32[5,8,128]{2,1,0:T(8,128)S(1)} %collective-permute-done.6.left.after_0, f32[5,8,128]{2,1,0:T(8,128)S(1)} %collective-permute-done.7.right.after_1, ...), custom_call_target="tpu_custom_call" | custom-call | flops 400000000 | bytes 20000000 | tf_op jit(solution)/shard_map/local_part/pallas_call | solution.py:456
  72.1 3.8 %all-to-all-done.1.received = f32[128,4,128]{2,1,0:T(4,128)S(1)} async-done(((f32[128,4,128]{2,1,0:T(4,128)}), f32[128,4,128]{2,1,0:T(4,128)S(1)}, u32[]{:S(2)}, u32[]{:S(2)}) %all-to-all-start.1) | async-done | bytes 262176 | tf_op jit(solution)/shard_map/all_to_all | solution.py:382
  75.9 1.3 %second_image.1 = (f32[4,8,128]{2,1,0:T(8,128)S(1)}, f32[4,8,128]{2,1,0:T(8,128)S(1)}, f32[1,128]{1,0:T(1,128)S(1)}, f32[128,128]{1,0:T(8,128)S(1)}) custom-call(f32[5,8,128]{2,1,0:T(8,128)S(1)} %edges.2.own.vector, f32[4,8,128]{2,1,0:T(8,128)S(1)} %get-tuple-element.13.vector.image, f32[4,8,128]{2,1,0:T(8,128)S(1)} %get-tuple-element.14.local_one, ...), custom_call_target="tpu_custom_call" | custom-call | tf_op jit(solution)/shard_map/second_image/pallas_call | solution.py:457
  77.2 15.5 %all_to_all.21 = f32[128,1,128]{2,1,0:T(1,128)S(1)} all-to-all(f32[128,1,128]{2,1,0:T(1,128)S(1)} %bitcast.11), channel_id=1, replica_groups=mesh['strip'=8,'blk'=16] {'strip','blk'}, dimensions={0} | all-to-all | bytes 131072 | tf_op jit(solution)/shard_map/all_to_all | solution.py:382
  92.7 1.4 %finish.1 = (f32[2,4,8,128]{3,2,1,0:T(8,128)}, f32[5]{0:T(128)}) custom-call(f32[5,8,128]{2,1,0:T(8,128)S(1)} %edges.2.own.vector, f32[4,8,128]{2,1,0:T(8,128)S(1)} %get-tuple-element.18.first, f32[4,8,128]{2,1,0:T(8,128)S(1)} %get-tuple-element.19.image, f32[1,128]{1,0:T(1,128)S(1)} %get-tuple-element.20.scalars, f32[128,128]{1,0:T(8,128)S(1)} %bitcast.10), custom_call_target="tpu_custom_call" | custom-call | tf_op jit(solution)/shard_map/finish/pallas_call | solution.py:466
  (4 shorter events, 0.0 us)
Async XLA Ops:
  0.6 2.8 %collective-permute-start = (f32[4,8,128]{2,1,0:T(8,128)}, f32[4,8,128]{2,1,0:T(8,128)S(1)}, u32[]{:S(2)}, u32[]{:S(2)}) collective-permute-start(f32[4,8,128]{2,1,0:T(8,128)} %vector.1), channel_id=1, source_target_pairs={{0,16},{16,0},{32,48},{48,32},{64,80},{80,64},{96,112},{112,96},{1... | collective-permute-start | bytes 49160 | tf_op jit(solution)/shard_map/ppermute | solution.py:388
  2.1 3.4 %collective-permute-start.1 = (f32[4,8,128]{2,1,0:T(8,128)}, f32[4,8,128]{2,1,0:T(8,128)S(1)}, u32[]{:S(2)}, u32[]{:S(2)}) collective-permute-start(f32[4,8,128]{2,1,0:T(8,128)} %vector.1), channel_id=1, source_target_pairs={{0,112},{16,32},{32,16},{48,64},{64,48},{80,96},{96,80},{112,0},{1... | collective-permute-start | bytes 49160 | tf_op jit(solution)/shard_map/ppermute | solution.py:388
  5.5 0.7 copy-start.1
  6.2 7.3 %collective-permute-start.3 = (f32[5,8,128]{2,1,0:T(8,128)S(1)}, f32[5,8,128]{2,1,0:T(8,128)S(1)}, u32[]{:S(2)}, u32[]{:S(2)}) collective-permute-start(f32[5,8,128]{2,1,0:T(8,128)S(1)} %edges.2.own.vector), channel_id=1, source_target_pairs={{1,0},{2,1},{3,2},{4,3},{5,4},{6,5},{7,6},{8,7},{9,8},{10,9},{11,1... | collective-permute-start | bytes 61448 | tf_op jit(solution)/shard_map/ppermute | solution.py:394
  12.6 6.0 %collective-permute-start.2 = (f32[5,8,128]{2,1,0:T(8,128)S(1)}, f32[5,8,128]{2,1,0:T(8,128)S(1)}, u32[]{:S(2)}, u32[]{:S(2)}) collective-permute-start(f32[5,8,128]{2,1,0:T(8,128)S(1)} %edges.2.own.vector), channel_id=1, source_target_pairs={{0,1},{1,2},{2,3},{3,4},{4,5},{5,6},{6,7},{7,8},{8,9},{9,10},{10,1... | collective-permute-start | bytes 61448 | tf_op jit(solution)/shard_map/ppermute | solution.py:394
  18.6 11.5 %copy-start = (f32[4,8,128]{2,1,0:T(8,128)S(1)}, f32[4,8,128]{2,1,0:T(8,128)}, u32[]{:S(2)}) copy-start(f32[4,8,128]{2,1,0:T(8,128)} %conductivity.3) | copy-start | bytes 49156
  18.6 11.5 %copy-start.2 = (s32[48]{0:T(128)S(1)}, s32[48]{0:T(128)}, u32[]{:S(2)}) copy-start(s32[48]{0:T(128)} %near_pair.3) | copy-start | bytes 580
  23.9 17.5 %all-to-all-start = ((f32[128,4,128]{2,1,0:T(4,128)}), f32[128,4,128]{2,1,0:T(4,128)S(1)}, u32[]{:S(2)}, u32[]{:S(2)}) async-start(f32[128,4,128]{2,1,0:T(4,128)} %first_far.1), calls=%async_computation | async-start | bytes 524288 | tf_op jit(solution)/shard_map/all_to_all | solution.py:382
  41.9 3.2 %collective-permute-start.5 = (f32[4,8,128]{2,1,0:T(8,128)S(1)}, f32[4,8,128]{2,1,0:T(8,128)S(1)}, u32[]{:S(2)}, u32[]{:S(2)}) collective-permute-start(f32[4,8,128]{2,1,0:T(8,128)S(1)} %get-tuple-element.13.vector.image), channel_id=1, source_target_pairs={{0,112},{16,32},{32,16},{48,64},{64,48},{80,96},{96,80},{112,0},{1... | collective-permute-start | bytes 49160 | tf_op jit(solution)/shard_map/ppermute | solution.py:388
  42.9 2.3 %collective-permute-start.4 = (f32[4,8,128]{2,1,0:T(8,128)S(1)}, f32[4,8,128]{2,1,0:T(8,128)S(1)}, u32[]{:S(2)}, u32[]{:S(2)}) collective-permute-start(f32[4,8,128]{2,1,0:T(8,128)S(1)} %get-tuple-element.13.vector.image), channel_id=1, source_target_pairs={{0,16},{16,0},{32,48},{48,32},{64,80},{80,64},{96,112},{112,96},{1... | collective-permute-start | bytes 49160 | tf_op jit(solution)/shard_map/ppermute | solution.py:388
  45.1 2.8 %collective-permute-start.7 = (f32[5,8,128]{2,1,0:T(8,128)S(1)}, f32[5,8,128]{2,1,0:T(8,128)S(1)}, u32[]{:S(2)}, u32[]{:S(2)}) collective-permute-start(f32[5,8,128]{2,1,0:T(8,128)S(1)} %edges.3.own), channel_id=1, source_target_pairs={{1,0},{2,1},{3,2},{4,3},{5,4},{6,5},{7,6},{8,7},{9,8},{10,9},{11,1... | collective-permute-start | bytes 61448 | tf_op jit(solution)/shard_map/ppermute | solution.py:394
  47.1 6.0 %collective-permute-start.6 = (f32[5,8,128]{2,1,0:T(8,128)S(1)}, f32[5,8,128]{2,1,0:T(8,128)S(1)}, u32[]{:S(2)}, u32[]{:S(2)}) collective-permute-start(f32[5,8,128]{2,1,0:T(8,128)S(1)} %edges.3.own), channel_id=1, source_target_pairs={{0,1},{1,2},{2,3},{3,4},{4,5},{5,6},{6,7},{7,8},{8,9},{9,10},{10,1... | collective-permute-start | bytes 61448 | tf_op jit(solution)/shard_map/ppermute | solution.py:394
  58.6 17.3 %all-to-all-start.1 = ((f32[128,4,128]{2,1,0:T(4,128)}), f32[128,4,128]{2,1,0:T(4,128)S(1)}, u32[]{:S(2)}, u32[]{:S(2)}) async-start(f32[128,4,128]{2,1,0:T(4,128)} %second_far.1), calls=%async_computation.1 | async-start | bytes 524288 | tf_op jit(solution)/shard_map/all_to_all | solution.py:382

commit v3 on v2

--- a/solution.py
+++ b/solution.py
@@ -150,39 +150,53 @@
     return a, b, c
 
 
-def far(payload, vector, source_row, right_hbm, left_hbm, right, left, right_sems, left_sems, gathered, coefficients, parts):
-    row = lax.broadcasted_iota(jnp.int32, (LEN, LEN), 0)
-    from_row = jnp.where(row == source_row, 1.0, 0.0).T.astype(BF16)
+def own_block():
+    sub = lax.broadcasted_iota(jnp.int32, (FAR_CHUNK, FAR_CHUNK * RANK), 0)
+    lane = lax.broadcasted_iota(jnp.int32, (FAR_CHUNK, FAR_CHUNK * RANK), 1)
+    return lane // RANK == sub
+
+
+def summed(x, parts):
+    if parts == 1:
+        return x
+    return x[0:FAR_CHUNK] + (x[FAR_CHUNK : 2 * FAR_CHUNK] + x[2 * FAR_CHUNK :])
+
+
+def project(parts, source_hbm, vector_in, right_hbm, coefficients, vector, right, sems, gathered, rows, row_sem, vector_sem):
+    copy = pltpu.make_async_copy(source_hbm, rows, row_sem)
+    vector_copy = pltpu.make_async_copy(vector_in, vector, vector_sem)
+    copy.start()
+    vector_copy.start()
+    for n in range(FAR_COPIES):
+        far_copy(right_hbm, right, sems, n).start()
+    vector_copy.wait()
     pieces = [[x.astype(BF16)] if parts == 1 else split3(x) for x in (vector[b] for b in range(3))]
     below = jnp.zeros((LEN - ROWS, LEN), F32)
     sources = [jnp.concatenate([pieces[b][k].astype(F32), below], axis=0).astype(BF16) for k in range(parts) for b in range(3)]
     sources = jnp.concatenate(sources, axis=1)
+    row = lax.broadcasted_iota(jnp.int32, (LEN, LEN), 0)
+    copy.wait()
+    from_row = jnp.where(row == rows[...], 1.0, 0.0).T.astype(BF16)
     gathered[...] = lax.dot_general(from_row, sources, PLAIN, preferred_element_type=F32).astype(BF16)
-    rows = FAR_CHUNK * RANK
-    sub = lax.broadcasted_iota(jnp.int32, (FAR_CHUNK, rows), 0)
-    lane = lax.broadcasted_iota(jnp.int32, (FAR_CHUNK, rows), 1)
-    own = lane // RANK == sub
-
-    def summed(x):
-        if parts == 1:
-            return x
-        return x[0:FAR_CHUNK] + (x[FAR_CHUNK : 2 * FAR_CHUNK] + x[2 * FAR_CHUNK :])
-
+    own = own_block()
     for n in range(FAR_CHUNKS):
         if n % FAR_PER_COPY == 0:
-            far_copy(right_hbm, right, right_sems, n // FAR_PER_COPY).wait()
+            far_copy(right_hbm, right, sems, n // FAR_PER_COPY).wait()
         d = pl.ds(n * FAR_CHUNK, FAR_CHUNK)
         source = jnp.concatenate([gathered[d, 3 * LEN * k : 3 * LEN * (k + 1)] for k in range(parts)], axis=0)
-        matrix = jnp.concatenate([right[d, b].reshape(rows, LEN) for b in range(3)], axis=1)
-        c = summed(lax.dot_general(source, matrix, TRANS_B, preferred_element_type=F32))
+        matrix = jnp.concatenate([right[d, b].reshape(FAR_CHUNK * RANK, LEN) for b in range(3)], axis=1)
+        c = summed(lax.dot_general(source, matrix, TRANS_B, preferred_element_type=F32), parts)
         c = jnp.where(own, c, 0.0)
         coefficients[n] = c.astype(BF16) if parts == 1 else jnp.concatenate(split3(c), axis=0)
+
+
+def expand(parts, coefficients, left_hbm, payload, left, sems):
     for n in range(FAR_CHUNKS):
         if n % FAR_PER_COPY == 0:
-            far_copy(left_hbm, left, left_sems, n // FAR_PER_COPY).wait()
+            far_copy(left_hbm, left, sems, n // FAR_PER_COPY).wait()
         d = pl.ds(n * FAR_CHUNK, FAR_CHUNK)
-        matrix = jnp.concatenate([left[d, a].reshape(rows, LEN) for a in range(3)], axis=1)
-        result = summed(lax.dot_general(coefficients[n], matrix, PLAIN, preferred_element_type=F32))
+        matrix = jnp.concatenate([left[d, a].reshape(FAR_CHUNK * RANK, LEN) for a in range(3)], axis=1)
+        result = summed(lax.dot_general(coefficients[n], matrix, PLAIN, preferred_element_type=F32), parts)
         for a in range(3):
             payload[d, a, :] = result[:, a * LEN : (a + 1) * LEN]
 
@@ -219,17 +233,8 @@
     return out + [vector[3] + vector[0] - local[3]]
 
 
-def far_scratch(parts, rows):
-    return [
-        pltpu.VMEM((DEVICES, 3, RANK, LEN), BF16),
-        pltpu.VMEM((DEVICES, 3, RANK, LEN), BF16),
-        pltpu.SemaphoreType.DMA((FAR_COPIES,)),
-        pltpu.SemaphoreType.DMA((FAR_COPIES,)),
-        pltpu.VMEM((DEVICES, parts * 3 * LEN), BF16),
-        pltpu.VMEM((FAR_CHUNKS, parts * FAR_CHUNK, FAR_CHUNK * RANK), BF16),
-        pltpu.VMEM((rows, 1, LEN), jnp.int32),
-        pltpu.SemaphoreType.DMA((rows,)),
-    ]
+def far_scratch():
+    return [pltpu.VMEM((DEVICES, 3, RANK, LEN), BF16), pltpu.SemaphoreType.DMA((FAR_COPIES,))]
 
 
 def near_scratch():
@@ -239,46 +244,26 @@
     ]
 
 
-def start_far(right_hbm, left_hbm, right, left, right_sems, left_sems):
-    for n in range(FAR_COPIES):
-        far_copy(right_hbm, right, right_sems, n).start()
-    for n in range(FAR_COPIES):
-        far_copy(left_hbm, left, left_sems, n).start()
-
-
-def row_copies(sources, rows, sems):
-    return [pltpu.make_async_copy(source, rows.at[i], sems.at[i]) for i, source in enumerate(sources)]
-
-
 def start_near(kernel_hbm, kernels, sems):
     for n in range(NEAR_CHUNKS):
         near_copy(kernel_hbm, kernels, sems, n).start()
 
 
-def first_far(
-    source_hbm, target_hbm, vector, after_0, after_1, right_hbm, left_hbm, payload,
-    right, left, right_sems, left_sems, gathered, coefficients, rows, row_sems,
-):
-    copies = row_copies((source_hbm, target_hbm), rows, row_sems)
-    for copy in copies:
-        copy.start()
-    start_far(right_hbm, left_hbm, right, left, right_sems, left_sems)
-    for copy in copies:
-        copy.wait()
-    payload[:, 3, :] = jnp.broadcast_to(rows[1].astype(F32), (DEVICES, LEN)).T
-    far(payload, vector, rows[0], right_hbm, left_hbm, right, left, right_sems, left_sems, gathered, coefficients, 1)
-
-
-def second_far(
-    source_hbm, vector, row, after_0, after_1, right_hbm, left_hbm, payload,
-    right, left, right_sems, left_sems, gathered, coefficients, rows, row_sems,
-):
-    (copy,) = row_copies((source_hbm,), rows, row_sems)
+def first_expand(target_hbm, after, coefficients, left_hbm, payload, left, sems, rows, row_sem):
+    copy = pltpu.make_async_copy(target_hbm, rows, row_sem)
     copy.start()
-    start_far(right_hbm, left_hbm, right, left, right_sems, left_sems)
+    for n in range(FAR_COPIES):
+        far_copy(left_hbm, left, sems, n).start()
+    copy.wait()
+    payload[:, 3, :] = jnp.broadcast_to(rows[...].astype(F32), (DEVICES, LEN)).T
+    expand(1, coefficients, left_hbm, payload, left, sems)
+
+
+def second_expand(row, after, coefficients, left_hbm, payload, left, sems):
+    for n in range(FAR_COPIES):
+        far_copy(left_hbm, left, sems, n).start()
     payload[:, 3, :] = jnp.broadcast_to(row[...], (DEVICES, LEN))
-    copy.wait()
-    far(payload, vector, rows[0], right_hbm, left_hbm, right, left, right_sems, left_sems, gathered, coefficients, 3)
+    expand(3, coefficients, left_hbm, payload, left, sems)
 
 
 def edges(vector, swap_a, swap_b, out):
@@ -291,15 +276,17 @@
     out[4, 4:8, :] = jnp.where(strip < STRIPS - 1, below, 0.0)
 
 
-def local_part(near_pair, conductivity, own, left, right, kernel_hbm, rounded, full, around, kernels, sems):
+def local_part(near_pair, conductivity, own, swap_a, swap_b, kernel_hbm, rounded, full, around, kernels, sems):
     start_near(kernel_hbm, kernels, sems)
     _, blk = place()
-    for column, blocks, inside in ((0, left, blk > 0), (1, own, None), (2, right, blk < BLKS - 1)):
-        keep = (lambda x: x) if inside is None else (lambda x, inside=inside: jnp.where(inside, x, 0.0))
+    even = lax.rem(blk, 2) == 0
+    left = jnp.where(blk > 0, jnp.where(even, swap_b[...], swap_a[...]), 0.0)
+    right = jnp.where(blk < BLKS - 1, jnp.where(even, swap_a[...], swap_b[...]), 0.0)
+    for column, blocks in enumerate((left, own[...], right)):
         base = 10 * column
-        around[:, base + 1 : base + 9, :] = keep(blocks[0:4])
-        around[:, base, :] = keep(blocks[4, 0:4, :])
-        around[:, base + 9, :] = keep(blocks[4, 4:8, :])
+        around[:, base + 1 : base + 9, :] = blocks[0:4]
+        around[:, base, :] = blocks[4, 0:4]
+        around[:, base + 9, :] = blocks[4, 4:8]
     flux_sum = flux(around, conductivity)
     rounded[3] = flux_sum
     full[3] = flux_sum
@@ -388,18 +375,35 @@
     return lax.ppermute(x, axis, even), lax.ppermute(x, axis, odd)
 
 
-def sides(x):
-    up = [(i, (i + 1) % BLKS) for i in range(BLKS)]
-    down = [(j, i) for i, j in up]
-    return lax.ppermute(x, "blk", up), lax.ppermute(x, "blk", down)
-
-
-def with_halo(vector):
+def own_blocks(parts, source_row, vector, right):
     swap_a, swap_b = swaps(vector, "strip", STRIPS)
-    own = pl.pallas_call(edges, out_shape=shape(5, ROWS, LEN), in_specs=[VMEM] * 3, out_specs=VMEM, compiler_params=limit(4), name="edges")(
-        vector, swap_a, swap_b
-    )
-    return (own, *sides(own))
+    coefficients, vector = projected(parts, source_row, in_hbm(vector) if parts == 1 else vector, right)
+    own = pl.pallas_call(
+        edges,
+        out_shape=shape(5, ROWS, LEN),
+        in_specs=[VMEM] * 3,
+        out_specs=VMEM,
+        compiler_params=limit(4),
+        name="edges",
+    )(vector, swap_a, swap_b)
+    return own, coefficients
+
+
+def projected(parts, source_row, vector, right):
+    return pl.pallas_call(
+        functools.partial(project, parts),
+        out_shape=(
+            jax.ShapeDtypeStruct((FAR_CHUNKS, parts * FAR_CHUNK, FAR_CHUNK * RANK), BF16),
+            shape(4, ROWS, LEN),
+        ),
+        in_specs=[HBM, HBM if parts == 1 else ANY, HBM],
+        out_specs=(VMEM, VMEM),
+        scratch_shapes=far_scratch()
+        + [pltpu.VMEM((DEVICES, parts * 3 * LEN), BF16), pltpu.VMEM((1, LEN), jnp.int32), pltpu.SemaphoreType.DMA, pltpu.SemaphoreType.DMA],
+        compiler_params=limit(12),
+        cost_estimate=pl.CostEstimate(flops=2 * 10**8, bytes_accessed=10**7, transcendentals=0),
+        name="project",
+    )(source_row, vector, right)
 
 
 def local(vector, conductivity, near_kernel, near_pair, far_right, far_left, far_source_row, far_target_row):
@@ -421,17 +425,24 @@
         name="local_part",
     )
 
-    blocks = with_halo(vector)
-    start = blocks[0]
-    payload = pl.pallas_call(
-        first_far,
+    expand_call = functools.partial(
+        pl.pallas_call,
         out_shape=slots,
-        in_specs=[HBM, HBM, VMEM, ANY, ANY, HBM, HBM],
         out_specs=VMEM,
-        scratch_shapes=far_scratch(1, 2),
         compiler_params=limit(12),
-        name="first_far",
-    )(source_row, target_row, blocks[0], blocks[1], blocks[2], right, left)
+        cost_estimate=pl.CostEstimate(flops=2 * 10**8, bytes_accessed=10**7, transcendentals=0),
+    )
+
+    start, coefficients = own_blocks(1, source_row, vector, right)
+    blocks = swaps(start, "blk", BLKS)
+    payload = expand_call(
+        first_expand,
+        in_specs=[HBM, ANY, VMEM, HBM],
+        scratch_shapes=far_scratch() + [pltpu.VMEM((1, LEN), jnp.int32), pltpu.SemaphoreType.DMA],
+        name="first_expand",
+    )(target_row, start, coefficients, left)
+    payload, *blocks = lax.optimization_barrier((payload, *blocks))
+    blocks = (start, *blocks)
     received_one = exchange(payload)
     rounded_one, local_one = local_call()(near_pair, conductivity, *blocks, near_kernel)
     image, far_one, row = pl.pallas_call(
@@ -442,16 +453,13 @@
         compiler_params=limit(4),
         name="first_image",
     )(start, rounded_one, received_one)
-    blocks = with_halo(image)
-    payload = pl.pallas_call(
-        second_far,
-        out_shape=slots,
-        in_specs=[HBM, VMEM, VMEM, ANY, ANY, HBM, HBM],
-        out_specs=VMEM,
-        scratch_shapes=far_scratch(3, 1),
-        compiler_params=limit(12),
-        name="second_far",
-    )(source_row, image, row, blocks[1], blocks[2], right, left)
+    own, coefficients = own_blocks(3, source_row, image, right)
+    blocks = swaps(own, "blk", BLKS)
+    payload = expand_call(
+        second_expand, in_specs=[VMEM, ANY, VMEM, HBM], scratch_shapes=far_scratch(), name="second_expand"
+    )(row, own, coefficients, left)
+    payload, *blocks = lax.optimization_barrier((payload, *blocks))
+    blocks = (own, *blocks)
     received_two = exchange(payload)
     _, local_two = local_call()(near_pair, conductivity, *blocks, near_kernel)
     first, image_two, scalars, rows = pl.pallas_call(

time: 94.4 us -> 81.9 us (0.87)
  waiting for transfers between devices: 24 us -> 8.13 us
  starting transfers between devices: 24.4 us -> 27.8 us
    ppermute x4 -> x0, waiting for transfers between devices: 11.9 us -> none  [sides(): return (lax.ppermute(x, 'blk', up), lax.ppermute(x, 'blk', down))]
    ppermute x4 -> x8, starting transfers between devices: 4.09 us -> 14.3 us  [swaps(): return (lax.ppermute(x, axis, even), lax.ppermute(x, axis, odd))]
    ppermute x4 -> x0, starting transfers between devices: 8.28 us -> none  [sides(): return (lax.ppermute(x, 'blk', up), lax.ppermute(x, 'blk', down))]
    ppermute x4 -> x8, waiting for transfers between devices: 3.96 us -> 0.22 us  [swaps(): return (lax.ppermute(x, axis, even), lax.ppermute(x, axis, odd))]
    all_to_all x2, starting transfers between devices: 12.1 us -> 13.5 us  [exchange(): return lax.all_to_all(x, ('strip', 'blk'), 0, 0, tiled=True)]
    pallas_call x4 -> x6, Pallas kernels: 11 us -> 11.7 us  [the longest x2 5.68 us: projected(): pl.pallas_call(functools.partial(project, parts), out_shape=(jax.ShapeDty...]
  transfers between devices with their start and end apart: 10 -> 10, of which waited for: 8 -> 3; matrix products, arithmetic and copies ran while one was open for 0% -> 0% of each run, Pallas kernels for 15% -> 32%
where the time goes in v3:
time: 81.9 us; the launch traced here: 81.7 us
  Pallas kernels  29.5 us (36%)
  starting transfers between devices  27.8 us (34%)
  blocking collectives  15.5 us (19%)
  waiting for transfers between devices  8.13 us (10%)
    all_to_all x1, blocking collectives, exchange(): return lax.all_to_all(x, ('strip', 'blk'), 0, 0, tiled=True)  15.5 us
    ppermute x8, starting transfers between devices, swaps(): return (lax.ppermute(x, axis, even), lax.ppermute(x, axis, odd))  14.3 us
    all_to_all x2, starting transfers between devices, exchange(): return lax.all_to_all(x, ('strip', 'blk'), 0, 0, tiled=True)  13.5 us
    all_to_all x2, waiting for transfers between devices, exchange(): return lax.all_to_all(x, ('strip', 'blk'), 0, 0, tiled=True)  7.91 us
    pallas_call x1, Pallas kernels, local(): _, local_two = local_call()(near_pair, conductivity, *blocks, near_kernel)  7.57 us
    pallas_call x1, Pallas kernels, local(): local_call()(near_pair, conductivity, *blocks, near_kernel)  6.97 us
    pallas_call x2, Pallas kernels, projected(): pl.pallas_call(functools.partial(project, parts), out_shape=(jax.ShapeDty...  5.68 us
    pallas_call x1, Pallas kernels, local(): expand_call(first_expand, in_specs=[HBM, ANY, VMEM, HBM], scratch_shapes=...  3.14 us
  transfers between devices with their start and end apart: 10, of which 3 were waited for; matrix products, arithmetic and copies ran while one was open for 0% of the time, Pallas kernels for 32%

profile of v3, /device:TPU:1, one launch (start us, length us, event | category | flops | bytes accessed | tf_op | source)
XLA Modules:
  0.0 81.7 jit_solution(12063693939054831959)
XLA Ops:
  0.6 2.7 %collective-permute-start.1 = (f32[4,8,128]{2,1,0:T(8,128)}, f32[4,8,128]{2,1,0:T(8,128)S(1)}, u32[]{:S(2)}, u32[]{:S(2)}) collective-permute-start(f32[4,8,128]{2,1,0:T(8,128)} %vector_in.1), channel_id=1, source_target_pairs={{0,112},{16,32},{32,16},{48,64},{64,48},{80,96},{96,80},{112,0},{1... | collective-permute-start | bytes 49160 | tf_op jit(solution)/shard_map/ppermute | solution.py:375
  3.3 1.1 %collective-permute-start = (f32[4,8,128]{2,1,0:T(8,128)}, f32[4,8,128]{2,1,0:T(8,128)S(1)}, u32[]{:S(2)}, u32[]{:S(2)}) collective-permute-start(f32[4,8,128]{2,1,0:T(8,128)} %vector_in.1), channel_id=1, source_target_pairs={{0,16},{16,0},{32,48},{48,32},{64,80},{80,64},{96,112},{112,96},{1... | collective-permute-start | bytes 49160 | tf_op jit(solution)/shard_map/ppermute | solution.py:375
  4.4 3.0 %project.2 = (bf16[8,16,512]{2,1,0:T(8,128)(2,1)S(1)}, f32[4,8,128]{2,1,0:T(8,128)S(1)}) custom-call(s32[1,128]{1,0:T(1,128)} %source_hbm.3, f32[4,8,128]{2,1,0:T(8,128)} %vector_in.1, bf16[128,3,32,128]{3,2,1,0:T(8,128)(2,1)} %bitcast.14), custom_call_target="tpu_custom_call" | custom-call | flops 200000000 | bytes 10000000 | tf_op jit(solution)/shard_map/project/pallas_call | solution.py:393
  7.5 0.0 collective-permute-done.1.swap_b
  7.5 0.0 collective-permute-done.swap_a
  7.5 6.3 %collective-permute-start.3 = (f32[5,8,128]{2,1,0:T(8,128)S(1)}, f32[5,8,128]{2,1,0:T(8,128)S(1)}, u32[]{:S(2)}, u32[]{:S(2)}) collective-permute-start(f32[5,8,128]{2,1,0:T(8,128)S(1)} %edges.2.after.own.vector), channel_id=1, source_target_pairs={{0,15},{1,2},{2,1},{3,4},{4,3},{5,6},{6,5},{7,8},{8,7},{9,10},{10,... | collective-permute-start | bytes 61448 | tf_op jit(solution)/shard_map/ppermute | solution.py:375
  13.8 0.0 collective-permute-start.2
  13.8 3.1 %first_expand.1 = f32[128,4,128]{2,1,0:T(4,128)} custom-call(s32[1,128]{1,0:T(1,128)} %target_hbm.1, f32[5,8,128]{2,1,0:T(8,128)S(1)} %edges.2.after.own.vector, bf16[8,16,512]{2,1,0:T(8,128)(2,1)S(1)} %get-tuple-element.23.coefficients, bf16[128,3,32,128]{3,2,1,0:T(8,128)(2,1)} %bitcast.12), custom_call_target="tpu_custom_call" | custom-call | flops 200000000 | bytes 10000000 | tf_op jit(solution)/shard_map/first_expand/pallas_call | solution.py:438
  17.0 0.0 collective-permute-done.3.swap_b
  17.0 0.0 collective-permute-done.2.swap_a
  17.0 6.7 %all-to-all-start = ((f32[128,4,128]{2,1,0:T(4,128)}), f32[128,4,128]{2,1,0:T(4,128)S(1)}, u32[]{:S(2)}, u32[]{:S(2)}) async-start(f32[128,4,128]{2,1,0:T(4,128)} %first_expand.1), calls=%async_computation | async-start | bytes 524288 | tf_op jit(solution)/shard_map/all_to_all | solution.py:369
  23.6 0.0 copy-done
  23.7 0.0 copy-done.1
  23.7 7.0 %local_part.2 = (f32[4,8,128]{2,1,0:T(8,128)S(1)}, f32[4,8,128]{2,1,0:T(8,128)S(1)}) custom-call(s32[48]{0:T(128)S(1)} %copy-done.1, f32[4,8,128]{2,1,0:T(8,128)S(1)} %copy-done, f32[5,8,128]{2,1,0:T(8,128)S(1)} %edges.2.after.own.vector, f32[5,8,128]{2,1,0:T(8,128)S(1)} %collective-permute-done.2.swap_a, f32[5,8,128]{2,1,0:T(8,128)S(1)} %collective-permute-done.3.swap_b, ...), custom_call_target="tpu_custom_call" | custom-call | flops 400000000 | bytes 20000000 | tf_op jit(solution)/shard_map/local_part/pallas_call | solution.py:447
  30.6 4.2 %all-to-all-done.received.target = f32[128,4,128]{2,1,0:T(4,128)S(1)} async-done(((f32[128,4,128]{2,1,0:T(4,128)}), f32[128,4,128]{2,1,0:T(4,128)S(1)}, u32[]{:S(2)}, u32[]{:S(2)}) %all-to-all-start) | async-done | bytes 262176 | tf_op jit(solution)/shard_map/all_to_all | solution.py:369
  34.9 0.5 first_image.1
  35.4 0.9 %collective-permute-start.5 = (f32[4,8,128]{2,1,0:T(8,128)S(1)}, f32[4,8,128]{2,1,0:T(8,128)S(1)}, u32[]{:S(2)}, u32[]{:S(2)}) collective-permute-start(f32[4,8,128]{2,1,0:T(8,128)S(1)} %get-tuple-element.28.vector_in.image), channel_id=1, source_target_pairs={{0,112},{16,32},{32,16},{48,64},{64,48},{80,96},{96,80},{112,0},{1... | collective-permute-start | bytes 49160 | tf_op jit(solution)/shard_map/ppermute | solution.py:375
  36.3 0.4 collective-permute-start.4
  36.7 2.6 %project.3 = (bf16[8,48,512]{2,1,0:T(8,128)(2,1)S(1)}, f32[4,8,128]{2,1,0:T(8,128)S(1)}) custom-call(s32[1,128]{1,0:T(1,128)} %source_hbm.3, f32[4,8,128]{2,1,0:T(8,128)S(1)} %get-tuple-element.28.vector_in.image, bf16[128,3,32,128]{3,2,1,0:T(8,128)(2,1)} %bitcast.15), custom_call_target="tpu_custom_call" | custom-call | flops 200000000 | bytes 10000000 | tf_op jit(solution)/shard_map/project/pallas_call | solution.py:393
  39.3 0.0 collective-permute-done.5.swap_b
  39.3 0.0 collective-permute-done.4.swap_a
  39.4 2.9 %collective-permute-start.7 = (f32[5,8,128]{2,1,0:T(8,128)S(1)}, f32[5,8,128]{2,1,0:T(8,128)S(1)}, u32[]{:S(2)}, u32[]{:S(2)}) collective-permute-start(f32[5,8,128]{2,1,0:T(8,128)S(1)} %edges.3.after.own), channel_id=1, source_target_pairs={{0,15},{1,2},{2,1},{3,4},{4,3},{5,6},{6,5},{7,8},{8,7},{9,10},{10,... | collective-permute-start | bytes 61448 | tf_op jit(solution)/shard_map/ppermute | solution.py:375
  42.3 0.0 collective-permute-start.6
  42.3 2.9 %second_expand.1 = f32[128,4,128]{2,1,0:T(4,128)} custom-call(f32[1,128]{1,0:T(1,128)S(1)} %get-tuple-element.31.row, f32[5,8,128]{2,1,0:T(8,128)S(1)} %edges.3.after.own, bf16[8,48,512]{2,1,0:T(8,128)(2,1)S(1)} %get-tuple-element.32.coefficients, bf16[128,3,32,128]{3,2,1,0:T(8,128)(2,1)} %bitcast.13), custom_call_target="tpu_custom_call" | custom-call | flops 200000000 | bytes 10000000 | tf_op jit(solution)/shard_map/second_expand/pallas_call | solution.py:458
  45.2 0.2 collective-permute-done.7.swap_b
  45.4 0.0 collective-permute-done.6.swap_a
  45.4 6.8 %all-to-all-start.1 = ((f32[128,4,128]{2,1,0:T(4,128)}), f32[128,4,128]{2,1,0:T(4,128)S(1)}, u32[]{:S(2)}, u32[]{:S(2)}) async-start(f32[128,4,128]{2,1,0:T(4,128)} %second_expand.1), calls=%async_computation.1 | async-start | bytes 524288 | tf_op jit(solution)/shard_map/all_to_all | solution.py:369
  52.2 7.6 %local_part.3 = (f32[4,8,128]{2,1,0:T(8,128)}, f32[4,8,128]{2,1,0:T(8,128)S(1)}) custom-call(s32[48]{0:T(128)S(1)} %copy-done.1, f32[4,8,128]{2,1,0:T(8,128)S(1)} %copy-done, f32[5,8,128]{2,1,0:T(8,128)S(1)} %edges.3.after.own, f32[5,8,128]{2,1,0:T(8,128)S(1)} %collective-permute-done.6.swap_a, f32[5,8,128]{2,1,0:T(8,128)S(1)} %collective-permute-done.7.swap_b, ...), custom_call_target="tpu_custom_call" | custom-call | flops 400000000 | bytes 20000000 | tf_op jit(solution)/shard_map/local_part/pallas_call | solution.py:464
  59.8 3.7 %all-to-all-done.1.received = f32[128,4,128]{2,1,0:T(4,128)S(1)} async-done(((f32[128,4,128]{2,1,0:T(4,128)}), f32[128,4,128]{2,1,0:T(4,128)S(1)}, u32[]{:S(2)}, u32[]{:S(2)}) %all-to-all-start.1) | async-done | bytes 262176 | tf_op jit(solution)/shard_map/all_to_all | solution.py:369
  63.5 1.3 %second_image.1 = (f32[4,8,128]{2,1,0:T(8,128)S(1)}, f32[4,8,128]{2,1,0:T(8,128)S(1)}, f32[1,128]{1,0:T(1,128)S(1)}, f32[128,128]{1,0:T(8,128)S(1)}) custom-call(f32[5,8,128]{2,1,0:T(8,128)S(1)} %edges.2.after.own.vector, f32[4,8,128]{2,1,0:T(8,128)S(1)} %get-tuple-element.28.vector_in.image, f32[4,8,128]{2,1,0:T(8,128)S(1)} %get-tuple-element.29.local_one, ...), custom_call_target="tpu_custom_call" | custom-call | tf_op jit(solution)/shard_map/second_image/pallas_call | solution.py:465
  64.7 15.5 %all_to_all.21 = f32[128,1,128]{2,1,0:T(1,128)S(1)} all-to-all(f32[128,1,128]{2,1,0:T(1,128)S(1)} %bitcast.11), channel_id=1, replica_groups=mesh['strip'=8,'blk'=16] {'strip','blk'}, dimensions={0} | all-to-all | bytes 131072 | tf_op jit(solution)/shard_map/all_to_all | solution.py:369
  80.2 1.4 %finish.1 = (f32[2,4,8,128]{3,2,1,0:T(8,128)}, f32[5]{0:T(128)}) custom-call(f32[5,8,128]{2,1,0:T(8,128)S(1)} %edges.2.after.own.vector, f32[4,8,128]{2,1,0:T(8,128)S(1)} %get-tuple-element.38.first, f32[4,8,128]{2,1,0:T(8,128)S(1)} %get-tuple-element.39.image, f32[1,128]{1,0:T(1,128)S(1)} %get-tuple-element.40.scalars, f32[128,128]{1,0:T(8,128)S(1)} %bitcast.10), custom_call_target="tpu_custom_call" | custom-call | tf_op jit(solution)/shard_map/finish/pallas_call | solution.py:474
  (4 shorter events, 0.0 us)
Async XLA Ops:
  0.6 6.8 %collective-permute-start.1 = (f32[4,8,128]{2,1,0:T(8,128)}, f32[4,8,128]{2,1,0:T(8,128)S(1)}, u32[]{:S(2)}, u32[]{:S(2)}) collective-permute-start(f32[4,8,128]{2,1,0:T(8,128)} %vector_in.1), channel_id=1, source_target_pairs={{0,112},{16,32},{32,16},{48,64},{64,48},{80,96},{96,80},{112,0},{1... | collective-permute-start | bytes 49160 | tf_op jit(solution)/shard_map/ppermute | solution.py:375
  3.3 4.2 %collective-permute-start = (f32[4,8,128]{2,1,0:T(8,128)}, f32[4,8,128]{2,1,0:T(8,128)S(1)}, u32[]{:S(2)}, u32[]{:S(2)}) collective-permute-start(f32[4,8,128]{2,1,0:T(8,128)} %vector_in.1), channel_id=1, source_target_pairs={{0,16},{16,0},{32,48},{48,32},{64,80},{80,64},{96,112},{112,96},{1... | collective-permute-start | bytes 49160 | tf_op jit(solution)/shard_map/ppermute | solution.py:375
  4.4 19.2 %copy-start = (f32[4,8,128]{2,1,0:T(8,128)S(1)}, f32[4,8,128]{2,1,0:T(8,128)}, u32[]{:S(2)}) copy-start(f32[4,8,128]{2,1,0:T(8,128)} %conductivity.3) | copy-start | bytes 49156
  4.4 19.2 %copy-start.1 = (s32[48]{0:T(128)S(1)}, s32[48]{0:T(128)}, u32[]{:S(2)}) copy-start(s32[48]{0:T(128)} %near_pair.3) | copy-start | bytes 580
  7.5 9.4 %collective-permute-start.3 = (f32[5,8,128]{2,1,0:T(8,128)S(1)}, f32[5,8,128]{2,1,0:T(8,128)S(1)}, u32[]{:S(2)}, u32[]{:S(2)}) collective-permute-start(f32[5,8,128]{2,1,0:T(8,128)S(1)} %edges.2.after.own.vector), channel_id=1, source_target_pairs={{0,15},{1,2},{2,1},{3,4},{4,3},{5,6},{6,5},{7,8},{8,7},{9,10},{10,... | collective-permute-start | bytes 61448 | tf_op jit(solution)/shard_map/ppermute | solution.py:375
  13.8 3.2 %collective-permute-start.2 = (f32[5,8,128]{2,1,0:T(8,128)S(1)}, f32[5,8,128]{2,1,0:T(8,128)S(1)}, u32[]{:S(2)}, u32[]{:S(2)}) collective-permute-start(f32[5,8,128]{2,1,0:T(8,128)S(1)} %edges.2.after.own.vector), channel_id=1, source_target_pairs={{0,1},{1,0},{2,3},{3,2},{4,5},{5,4},{6,7},{7,6},{8,9},{9,8},{10,11... | collective-permute-start | bytes 61448 | tf_op jit(solution)/shard_map/ppermute | solution.py:375
  17.0 17.9 %all-to-all-start = ((f32[128,4,128]{2,1,0:T(4,128)}), f32[128,4,128]{2,1,0:T(4,128)S(1)}, u32[]{:S(2)}, u32[]{:S(2)}) async-start(f32[128,4,128]{2,1,0:T(4,128)} %first_expand.1), calls=%async_computation | async-start | bytes 524288 | tf_op jit(solution)/shard_map/all_to_all | solution.py:369
  35.4 4.0 %collective-permute-start.5 = (f32[4,8,128]{2,1,0:T(8,128)S(1)}, f32[4,8,128]{2,1,0:T(8,128)S(1)}, u32[]{:S(2)}, u32[]{:S(2)}) collective-permute-start(f32[4,8,128]{2,1,0:T(8,128)S(1)} %get-tuple-element.28.vector_in.image), channel_id=1, source_target_pairs={{0,112},{16,32},{32,16},{48,64},{64,48},{80,96},{96,80},{112,0},{1... | collective-permute-start | bytes 49160 | tf_op jit(solution)/shard_map/ppermute | solution.py:375
  36.3 3.0 %collective-permute-start.4 = (f32[4,8,128]{2,1,0:T(8,128)S(1)}, f32[4,8,128]{2,1,0:T(8,128)S(1)}, u32[]{:S(2)}, u32[]{:S(2)}) collective-permute-start(f32[4,8,128]{2,1,0:T(8,128)S(1)} %get-tuple-element.28.vector_in.image), channel_id=1, source_target_pairs={{0,16},{16,0},{32,48},{48,32},{64,80},{80,64},{96,112},{112,96},{1... | collective-permute-start | bytes 49160 | tf_op jit(solution)/shard_map/ppermute | solution.py:375
  39.4 6.0 %collective-permute-start.7 = (f32[5,8,128]{2,1,0:T(8,128)S(1)}, f32[5,8,128]{2,1,0:T(8,128)S(1)}, u32[]{:S(2)}, u32[]{:S(2)}) collective-permute-start(f32[5,8,128]{2,1,0:T(8,128)S(1)} %edges.3.after.own), channel_id=1, source_target_pairs={{0,15},{1,2},{2,1},{3,4},{4,3},{5,6},{6,5},{7,8},{8,7},{9,10},{10,... | collective-permute-start | bytes 61448 | tf_op jit(solution)/shard_map/ppermute | solution.py:375
  42.3 3.1 %collective-permute-start.6 = (f32[5,8,128]{2,1,0:T(8,128)S(1)}, f32[5,8,128]{2,1,0:T(8,128)S(1)}, u32[]{:S(2)}, u32[]{:S(2)}) collective-permute-start(f32[5,8,128]{2,1,0:T(8,128)S(1)} %edges.3.after.own), channel_id=1, source_target_pairs={{0,1},{1,0},{2,3},{3,2},{4,5},{5,4},{6,7},{7,6},{8,9},{9,8},{10,11... | collective-permute-start | bytes 61448 | tf_op jit(solution)/shard_map/ppermute | solution.py:375
  45.4 18.1 %all-to-all-start.1 = ((f32[128,4,128]{2,1,0:T(4,128)}), f32[128,4,128]{2,1,0:T(4,128)S(1)}, u32[]{:S(2)}, u32[]{:S(2)}) async-start(f32[128,4,128]{2,1,0:T(4,128)} %second_expand.1), calls=%async_computation.1 | async-start | bytes 524288 | tf_op jit(solution)/shard_map/all_to_all | solution.py:369

commit v4 on v3

--- a/solution.py
+++ b/solution.py
@@ -108,11 +108,11 @@
     return strip, blk
 
 
-def near(around, near_pair, kernel_hbm, kernels, sems):
+def near(around, near_pair, kernels, wait):
     sub = lax.broadcasted_iota(jnp.int32, (8, LEN), 0)
 
     def chunk(n, total):
-        near_copy(kernel_hbm, kernels, sems, n).wait()
+        wait(n)
         rows, matrices = [], []
         for i in range(NEAR_CHUNK):
             p = n * NEAR_CHUNK + i
@@ -162,26 +162,18 @@
     return x[0:FAR_CHUNK] + (x[FAR_CHUNK : 2 * FAR_CHUNK] + x[2 * FAR_CHUNK :])
 
 
-def project(parts, source_hbm, vector_in, right_hbm, coefficients, vector, right, sems, gathered, rows, row_sem, vector_sem):
-    copy = pltpu.make_async_copy(source_hbm, rows, row_sem)
-    vector_copy = pltpu.make_async_copy(vector_in, vector, vector_sem)
-    copy.start()
-    vector_copy.start()
-    for n in range(FAR_COPIES):
-        far_copy(right_hbm, right, sems, n).start()
-    vector_copy.wait()
+def project(parts, source_row, vector, coefficients, right, gathered, copies):
     pieces = [[x.astype(BF16)] if parts == 1 else split3(x) for x in (vector[b] for b in range(3))]
     below = jnp.zeros((LEN - ROWS, LEN), F32)
     sources = [jnp.concatenate([pieces[b][k].astype(F32), below], axis=0).astype(BF16) for k in range(parts) for b in range(3)]
     sources = jnp.concatenate(sources, axis=1)
     row = lax.broadcasted_iota(jnp.int32, (LEN, LEN), 0)
-    copy.wait()
-    from_row = jnp.where(row == rows[...], 1.0, 0.0).T.astype(BF16)
+    from_row = jnp.where(row == source_row, 1.0, 0.0).T.astype(BF16)
     gathered[...] = lax.dot_general(from_row, sources, PLAIN, preferred_element_type=F32).astype(BF16)
     own = own_block()
     for n in range(FAR_CHUNKS):
-        if n % FAR_PER_COPY == 0:
-            far_copy(right_hbm, right, sems, n // FAR_PER_COPY).wait()
+        if copies and n % FAR_PER_COPY == 0:
+            copies[n // FAR_PER_COPY].wait()
         d = pl.ds(n * FAR_CHUNK, FAR_CHUNK)
         source = jnp.concatenate([gathered[d, 3 * LEN * k : 3 * LEN * (k + 1)] for k in range(parts)], axis=0)
         matrix = jnp.concatenate([right[d, b].reshape(FAR_CHUNK * RANK, LEN) for b in range(3)], axis=1)
@@ -190,15 +182,19 @@
         coefficients[n] = c.astype(BF16) if parts == 1 else jnp.concatenate(split3(c), axis=0)
 
 
-def expand(parts, coefficients, left_hbm, payload, left, sems):
+def expand(parts, coefficients, left, out, payload, sems):
+    copies = []
     for n in range(FAR_CHUNKS):
-        if n % FAR_PER_COPY == 0:
-            far_copy(left_hbm, left, sems, n // FAR_PER_COPY).wait()
         d = pl.ds(n * FAR_CHUNK, FAR_CHUNK)
         matrix = jnp.concatenate([left[d, a].reshape(FAR_CHUNK * RANK, LEN) for a in range(3)], axis=1)
         result = summed(lax.dot_general(coefficients[n], matrix, PLAIN, preferred_element_type=F32), parts)
         for a in range(3):
             payload[d, a, :] = result[:, a * LEN : (a + 1) * LEN]
+        if n % FAR_PER_COPY == FAR_PER_COPY - 1:
+            copies.append(far_copy(payload, out, sems, n // FAR_PER_COPY))
+            copies[-1].start()
+    for copy in copies:
+        copy.wait()
 
 
 def far_sum(received, target):
@@ -233,40 +229,46 @@
     return out + [vector[3] + vector[0] - local[3]]
 
 
-def far_scratch():
-    return [pltpu.VMEM((DEVICES, 3, RANK, LEN), BF16), pltpu.SemaphoreType.DMA((FAR_COPIES,))]
-
-
-def near_scratch():
-    return [
-        pltpu.VMEM((PAIRS, 3, 3, LEN, LEN), BF16),
-        pltpu.SemaphoreType.DMA((NEAR_CHUNKS,)),
-    ]
-
-
 def start_near(kernel_hbm, kernels, sems):
     for n in range(NEAR_CHUNKS):
         near_copy(kernel_hbm, kernels, sems, n).start()
 
 
-def first_expand(target_hbm, after, coefficients, left_hbm, payload, left, sems, rows, row_sem):
-    copy = pltpu.make_async_copy(target_hbm, rows, row_sem)
-    copy.start()
-    for n in range(FAR_COPIES):
-        far_copy(left_hbm, left, sems, n).start()
-    copy.wait()
-    payload[:, 3, :] = jnp.broadcast_to(rows[...].astype(F32), (DEVICES, LEN)).T
-    expand(1, coefficients, left_hbm, payload, left, sems)
-
-
-def second_expand(row, after, coefficients, left_hbm, payload, left, sems):
-    for n in range(FAR_COPIES):
-        far_copy(left_hbm, left, sems, n).start()
+def bring(
+    source_hbm, target_hbm, vector_hbm, right_hbm, left_hbm, vector, source_row, target_row, right, left, sems
+):
+    pairs = (
+        (source_hbm, source_row), (vector_hbm, vector), (target_hbm, target_row), (right_hbm, right), (left_hbm, left),
+    )
+    copies = [pltpu.make_async_copy(x, y, sems.at[i]) for i, (x, y) in enumerate(pairs)]
+    for copy in copies:
+        copy.start()
+    for copy in copies:
+        copy.wait()
+
+
+def first_project(source_row, vector, right, coefficients, gathered):
+    project(1, source_row[...], vector, coefficients, right, gathered, None)
+
+
+def second_project(source_row, vector, right_hbm, coefficients, right, gathered, right_sems):
+    rights = [far_copy(right_hbm, right, right_sems, n) for n in range(FAR_COPIES)]
+    for copy in rights:
+        copy.start()
+    project(3, source_row[...], vector, coefficients, right, gathered, rights)
+
+
+def first_expand(target_row, after, coefficients, left, out, payload, sems):
+    payload[:, 3, :] = jnp.broadcast_to(target_row[...].astype(F32), (DEVICES, LEN)).T
+    expand(1, coefficients, left, out, payload, sems)
+
+
+def second_expand(row, after, coefficients, left, out, payload, sems):
     payload[:, 3, :] = jnp.broadcast_to(row[...], (DEVICES, LEN))
-    expand(3, coefficients, left_hbm, payload, left, sems)
-
-
-def edges(vector, swap_a, swap_b, out):
+    expand(3, coefficients, left, out, payload, sems)
+
+
+def edges(vector, swap_a, swap_b, after, out):
     strip, _ = place()
     even = lax.rem(strip, 2) == 0
     above = jnp.where(even, swap_b[:, ROWS - 1, :], swap_a[:, ROWS - 1, :])
@@ -290,7 +292,7 @@
     flux_sum = flux(around, conductivity)
     rounded[3] = flux_sum
     full[3] = flux_sum
-    near_rounded, near_full = near(around, near_pair, kernel_hbm, kernels, sems)
+    near_rounded, near_full = near(around, near_pair, kernels, lambda n: near_copy(kernel_hbm, kernels, sems, n).wait())
     for a in range(3):
         rounded[a] = near_rounded[:, a * LEN : (a + 1) * LEN]
         full[a] = near_full[:, a * LEN : (a + 1) * LEN]
@@ -375,35 +377,15 @@
     return lax.ppermute(x, axis, even), lax.ppermute(x, axis, odd)
 
 
-def own_blocks(parts, source_row, vector, right):
-    swap_a, swap_b = swaps(vector, "strip", STRIPS)
-    coefficients, vector = projected(parts, source_row, in_hbm(vector) if parts == 1 else vector, right)
-    own = pl.pallas_call(
+def own_blocks(in_vmem, swap_a, swap_b, after):
+    return pl.pallas_call(
         edges,
         out_shape=shape(5, ROWS, LEN),
-        in_specs=[VMEM] * 3,
+        in_specs=[VMEM] * 3 + [ANY],
         out_specs=VMEM,
         compiler_params=limit(4),
         name="edges",
-    )(vector, swap_a, swap_b)
-    return own, coefficients
-
-
-def projected(parts, source_row, vector, right):
-    return pl.pallas_call(
-        functools.partial(project, parts),
-        out_shape=(
-            jax.ShapeDtypeStruct((FAR_CHUNKS, parts * FAR_CHUNK, FAR_CHUNK * RANK), BF16),
-            shape(4, ROWS, LEN),
-        ),
-        in_specs=[HBM, HBM if parts == 1 else ANY, HBM],
-        out_specs=(VMEM, VMEM),
-        scratch_shapes=far_scratch()
-        + [pltpu.VMEM((DEVICES, parts * 3 * LEN), BF16), pltpu.VMEM((1, LEN), jnp.int32), pltpu.SemaphoreType.DMA, pltpu.SemaphoreType.DMA],
-        compiler_params=limit(12),
-        cost_estimate=pl.CostEstimate(flops=2 * 10**8, bytes_accessed=10**7, transcendentals=0),
-        name="project",
-    )(source_row, vector, right)
+    )(in_vmem, swap_a, swap_b, after)
 
 
 def local(vector, conductivity, near_kernel, near_pair, far_right, far_left, far_source_row, far_target_row):
@@ -413,38 +395,69 @@
     source_row, target_row = in_hbm(far_source_row), in_hbm(far_target_row)
     block, slots, line = shape(4, ROWS, LEN), shape(DEVICES, 4, LEN), shape(1, LEN)
 
+    factors = jax.ShapeDtypeStruct((DEVICES, 3, RANK, LEN), BF16)
+    far_buffer = pltpu.VMEM((DEVICES, 3, RANK, LEN), BF16)
+    integers = jax.ShapeDtypeStruct((1, LEN), jnp.int32)
+    cost = pl.CostEstimate(flops=2 * 10**8, bytes_accessed=10**7, transcendentals=0)
+
+    def gathered_and_coefficients(parts):
+        gathered = pltpu.VMEM((DEVICES, parts * 3 * LEN), BF16)
+        return gathered, jax.ShapeDtypeStruct((FAR_CHUNKS, parts * FAR_CHUNK, FAR_CHUNK * RANK), BF16)
+
+    expand_call = functools.partial(
+        pl.pallas_call,
+        out_shape=pltpu.HBM(slots.shape, F32),
+        in_specs=[VMEM, ANY, VMEM, VMEM],
+        out_specs=HBM,
+        scratch_shapes=[pltpu.VMEM(slots.shape, F32), pltpu.SemaphoreType.DMA((FAR_COPIES,))],
+        compiler_params=limit(4),
+        cost_estimate=cost,
+    )
+
     local_call = functools.partial(
         pl.pallas_call,
         local_part,
         out_shape=(block, block),
         in_specs=[SMEM, VMEM, VMEM, VMEM, VMEM, HBM],
         out_specs=(VMEM, VMEM),
-        scratch_shapes=[pltpu.VMEM((4, HALO, LEN), F32)] + near_scratch(),
+        scratch_shapes=[
+            pltpu.VMEM((4, HALO, LEN), F32),
+            pltpu.VMEM((PAIRS, 3, 3, LEN, LEN), BF16),
+            pltpu.SemaphoreType.DMA((NEAR_CHUNKS,)),
+        ],
         compiler_params=limit(20),
         cost_estimate=pl.CostEstimate(flops=4 * 10**8, bytes_accessed=2 * 10**7, transcendentals=0),
         name="local_part",
     )
 
-    expand_call = functools.partial(
-        pl.pallas_call,
-        out_shape=slots,
+    swapped = swaps(vector, "strip", STRIPS)
+    vector_vmem, source_row, target_row, right_vmem, left = pl.pallas_call(
+        bring,
+        out_shape=(block, integers, integers, factors, factors),
+        in_specs=[HBM] * 5,
+        out_specs=(VMEM,) * 5,
+        scratch_shapes=[pltpu.SemaphoreType.DMA((5,))],
+        compiler_params=limit(4),
+        cost_estimate=cost,
+        name="bring",
+    )(source_row, target_row, in_hbm(vector), right, left)
+    start = own_blocks(vector_vmem, *swapped, source_row)
+    sides = swaps(start, "blk", BLKS)
+    gathered, coefficients = gathered_and_coefficients(1)
+    coefficients = pl.pallas_call(
+        first_project,
+        out_shape=coefficients,
+        in_specs=[VMEM] * 3,
         out_specs=VMEM,
-        compiler_params=limit(12),
-        cost_estimate=pl.CostEstimate(flops=2 * 10**8, bytes_accessed=10**7, transcendentals=0),
-    )
-
-    start, coefficients = own_blocks(1, source_row, vector, right)
-    blocks = swaps(start, "blk", BLKS)
-    payload = expand_call(
-        first_expand,
-        in_specs=[HBM, ANY, VMEM, HBM],
-        scratch_shapes=far_scratch() + [pltpu.VMEM((1, LEN), jnp.int32), pltpu.SemaphoreType.DMA],
-        name="first_expand",
-    )(target_row, start, coefficients, left)
-    payload, *blocks = lax.optimization_barrier((payload, *blocks))
-    blocks = (start, *blocks)
+        scratch_shapes=[gathered],
+        compiler_params=limit(4),
+        cost_estimate=cost,
+        name="first_project",
+    )(source_row, start, right_vmem)
+    payload = expand_call(first_expand, name="first_expand")(target_row, start, coefficients, left)
+    payload, *sides = lax.optimization_barrier((payload, *sides))
     received_one = exchange(payload)
-    rounded_one, local_one = local_call()(near_pair, conductivity, *blocks, near_kernel)
+    rounded_one, local_one = local_call()(near_pair, conductivity, start, *sides, near_kernel)
     image, far_one, row = pl.pallas_call(
         first_image,
         out_shape=(block, shape(3, ROWS, LEN), line),
@@ -453,15 +466,24 @@
         compiler_params=limit(4),
         name="first_image",
     )(start, rounded_one, received_one)
-    own, coefficients = own_blocks(3, source_row, image, right)
-    blocks = swaps(own, "blk", BLKS)
-    payload = expand_call(
-        second_expand, in_specs=[VMEM, ANY, VMEM, HBM], scratch_shapes=far_scratch(), name="second_expand"
-    )(row, own, coefficients, left)
-    payload, *blocks = lax.optimization_barrier((payload, *blocks))
-    blocks = (own, *blocks)
+    swapped = swaps(image, "strip", STRIPS)
+    own = own_blocks(image, *swapped, row)
+    sides = swaps(own, "blk", BLKS)
+    gathered, coefficients = gathered_and_coefficients(3)
+    coefficients = pl.pallas_call(
+        second_project,
+        out_shape=coefficients,
+        in_specs=[VMEM, VMEM, HBM],
+        out_specs=VMEM,
+        scratch_shapes=[far_buffer, gathered, pltpu.SemaphoreType.DMA((FAR_COPIES,))],
+        compiler_params=limit(8),
+        cost_estimate=cost,
+        name="second_project",
+    )(source_row, own, right)
+    payload = expand_call(second_expand, name="second_expand")(row, own, coefficients, left)
+    payload, *sides = lax.optimization_barrier((payload, *sides))
     received_two = exchange(payload)
-    _, local_two = local_call()(near_pair, conductivity, *blocks, near_kernel)
+    _, local_two = local_call()(near_pair, conductivity, own, *sides, near_kernel)
     first, image_two, scalars, rows = pl.pallas_call(
         second_image,
         out_shape=(block, block, line, shape(DEVICES, LEN)),

time: 81.9 us -> 82.4 us (level)
  Pallas kernels: 29.5 us -> 26.9 us
  waiting for transfers between devices: 8.13 us -> 9.63 us
    pallas_call x8 -> x9, Pallas kernels: 26.3 us -> 23.7 us  [the longest x1 7.57 us: local(): local_call()(near_pair, conductivity, own, *sides, near_kernel)]
    ppermute x8, waiting for transfers between devices: 0.22 us -> 2.38 us  [swaps(): return (lax.ppermute(x, axis, even), lax.ppermute(x, axis, odd))]
    all_to_all x2, starting transfers between devices: 13.5 us -> 14.8 us  [exchange(): return lax.all_to_all(x, ('strip', 'blk'), 0, 0, tiled=True)]
    ppermute x8, starting transfers between devices: 14.3 us -> 13.3 us  [swaps(): return (lax.ppermute(x, axis, even), lax.ppermute(x, axis, odd))]
  transfers between devices with their start and end apart: 10 -> 10, of which waited for: 3 -> 5; matrix products, arithmetic and copies ran while one was open for 0% -> 0% of each run, Pallas kernels for 32% -> 29%
where the time goes in v4:
time: 82.4 us; the launch traced here: 82.2 us
  starting transfers between devices  28.1 us (34%)
  Pallas kernels  26.9 us (33%)
  blocking collectives  16.1 us (20%)
  waiting for transfers between devices  9.63 us (12%)
    all_to_all x1, blocking collectives, exchange(): return lax.all_to_all(x, ('strip', 'blk'), 0, 0, tiled=True)  16.1 us
    all_to_all x2, starting transfers between devices, exchange(): return lax.all_to_all(x, ('strip', 'blk'), 0, 0, tiled=True)  14.8 us
    ppermute x8, starting transfers between devices, swaps(): return (lax.ppermute(x, axis, even), lax.ppermute(x, axis, odd))  13.3 us
    pallas_call x1, Pallas kernels, local(): local_call()(near_pair, conductivity, own, *sides, near_kernel)  7.57 us
    all_to_all x2, waiting for transfers between devices, exchange(): return lax.all_to_all(x, ('strip', 'blk'), 0, 0, tiled=True)  7.25 us
    pallas_call x1, Pallas kernels, local(): local_call()(near_pair, conductivity, start, *sides, near_kernel)  6.97 us
    pallas_call x1, Pallas kernels, local(): pl.pallas_call(bring, out_shape=(block, integers, integers, factors, fact...  2.93 us
    pallas_call x1, Pallas kernels, local(): pl.pallas_call(second_project, out_shape=coefficients, in_specs=[VMEM, VM...  2.6 us
  transfers between devices with their start and end apart: 10, of which 5 were waited for; matrix products, arithmetic and copies ran while one was open for 0% of the time, Pallas kernels for 29%

profile of v4, /device:TPU:1, one launch (start us, length us, event | category | flops | bytes accessed | tf_op | source)
XLA Modules:
  0.0 82.2 jit_solution(3423406028803817869)
XLA Ops:
  0.6 2.7 %collective-permute-start.1 = (f32[4,8,128]{2,1,0:T(8,128)}, f32[4,8,128]{2,1,0:T(8,128)S(1)}, u32[]{:S(2)}, u32[]{:S(2)}) collective-permute-start(f32[4,8,128]{2,1,0:T(8,128)} %vector_hbm.1), channel_id=1, source_target_pairs={{0,112},{16,32},{32,16},{48,64},{64,48},{80,96},{96,80},{112,0},{1... | collective-permute-start | bytes 49160 | tf_op jit(solution)/shard_map/ppermute | solution.py:377
  3.3 1.1 %collective-permute-start = (f32[4,8,128]{2,1,0:T(8,128)}, f32[4,8,128]{2,1,0:T(8,128)S(1)}, u32[]{:S(2)}, u32[]{:S(2)}) collective-permute-start(f32[4,8,128]{2,1,0:T(8,128)} %vector_hbm.1), channel_id=1, source_target_pairs={{0,16},{16,0},{32,48},{48,32},{64,80},{80,64},{96,112},{112,96},{1... | collective-permute-start | bytes 49160 | tf_op jit(solution)/shard_map/ppermute | solution.py:377
  4.4 2.9 %bring.1 = (f32[4,8,128]{2,1,0:T(8,128)S(1)}, s32[1,128]{1,0:T(1,128)S(1)}, s32[1,128]{1,0:T(1,128)S(1)}, bf16[128,3,32,128]{3,2,1,0:T(8,128)(2,1)S(1)}, bf16[128,3,32,128]{3,2,1,0:T(8,128)(2,1)S(1)}) custom-call(s32[1,128]{1,0:T(1,128)} %source_hbm.1, s32[1,128]{1,0:T(1,128)} %target_hbm.1, f32[4,8,128]{2,1,0:T(8,128)} %vector_hbm.1, ...), custom_call_target="tpu_custom_call" | custom-call | flops 200000000 | bytes 10000000 | tf_op jit(solution)/shard_map/bring/pallas_call | solution.py:434
  7.3 0.0 collective-permute-done.1.swap_b
  7.4 0.0 collective-permute-done.swap_a
  7.4 6.3 %collective-permute-start.3 = (f32[5,8,128]{2,1,0:T(8,128)S(1)}, f32[5,8,128]{2,1,0:T(8,128)S(1)}, u32[]{:S(2)}, u32[]{:S(2)}) collective-permute-start(f32[5,8,128]{2,1,0:T(8,128)S(1)} %edges.2.vector.after.own), channel_id=1, source_target_pairs={{0,15},{1,2},{2,1},{3,4},{4,3},{5,6},{6,5},{7,8},{8,7},{9,10},{10,... | collective-permute-start | bytes 61448 | tf_op jit(solution)/shard_map/ppermute | solution.py:377
  13.7 0.0 collective-permute-start.2
  13.7 1.0 %first_project.1.coefficients = bf16[8,16,512]{2,1,0:T(8,128)(2,1)S(1)} custom-call(s32[1,128]{1,0:T(1,128)S(1)} %get-tuple-element.24.after.source_row, f32[5,8,128]{2,1,0:T(8,128)S(1)} %edges.2.vector.after.own, bf16[128,3,32,128]{3,2,1,0:T(8,128)(2,1)S(1)} %get-tuple-element.26.right), custom_call_target="tpu_custom_call" | custom-call | flops 200000000 | bytes 10000000 | tf_op jit(solution)/shard_map/first_project/pallas_call | solution.py:447
  14.7 1.2 %first_expand.1 = f32[128,4,128]{2,1,0:T(4,128)} custom-call(s32[1,128]{1,0:T(1,128)S(1)} %get-tuple-element.25.target_row, f32[5,8,128]{2,1,0:T(8,128)S(1)} %edges.2.vector.after.own, bf16[8,16,512]{2,1,0:T(8,128)(2,1)S(1)} %first_project.1.coefficients, bf16[128,3,32,128]{3,2,1,0:T(8,128)(2,1)S(1)} %get-tuple-element.27.left), custom_call_target="tpu_custom_call" | custom-call | flops 200000000 | bytes 10000000 | tf_op jit(solution)/shard_map/first_expand/pallas_call | solution.py:457
  16.0 0.0 collective-permute-done.3.swap_b
  16.0 0.3 collective-permute-done.2.swap_a
  16.3 7.2 %all-to-all-start = ((f32[128,4,128]{2,1,0:T(4,128)}), f32[128,4,128]{2,1,0:T(4,128)S(1)}, u32[]{:S(2)}, u32[]{:S(2)}) async-start(f32[128,4,128]{2,1,0:T(4,128)} %first_expand.1), calls=%async_computation | async-start | bytes 524288 | tf_op jit(solution)/shard_map/all_to_all | solution.py:371
  23.5 7.0 %local_part.2 = (f32[4,8,128]{2,1,0:T(8,128)S(1)}, f32[4,8,128]{2,1,0:T(8,128)S(1)}) custom-call(s32[48]{0:T(128)S(1)} %copy-done.1, f32[4,8,128]{2,1,0:T(8,128)S(1)} %copy-done, f32[5,8,128]{2,1,0:T(8,128)S(1)} %edges.2.vector.after.own, f32[5,8,128]{2,1,0:T(8,128)S(1)} %collective-permute-done.2.swap_a, f32[5,8,128]{2,1,0:T(8,128)S(1)} %collective-permute-done.3.swap_b, ...), custom_call_target="tpu_custom_call" | custom-call | flops 400000000 | bytes 20000000 | tf_op jit(solution)/shard_map/local_part/pallas_call | solution.py:460
  30.5 4.2 %all-to-all-done.received.target = f32[128,4,128]{2,1,0:T(4,128)S(1)} async-done(((f32[128,4,128]{2,1,0:T(4,128)}), f32[128,4,128]{2,1,0:T(4,128)S(1)}, u32[]{:S(2)}, u32[]{:S(2)}) %all-to-all-start) | async-done | bytes 262176 | tf_op jit(solution)/shard_map/all_to_all | solution.py:371
  34.8 0.5 first_image.1
  35.2 0.9 %collective-permute-start.5 = (f32[4,8,128]{2,1,0:T(8,128)S(1)}, f32[4,8,128]{2,1,0:T(8,128)S(1)}, u32[]{:S(2)}, u32[]{:S(2)}) collective-permute-start(f32[4,8,128]{2,1,0:T(8,128)S(1)} %get-tuple-element.32.vector.image), channel_id=1, source_target_pairs={{0,112},{16,32},{32,16},{48,64},{64,48},{80,96},{96,80},{112,0},{1... | collective-permute-start | bytes 49160 | tf_op jit(solution)/shard_map/ppermute | solution.py:377
  36.2 0.4 collective-permute-start.4
  36.6 1.9 %collective-permute-done.5.swap_b = f32[4,8,128]{2,1,0:T(8,128)S(1)} collective-permute-done((f32[4,8,128]{2,1,0:T(8,128)S(1)}, f32[4,8,128]{2,1,0:T(8,128)S(1)}, u32[]{:S(2)}, u32[]{:S(2)}) %collective-permute-start.5) | collective-permute-done | bytes 16416 | tf_op jit(solution)/shard_map/ppermute | solution.py:377
  38.4 0.0 collective-permute-done.4.swap_a
  38.5 1.9 %collective-permute-start.7 = (f32[5,8,128]{2,1,0:T(8,128)S(1)}, f32[5,8,128]{2,1,0:T(8,128)S(1)}, u32[]{:S(2)}, u32[]{:S(2)}) collective-permute-start(f32[5,8,128]{2,1,0:T(8,128)S(1)} %edges.3.vector.after.own), channel_id=1, source_target_pairs={{0,15},{1,2},{2,1},{3,4},{4,3},{5,6},{6,5},{7,8},{8,7},{9,10},{10,... | collective-permute-start | bytes 61448 | tf_op jit(solution)/shard_map/ppermute | solution.py:377
  40.4 0.0 collective-permute-start.6
  40.4 2.6 %second_project.1.coefficients = bf16[8,48,512]{2,1,0:T(8,128)(2,1)S(1)} custom-call(s32[1,128]{1,0:T(1,128)S(1)} %get-tuple-element.24.after.source_row, f32[5,8,128]{2,1,0:T(8,128)S(1)} %edges.3.vector.after.own, bf16[128,3,32,128]{3,2,1,0:T(8,128)(2,1)} %bitcast.13), custom_call_target="tpu_custom_call" | custom-call | flops 200000000 | bytes 10000000 | tf_op jit(solution)/shard_map/second_project/pallas_call | solution.py:473
  43.0 1.3 %second_expand.1 = f32[128,4,128]{2,1,0:T(4,128)} custom-call(f32[1,128]{1,0:T(1,128)S(1)} %get-tuple-element.34.after.row, f32[5,8,128]{2,1,0:T(8,128)S(1)} %edges.3.vector.after.own, bf16[8,48,512]{2,1,0:T(8,128)(2,1)S(1)} %second_project.1.coefficients, bf16[128,3,32,128]{3,2,1,0:T(8,128)(2,1)S(1)} %get-tuple-element.27.left), custom_call_target="tpu_custom_call" | custom-call | flops 200000000 | bytes 10000000 | tf_op jit(solution)/shard_map/second_expand/pallas_call | solution.py:483
  44.3 0.2 collective-permute-done.7.swap_b
  44.5 7.6 %all-to-all-start.1 = ((f32[128,4,128]{2,1,0:T(4,128)}), f32[128,4,128]{2,1,0:T(4,128)S(1)}, u32[]{:S(2)}, u32[]{:S(2)}) async-start(f32[128,4,128]{2,1,0:T(4,128)} %second_expand.1), calls=%async_computation.1 | async-start | bytes 524288 | tf_op jit(solution)/shard_map/all_to_all | solution.py:371
  52.1 0.0 copy-start.2
  52.1 0.6 copy-done.2
  52.7 7.6 %local_part.3 = (f32[4,8,128]{2,1,0:T(8,128)}, f32[4,8,128]{2,1,0:T(8,128)S(1)}) custom-call(s32[48]{0:T(128)S(1)} %copy-done.2, f32[4,8,128]{2,1,0:T(8,128)S(1)} %copy-done, f32[5,8,128]{2,1,0:T(8,128)S(1)} %edges.3.vector.after.own, f32[5,8,128]{2,1,0:T(8,128)S(1)} %collective-permute-done.6.swap_a, f32[5,8,128]{2,1,0:T(8,128)S(1)} %collective-permute-done.7.swap_b, ...), custom_call_target="tpu_custom_call" | custom-call | flops 400000000 | bytes 20000000 | tf_op jit(solution)/shard_map/local_part/pallas_call | solution.py:486
  60.3 3.0 %all-to-all-done.1.received = f32[128,4,128]{2,1,0:T(4,128)S(1)} async-done(((f32[128,4,128]{2,1,0:T(4,128)}), f32[128,4,128]{2,1,0:T(4,128)S(1)}, u32[]{:S(2)}, u32[]{:S(2)}) %all-to-all-start.1) | async-done | bytes 262176 | tf_op jit(solution)/shard_map/all_to_all | solution.py:371
  63.3 1.3 %second_image.1 = (f32[4,8,128]{2,1,0:T(8,128)S(1)}, f32[4,8,128]{2,1,0:T(8,128)S(1)}, f32[1,128]{1,0:T(1,128)S(1)}, f32[128,128]{1,0:T(8,128)S(1)}) custom-call(f32[5,8,128]{2,1,0:T(8,128)S(1)} %edges.2.vector.after.own, f32[4,8,128]{2,1,0:T(8,128)S(1)} %get-tuple-element.32.vector.image, f32[4,8,128]{2,1,0:T(8,128)S(1)} %get-tuple-element.33.local_one, ...), custom_call_target="tpu_custom_call" | custom-call | tf_op jit(solution)/shard_map/second_image/pallas_call | solution.py:487
  64.6 16.1 %all_to_all.21 = f32[128,1,128]{2,1,0:T(1,128)S(1)} all-to-all(f32[128,1,128]{2,1,0:T(1,128)S(1)} %bitcast.11), channel_id=1, replica_groups=mesh['strip'=8,'blk'=16] {'strip','blk'}, dimensions={0} | all-to-all | bytes 131072 | tf_op jit(solution)/shard_map/all_to_all | solution.py:371
  80.7 1.4 %finish.1 = (f32[2,4,8,128]{3,2,1,0:T(8,128)}, f32[5]{0:T(128)}) custom-call(f32[5,8,128]{2,1,0:T(8,128)S(1)} %edges.2.vector.after.own, f32[4,8,128]{2,1,0:T(8,128)S(1)} %get-tuple-element.40.first, f32[4,8,128]{2,1,0:T(8,128)S(1)} %get-tuple-element.41.image, f32[1,128]{1,0:T(1,128)S(1)} %get-tuple-element.42.scalars, f32[128,128]{1,0:T(8,128)S(1)} %bitcast.10), custom_call_target="tpu_custom_call" | custom-call | tf_op jit(solution)/shard_map/finish/pallas_call | solution.py:496
  (7 shorter events, 0.1 us)
Async XLA Ops:
  0.6 6.7 %collective-permute-start.1 = (f32[4,8,128]{2,1,0:T(8,128)}, f32[4,8,128]{2,1,0:T(8,128)S(1)}, u32[]{:S(2)}, u32[]{:S(2)}) collective-permute-start(f32[4,8,128]{2,1,0:T(8,128)} %vector_hbm.1), channel_id=1, source_target_pairs={{0,112},{16,32},{32,16},{48,64},{64,48},{80,96},{96,80},{112,0},{1... | collective-permute-start | bytes 49160 | tf_op jit(solution)/shard_map/ppermute | solution.py:377
  3.3 4.0 %collective-permute-start = (f32[4,8,128]{2,1,0:T(8,128)}, f32[4,8,128]{2,1,0:T(8,128)S(1)}, u32[]{:S(2)}, u32[]{:S(2)}) collective-permute-start(f32[4,8,128]{2,1,0:T(8,128)} %vector_hbm.1), channel_id=1, source_target_pairs={{0,16},{16,0},{32,48},{48,32},{64,80},{80,64},{96,112},{112,96},{1... | collective-permute-start | bytes 49160 | tf_op jit(solution)/shard_map/ppermute | solution.py:377
  7.4 8.6 %collective-permute-start.3 = (f32[5,8,128]{2,1,0:T(8,128)S(1)}, f32[5,8,128]{2,1,0:T(8,128)S(1)}, u32[]{:S(2)}, u32[]{:S(2)}) collective-permute-start(f32[5,8,128]{2,1,0:T(8,128)S(1)} %edges.2.vector.after.own), channel_id=1, source_target_pairs={{0,15},{1,2},{2,1},{3,4},{4,3},{5,6},{6,5},{7,8},{8,7},{9,10},{10,... | collective-permute-start | bytes 61448 | tf_op jit(solution)/shard_map/ppermute | solution.py:377
  13.7 2.6 %collective-permute-start.2 = (f32[5,8,128]{2,1,0:T(8,128)S(1)}, f32[5,8,128]{2,1,0:T(8,128)S(1)}, u32[]{:S(2)}, u32[]{:S(2)}) collective-permute-start(f32[5,8,128]{2,1,0:T(8,128)S(1)} %edges.2.vector.after.own), channel_id=1, source_target_pairs={{0,1},{1,0},{2,3},{3,2},{4,5},{5,4},{6,7},{7,6},{8,9},{9,8},{10,11... | collective-permute-start | bytes 61448 | tf_op jit(solution)/shard_map/ppermute | solution.py:377
  13.7 9.8 %copy-start = (f32[4,8,128]{2,1,0:T(8,128)S(1)}, f32[4,8,128]{2,1,0:T(8,128)}, u32[]{:S(2)}) copy-start(f32[4,8,128]{2,1,0:T(8,128)} %conductivity.3) | copy-start | bytes 49156
  13.7 9.8 %copy-start.1 = (s32[48]{0:T(128)S(1)}, s32[48]{0:T(128)}, u32[]{:S(2)}) copy-start(s32[48]{0:T(128)} %near_pair.3) | copy-start | bytes 580
  16.3 18.4 %all-to-all-start = ((f32[128,4,128]{2,1,0:T(4,128)}), f32[128,4,128]{2,1,0:T(4,128)S(1)}, u32[]{:S(2)}, u32[]{:S(2)}) async-start(f32[128,4,128]{2,1,0:T(4,128)} %first_expand.1), calls=%async_computation | async-start | bytes 524288 | tf_op jit(solution)/shard_map/all_to_all | solution.py:371
  35.2 3.2 %collective-permute-start.5 = (f32[4,8,128]{2,1,0:T(8,128)S(1)}, f32[4,8,128]{2,1,0:T(8,128)S(1)}, u32[]{:S(2)}, u32[]{:S(2)}) collective-permute-start(f32[4,8,128]{2,1,0:T(8,128)S(1)} %get-tuple-element.32.vector.image), channel_id=1, source_target_pairs={{0,112},{16,32},{32,16},{48,64},{64,48},{80,96},{96,80},{112,0},{1... | collective-permute-start | bytes 49160 | tf_op jit(solution)/shard_map/ppermute | solution.py:377
  36.2 2.3 %collective-permute-start.4 = (f32[4,8,128]{2,1,0:T(8,128)S(1)}, f32[4,8,128]{2,1,0:T(8,128)S(1)}, u32[]{:S(2)}, u32[]{:S(2)}) collective-permute-start(f32[4,8,128]{2,1,0:T(8,128)S(1)} %get-tuple-element.32.vector.image), channel_id=1, source_target_pairs={{0,16},{16,0},{32,48},{48,32},{64,80},{80,64},{96,112},{112,96},{1... | collective-permute-start | bytes 49160 | tf_op jit(solution)/shard_map/ppermute | solution.py:377
  38.5 6.0 %collective-permute-start.7 = (f32[5,8,128]{2,1,0:T(8,128)S(1)}, f32[5,8,128]{2,1,0:T(8,128)S(1)}, u32[]{:S(2)}, u32[]{:S(2)}) collective-permute-start(f32[5,8,128]{2,1,0:T(8,128)S(1)} %edges.3.vector.after.own), channel_id=1, source_target_pairs={{0,15},{1,2},{2,1},{3,4},{4,3},{5,6},{6,5},{7,8},{8,7},{9,10},{10,... | collective-permute-start | bytes 61448 | tf_op jit(solution)/shard_map/ppermute | solution.py:377
  40.4 4.1 %collective-permute-start.6 = (f32[5,8,128]{2,1,0:T(8,128)S(1)}, f32[5,8,128]{2,1,0:T(8,128)S(1)}, u32[]{:S(2)}, u32[]{:S(2)}) collective-permute-start(f32[5,8,128]{2,1,0:T(8,128)S(1)} %edges.3.vector.after.own), channel_id=1, source_target_pairs={{0,1},{1,0},{2,3},{3,2},{4,5},{5,4},{6,7},{7,6},{8,9},{9,8},{10,11... | collective-permute-start | bytes 61448 | tf_op jit(solution)/shard_map/ppermute | solution.py:377
  44.5 18.8 %all-to-all-start.1 = ((f32[128,4,128]{2,1,0:T(4,128)}), f32[128,4,128]{2,1,0:T(4,128)S(1)}, u32[]{:S(2)}, u32[]{:S(2)}) async-start(f32[128,4,128]{2,1,0:T(4,128)} %second_expand.1), calls=%async_computation.1 | async-start | bytes 524288 | tf_op jit(solution)/shard_map/all_to_all | solution.py:371
  52.1 0.7 copy-start.2

commit v5 on v4

--- a/solution.py
+++ b/solution.py
@@ -162,7 +162,7 @@
     return x[0:FAR_CHUNK] + (x[FAR_CHUNK : 2 * FAR_CHUNK] + x[2 * FAR_CHUNK :])
 
 
-def project(parts, source_row, vector, coefficients, right, gathered, copies):
+def project(parts, source_row, vector, coefficients, right, gathered):
     pieces = [[x.astype(BF16)] if parts == 1 else split3(x) for x in (vector[b] for b in range(3))]
     below = jnp.zeros((LEN - ROWS, LEN), F32)
     sources = [jnp.concatenate([pieces[b][k].astype(F32), below], axis=0).astype(BF16) for k in range(parts) for b in range(3)]
@@ -172,8 +172,6 @@
     gathered[...] = lax.dot_general(from_row, sources, PLAIN, preferred_element_type=F32).astype(BF16)
     own = own_block()
     for n in range(FAR_CHUNKS):
-        if copies and n % FAR_PER_COPY == 0:
-            copies[n // FAR_PER_COPY].wait()
         d = pl.ds(n * FAR_CHUNK, FAR_CHUNK)
         source = jnp.concatenate([gathered[d, 3 * LEN * k : 3 * LEN * (k + 1)] for k in range(parts)], axis=0)
         matrix = jnp.concatenate([right[d, b].reshape(FAR_CHUNK * RANK, LEN) for b in range(3)], axis=1)
@@ -234,12 +232,8 @@
         near_copy(kernel_hbm, kernels, sems, n).start()
 
 
-def bring(
-    source_hbm, target_hbm, vector_hbm, right_hbm, left_hbm, vector, source_row, target_row, right, left, sems
-):
-    pairs = (
-        (source_hbm, source_row), (vector_hbm, vector), (target_hbm, target_row), (right_hbm, right), (left_hbm, left),
-    )
+def bring(source_hbm, target_hbm, vector_hbm, right_hbm, vector, source_row, target_row, right, sems):
+    pairs = ((source_hbm, source_row), (vector_hbm, vector), (target_hbm, target_row), (right_hbm, right))
     copies = [pltpu.make_async_copy(x, y, sems.at[i]) for i, (x, y) in enumerate(pairs)]
     for copy in copies:
         copy.start()
@@ -247,15 +241,21 @@
         copy.wait()
 
 
-def first_project(source_row, vector, right, coefficients, gathered):
-    project(1, source_row[...], vector, coefficients, right, gathered, None)
-
-
-def second_project(source_row, vector, right_hbm, coefficients, right, gathered, right_sems):
-    rights = [far_copy(right_hbm, right, right_sems, n) for n in range(FAR_COPIES)]
-    for copy in rights:
-        copy.start()
-    project(3, source_row[...], vector, coefficients, right, gathered, rights)
+def bring_right(after, right_hbm, right, sem):
+    copy = pltpu.make_async_copy(right_hbm, right, sem)
+    copy.start()
+    copy.wait()
+
+
+def first_project(source_row, vector, right, left_hbm, coefficients, left, gathered, sem):
+    copy = pltpu.make_async_copy(left_hbm, left, sem)
+    copy.start()
+    project(1, source_row[...], vector, coefficients, right, gathered)
+    copy.wait()
+
+
+def second_project(source_row, vector, right, coefficients, gathered):
+    project(3, source_row[...], vector, coefficients, right, gathered)
 
 
 def first_expand(target_row, after, coefficients, left, out, payload, sems):
@@ -396,7 +396,6 @@
     block, slots, line = shape(4, ROWS, LEN), shape(DEVICES, 4, LEN), shape(1, LEN)
 
     factors = jax.ShapeDtypeStruct((DEVICES, 3, RANK, LEN), BF16)
-    far_buffer = pltpu.VMEM((DEVICES, 3, RANK, LEN), BF16)
     integers = jax.ShapeDtypeStruct((1, LEN), jnp.int32)
     cost = pl.CostEstimate(flops=2 * 10**8, bytes_accessed=10**7, transcendentals=0)
 
@@ -431,29 +430,29 @@
     )
 
     swapped = swaps(vector, "strip", STRIPS)
-    vector_vmem, source_row, target_row, right_vmem, left = pl.pallas_call(
+    vector_vmem, source_row, target_row, right_vmem = pl.pallas_call(
         bring,
-        out_shape=(block, integers, integers, factors, factors),
-        in_specs=[HBM] * 5,
-        out_specs=(VMEM,) * 5,
-        scratch_shapes=[pltpu.SemaphoreType.DMA((5,))],
+        out_shape=(block, integers, integers, factors),
+        in_specs=[HBM] * 4,
+        out_specs=(VMEM,) * 4,
+        scratch_shapes=[pltpu.SemaphoreType.DMA((4,))],
         compiler_params=limit(4),
         cost_estimate=cost,
         name="bring",
-    )(source_row, target_row, in_hbm(vector), right, left)
+    )(source_row, target_row, in_hbm(vector), right)
     start = own_blocks(vector_vmem, *swapped, source_row)
     sides = swaps(start, "blk", BLKS)
     gathered, coefficients = gathered_and_coefficients(1)
-    coefficients = pl.pallas_call(
+    coefficients, left = pl.pallas_call(
         first_project,
-        out_shape=coefficients,
-        in_specs=[VMEM] * 3,
-        out_specs=VMEM,
-        scratch_shapes=[gathered],
+        out_shape=(coefficients, factors),
+        in_specs=[VMEM, VMEM, VMEM, HBM],
+        out_specs=(VMEM, VMEM),
+        scratch_shapes=[gathered, pltpu.SemaphoreType.DMA],
         compiler_params=limit(4),
         cost_estimate=cost,
         name="first_project",
-    )(source_row, start, right_vmem)
+    )(source_row, start, right_vmem, left)
     payload = expand_call(first_expand, name="first_expand")(target_row, start, coefficients, left)
     payload, *sides = lax.optimization_barrier((payload, *sides))
     received_one = exchange(payload)
@@ -467,19 +466,29 @@
         name="first_image",
     )(start, rounded_one, received_one)
     swapped = swaps(image, "strip", STRIPS)
-    own = own_blocks(image, *swapped, row)
+    right_vmem = pl.pallas_call(
+        bring_right,
+        out_shape=factors,
+        in_specs=[ANY, HBM],
+        out_specs=VMEM,
+        scratch_shapes=[pltpu.SemaphoreType.DMA],
+        compiler_params=limit(4),
+        cost_estimate=cost,
+        name="bring_right",
+    )(image, right)
+    own = own_blocks(image, *swapped, right_vmem)
     sides = swaps(own, "blk", BLKS)
     gathered, coefficients = gathered_and_coefficients(3)
     coefficients = pl.pallas_call(
         second_project,
         out_shape=coefficients,
-        in_specs=[VMEM, VMEM, HBM],
+        in_specs=[VMEM] * 3,
         out_specs=VMEM,
-        scratch_shapes=[far_buffer, gathered, pltpu.SemaphoreType.DMA((FAR_COPIES,))],
-        compiler_params=limit(8),
+        scratch_shapes=[gathered],
+        compiler_params=limit(4),
         cost_estimate=cost,
         name="second_project",
-    )(source_row, own, right)
+    )(source_row, own, right_vmem)
     payload = expand_call(second_expand, name="second_expand")(row, own, coefficients, left)
     payload, *sides = lax.optimization_barrier((payload, *sides))
     received_two = exchange(payload)

time: 82.4 us -> 80.6 us (0.978)
  waiting for transfers between devices: 9.63 us -> 7.88 us
    ppermute x8, waiting for transfers between devices: 2.38 us -> 0.56 us  [swaps(): return (lax.ppermute(x, axis, even), lax.ppermute(x, axis, odd))]
    all_to_all x2, starting transfers between devices: 14.8 us -> 13.2 us  [exchange(): return lax.all_to_all(x, ('strip', 'blk'), 0, 0, tiled=True)]
    ppermute x8, starting transfers between devices: 13.3 us -> 14.3 us  [swaps(): return (lax.ppermute(x, axis, even), lax.ppermute(x, axis, odd))]
    pallas_call x3 -> x4, Pallas kernels: 6.58 us -> 6.97 us  [the longest x1 1.97 us: local(): pl.pallas_call(bring, out_shape=(block, integers, integers, factors), in_...]
  transfers between devices with their start and end apart: 10 -> 10, of which waited for: 5 -> 3; matrix products, arithmetic and copies ran while one was open for 0% -> 0% of each run, Pallas kernels for 29% -> 30%
where the time goes in v5:
time: 80.6 us; the launch traced here: 80.3 us
  starting transfers between devices  27.5 us (34%)
  Pallas kernels  27.3 us (34%)
  blocking collectives  16.1 us (20%)
  waiting for transfers between devices  7.88 us (10%)
  between operations  0.82 us (1%)
    all_to_all x1, blocking collectives, exchange(): return lax.all_to_all(x, ('strip', 'blk'), 0, 0, tiled=True)  16.1 us
    ppermute x8, starting transfers between devices, swaps(): return (lax.ppermute(x, axis, even), lax.ppermute(x, axis, odd))  14.3 us
    all_to_all x2, starting transfers between devices, exchange(): return lax.all_to_all(x, ('strip', 'blk'), 0, 0, tiled=True)  13.2 us
    pallas_call x1, Pallas kernels, local(): local_call()(near_pair, conductivity, own, *sides, near_kernel)  7.57 us
    all_to_all x2, waiting for transfers between devices, exchange(): return lax.all_to_all(x, ('strip', 'blk'), 0, 0, tiled=True)  7.32 us
    pallas_call x1, Pallas kernels, local(): local_call()(near_pair, conductivity, start, *sides, near_kernel)  6.97 us
    pallas_call x1, Pallas kernels, local(): pl.pallas_call(bring, out_shape=(block, integers, integers, factors), in_...  1.97 us
    pallas_call x1, Pallas kernels, local(): pl.pallas_call(first_project, out_shape=(coefficients, factors), in_specs...  1.9 us
  transfers between devices with their start and end apart: 10, of which 3 were waited for; matrix products, arithmetic and copies ran while one was open for 0% of the time, Pallas kernels for 30%

profile of v5, /device:TPU:1, one launch (start us, length us, event | category | flops | bytes accessed | tf_op | source)
XLA Modules:
  0.0 80.3 jit_solution(16084726088140555186)
XLA Ops:
  0.6 2.7 %collective-permute-start.1 = (f32[4,8,128]{2,1,0:T(8,128)}, f32[4,8,128]{2,1,0:T(8,128)S(1)}, u32[]{:S(2)}, u32[]{:S(2)}) collective-permute-start(f32[4,8,128]{2,1,0:T(8,128)} %vector_hbm.1), channel_id=1, source_target_pairs={{0,112},{16,32},{32,16},{48,64},{64,48},{80,96},{96,80},{112,0},{1... | collective-permute-start | bytes 49160 | tf_op jit(solution)/shard_map/ppermute | solution.py:377
  3.3 1.1 %collective-permute-start = (f32[4,8,128]{2,1,0:T(8,128)}, f32[4,8,128]{2,1,0:T(8,128)S(1)}, u32[]{:S(2)}, u32[]{:S(2)}) collective-permute-start(f32[4,8,128]{2,1,0:T(8,128)} %vector_hbm.1), channel_id=1, source_target_pairs={{0,16},{16,0},{32,48},{48,32},{64,80},{80,64},{96,112},{112,96},{1... | collective-permute-start | bytes 49160 | tf_op jit(solution)/shard_map/ppermute | solution.py:377
  4.4 2.0 %bring.1 = (f32[4,8,128]{2,1,0:T(8,128)S(1)}, s32[1,128]{1,0:T(1,128)S(1)}, s32[1,128]{1,0:T(1,128)S(1)}, bf16[128,3,32,128]{3,2,1,0:T(8,128)(2,1)S(1)}) custom-call(s32[1,128]{1,0:T(1,128)} %source_hbm.1, s32[1,128]{1,0:T(1,128)} %target_hbm.1, f32[4,8,128]{2,1,0:T(8,128)} %vector_hbm.1, bf16[128,3,32,128]{3,2,1,0:T(8,128)(2,1)} %bitcast.12), custom_call_target="tpu_custom_call" | custom-call | flops 200000000 | bytes 10000000 | tf_op jit(solution)/shard_map/bring/pallas_call | solution.py:433
  6.4 0.0 collective-permute-done.swap_a
  6.4 6.3 %collective-permute-start.3 = (f32[5,8,128]{2,1,0:T(8,128)S(1)}, f32[5,8,128]{2,1,0:T(8,128)S(1)}, u32[]{:S(2)}, u32[]{:S(2)}) collective-permute-start(f32[5,8,128]{2,1,0:T(8,128)S(1)} %edges.2.vector.after.own), channel_id=1, source_target_pairs={{0,15},{1,2},{2,1},{3,4},{4,3},{5,6},{6,5},{7,8},{8,7},{9,10},{10,... | collective-permute-start | bytes 61448 | tf_op jit(solution)/shard_map/ppermute | solution.py:377
  12.7 0.0 collective-permute-start.2
  12.7 1.9 %first_project.1 = (bf16[8,16,512]{2,1,0:T(8,128)(2,1)S(1)}, bf16[128,3,32,128]{3,2,1,0:T(8,128)(2,1)S(1)}) custom-call(s32[1,128]{1,0:T(1,128)S(1)} %get-tuple-element.25.after.source_row, f32[5,8,128]{2,1,0:T(8,128)S(1)} %edges.2.vector.after.own, bf16[128,3,32,128]{3,2,1,0:T(8,128)(2,1)S(1)} %get-tuple-element.27.right, bf16[128,3,32,128]{3,2,1,0:T(8,128)(2,1)} %bitcast.14), custom_call_target="tpu_custom_call" | custom-call | flops 200000000 | bytes 10000000 | tf_op jit(solution)/shard_map/first_project/pallas_call | solution.py:446
  14.6 0.0 copy-start
  14.7 0.0 copy-start.1
  14.7 1.2 %first_expand.1 = f32[128,4,128]{2,1,0:T(4,128)} custom-call(s32[1,128]{1,0:T(1,128)S(1)} %get-tuple-element.26.target_row, f32[5,8,128]{2,1,0:T(8,128)S(1)} %edges.2.vector.after.own, bf16[8,16,512]{2,1,0:T(8,128)(2,1)S(1)} %get-tuple-element.28.coefficients, bf16[128,3,32,128]{3,2,1,0:T(8,128)(2,1)S(1)} %get-tuple-element.29.left), custom_call_target="tpu_custom_call" | custom-call | flops 200000000 | bytes 10000000 | tf_op jit(solution)/shard_map/first_expand/pallas_call | solution.py:456
  15.9 0.0 collective-permute-done.2.swap_a
  15.9 6.7 %all-to-all-start = ((f32[128,4,128]{2,1,0:T(4,128)}), f32[128,4,128]{2,1,0:T(4,128)S(1)}, u32[]{:S(2)}, u32[]{:S(2)}) async-start(f32[128,4,128]{2,1,0:T(4,128)} %first_expand.1), calls=%async_computation | async-start | bytes 524288 | tf_op jit(solution)/shard_map/all_to_all | solution.py:371
  22.6 7.0 %local_part.2 = (f32[4,8,128]{2,1,0:T(8,128)S(1)}, f32[4,8,128]{2,1,0:T(8,128)S(1)}) custom-call(s32[48]{0:T(128)S(1)} %copy-done.1, f32[4,8,128]{2,1,0:T(8,128)S(1)} %copy-done, f32[5,8,128]{2,1,0:T(8,128)S(1)} %edges.2.vector.after.own, f32[5,8,128]{2,1,0:T(8,128)S(1)} %collective-permute-done.2.swap_a, f32[5,8,128]{2,1,0:T(8,128)S(1)} %collective-permute-done.3.swap_b, ...), custom_call_target="tpu_custom_call" | custom-call | flops 400000000 | bytes 20000000 | tf_op jit(solution)/shard_map/local_part/pallas_call | solution.py:459
  29.6 4.2 %all-to-all-done.received.target = f32[128,4,128]{2,1,0:T(4,128)S(1)} async-done(((f32[128,4,128]{2,1,0:T(4,128)}), f32[128,4,128]{2,1,0:T(4,128)S(1)}, u32[]{:S(2)}, u32[]{:S(2)}) %all-to-all-start) | async-done | bytes 262176 | tf_op jit(solution)/shard_map/all_to_all | solution.py:371
  33.9 0.5 first_image.1
  34.3 0.9 %collective-permute-start.5 = (f32[4,8,128]{2,1,0:T(8,128)S(1)}, f32[4,8,128]{2,1,0:T(8,128)S(1)}, u32[]{:S(2)}, u32[]{:S(2)}) collective-permute-start(f32[4,8,128]{2,1,0:T(8,128)S(1)} %get-tuple-element.34.after.vector.image), channel_id=1, source_target_pairs={{0,112},{16,32},{32,16},{48,64},{64,48},{80,96},{96,80},{112,0},{1... | collective-permute-start | bytes 49160 | tf_op jit(solution)/shard_map/ppermute | solution.py:377
  35.3 0.4 collective-permute-start.4
  35.7 1.9 %bring_right.1.after.right = bf16[128,3,32,128]{3,2,1,0:T(8,128)(2,1)S(1)} custom-call(f32[4,8,128]{2,1,0:T(8,128)S(1)} %get-tuple-element.34.after.vector.image, bf16[128,3,32,128]{3,2,1,0:T(8,128)(2,1)} %bitcast.13), custom_call_target="tpu_custom_call" | custom-call | flops 200000000 | bytes 10000000 | tf_op jit(solution)/shard_map/bring_right/pallas_call | solution.py:469
  37.6 0.0 collective-permute-done.5.swap_b
  37.6 2.9 %collective-permute-start.7 = (f32[5,8,128]{2,1,0:T(8,128)S(1)}, f32[5,8,128]{2,1,0:T(8,128)S(1)}, u32[]{:S(2)}, u32[]{:S(2)}) collective-permute-start(f32[5,8,128]{2,1,0:T(8,128)S(1)} %edges.3.vector.after.own), channel_id=1, source_target_pairs={{0,15},{1,2},{2,1},{3,4},{4,3},{5,6},{6,5},{7,8},{8,7},{9,10},{10,... | collective-permute-start | bytes 61448 | tf_op jit(solution)/shard_map/ppermute | solution.py:377
  40.6 0.0 collective-permute-start.6
  40.6 1.2 %second_project.1.coefficients = bf16[8,48,512]{2,1,0:T(8,128)(2,1)S(1)} custom-call(s32[1,128]{1,0:T(1,128)S(1)} %get-tuple-element.25.after.source_row, f32[5,8,128]{2,1,0:T(8,128)S(1)} %edges.3.vector.after.own, bf16[128,3,32,128]{3,2,1,0:T(8,128)(2,1)S(1)} %bring_right.1.after.right), custom_call_target="tpu_custom_call" | custom-call | flops 200000000 | bytes 10000000 | tf_op jit(solution)/shard_map/second_project/pallas_call | solution.py:482
  41.8 1.3 %second_expand.1 = f32[128,4,128]{2,1,0:T(4,128)} custom-call(f32[1,128]{1,0:T(1,128)S(1)} %get-tuple-element.36.row, f32[5,8,128]{2,1,0:T(8,128)S(1)} %edges.3.vector.after.own, bf16[8,48,512]{2,1,0:T(8,128)(2,1)S(1)} %second_project.1.coefficients, bf16[128,3,32,128]{3,2,1,0:T(8,128)(2,1)S(1)} %get-tuple-element.29.left), custom_call_target="tpu_custom_call" | custom-call | flops 200000000 | bytes 10000000 | tf_op jit(solution)/shard_map/second_expand/pallas_call | solution.py:492
  43.1 0.5 collective-permute-done.7.swap_b
  43.7 6.5 %all-to-all-start.1 = ((f32[128,4,128]{2,1,0:T(4,128)}), f32[128,4,128]{2,1,0:T(4,128)S(1)}, u32[]{:S(2)}, u32[]{:S(2)}) async-start(f32[128,4,128]{2,1,0:T(4,128)} %second_expand.1), calls=%async_computation.1 | async-start | bytes 524288 | tf_op jit(solution)/shard_map/all_to_all | solution.py:371
  50.1 0.0 copy-start.2
  50.2 0.6 copy-done.2
  50.8 7.6 %local_part.3 = (f32[4,8,128]{2,1,0:T(8,128)}, f32[4,8,128]{2,1,0:T(8,128)S(1)}) custom-call(s32[48]{0:T(128)S(1)} %copy-done.2, f32[4,8,128]{2,1,0:T(8,128)S(1)} %copy-done, f32[5,8,128]{2,1,0:T(8,128)S(1)} %edges.3.vector.after.own, f32[5,8,128]{2,1,0:T(8,128)S(1)} %collective-permute-done.6.swap_a, f32[5,8,128]{2,1,0:T(8,128)S(1)} %collective-permute-done.7.swap_b, ...), custom_call_target="tpu_custom_call" | custom-call | flops 400000000 | bytes 20000000 | tf_op jit(solution)/shard_map/local_part/pallas_call | solution.py:495
  58.4 3.1 %all-to-all-done.1.received = f32[128,4,128]{2,1,0:T(4,128)S(1)} async-done(((f32[128,4,128]{2,1,0:T(4,128)}), f32[128,4,128]{2,1,0:T(4,128)S(1)}, u32[]{:S(2)}, u32[]{:S(2)}) %all-to-all-start.1) | async-done | bytes 262176 | tf_op jit(solution)/shard_map/all_to_all | solution.py:371
  61.5 1.3 %second_image.1 = (f32[4,8,128]{2,1,0:T(8,128)S(1)}, f32[4,8,128]{2,1,0:T(8,128)S(1)}, f32[1,128]{1,0:T(1,128)S(1)}, f32[128,128]{1,0:T(8,128)S(1)}) custom-call(f32[5,8,128]{2,1,0:T(8,128)S(1)} %edges.2.vector.after.own, f32[4,8,128]{2,1,0:T(8,128)S(1)} %get-tuple-element.34.after.vector.image, f32[4,8,128]{2,1,0:T(8,128)S(1)} %get-tuple-element.35.local_one, ...), custom_call_target="tpu_custom_call" | custom-call | tf_op jit(solution)/shard_map/second_image/pallas_call | solution.py:496
  62.7 16.1 %all_to_all.21 = f32[128,1,128]{2,1,0:T(1,128)S(1)} all-to-all(f32[128,1,128]{2,1,0:T(1,128)S(1)} %bitcast.11), channel_id=1, replica_groups=mesh['strip'=8,'blk'=16] {'strip','blk'}, dimensions={0} | all-to-all | bytes 131072 | tf_op jit(solution)/shard_map/all_to_all | solution.py:371
  78.9 1.4 %finish.1 = (f32[2,4,8,128]{3,2,1,0:T(8,128)}, f32[5]{0:T(128)}) custom-call(f32[5,8,128]{2,1,0:T(8,128)S(1)} %edges.2.vector.after.own, f32[4,8,128]{2,1,0:T(8,128)S(1)} %get-tuple-element.42.first, f32[4,8,128]{2,1,0:T(8,128)S(1)} %get-tuple-element.43.image, f32[1,128]{1,0:T(1,128)S(1)} %get-tuple-element.44.scalars, f32[128,128]{1,0:T(8,128)S(1)} %bitcast.10), custom_call_target="tpu_custom_call" | custom-call | tf_op jit(solution)/shard_map/finish/pallas_call | solution.py:505
  (8 shorter events, 0.1 us)
Async XLA Ops:
  0.6 5.8 %collective-permute-start.1 = (f32[4,8,128]{2,1,0:T(8,128)}, f32[4,8,128]{2,1,0:T(8,128)S(1)}, u32[]{:S(2)}, u32[]{:S(2)}) collective-permute-start(f32[4,8,128]{2,1,0:T(8,128)} %vector_hbm.1), channel_id=1, source_target_pairs={{0,112},{16,32},{32,16},{48,64},{64,48},{80,96},{96,80},{112,0},{1... | collective-permute-start | bytes 49160 | tf_op jit(solution)/shard_map/ppermute | solution.py:377
  3.3 3.1 %collective-permute-start = (f32[4,8,128]{2,1,0:T(8,128)}, f32[4,8,128]{2,1,0:T(8,128)S(1)}, u32[]{:S(2)}, u32[]{:S(2)}) collective-permute-start(f32[4,8,128]{2,1,0:T(8,128)} %vector_hbm.1), channel_id=1, source_target_pairs={{0,16},{16,0},{32,48},{48,32},{64,80},{80,64},{96,112},{112,96},{1... | collective-permute-start | bytes 49160 | tf_op jit(solution)/shard_map/ppermute | solution.py:377
  6.4 9.5 %collective-permute-start.3 = (f32[5,8,128]{2,1,0:T(8,128)S(1)}, f32[5,8,128]{2,1,0:T(8,128)S(1)}, u32[]{:S(2)}, u32[]{:S(2)}) collective-permute-start(f32[5,8,128]{2,1,0:T(8,128)S(1)} %edges.2.vector.after.own), channel_id=1, source_target_pairs={{0,15},{1,2},{2,1},{3,4},{4,3},{5,6},{6,5},{7,8},{8,7},{9,10},{10,... | collective-permute-start | bytes 61448 | tf_op jit(solution)/shard_map/ppermute | solution.py:377
  12.7 3.2 %collective-permute-start.2 = (f32[5,8,128]{2,1,0:T(8,128)S(1)}, f32[5,8,128]{2,1,0:T(8,128)S(1)}, u32[]{:S(2)}, u32[]{:S(2)}) collective-permute-start(f32[5,8,128]{2,1,0:T(8,128)S(1)} %edges.2.vector.after.own), channel_id=1, source_target_pairs={{0,1},{1,0},{2,3},{3,2},{4,5},{5,4},{6,7},{7,6},{8,9},{9,8},{10,11... | collective-permute-start | bytes 61448 | tf_op jit(solution)/shard_map/ppermute | solution.py:377
  14.6 8.0 %copy-start = (f32[4,8,128]{2,1,0:T(8,128)S(1)}, f32[4,8,128]{2,1,0:T(8,128)}, u32[]{:S(2)}) copy-start(f32[4,8,128]{2,1,0:T(8,128)} %conductivity.3) | copy-start | bytes 49156
  14.7 8.0 %copy-start.1 = (s32[48]{0:T(128)S(1)}, s32[48]{0:T(128)}, u32[]{:S(2)}) copy-start(s32[48]{0:T(128)} %near_pair.3) | copy-start | bytes 580
  15.9 17.9 %all-to-all-start = ((f32[128,4,128]{2,1,0:T(4,128)}), f32[128,4,128]{2,1,0:T(4,128)S(1)}, u32[]{:S(2)}, u32[]{:S(2)}) async-start(f32[128,4,128]{2,1,0:T(4,128)} %first_expand.1), calls=%async_computation | async-start | bytes 524288 | tf_op jit(solution)/shard_map/all_to_all | solution.py:371
  34.3 3.2 %collective-permute-start.5 = (f32[4,8,128]{2,1,0:T(8,128)S(1)}, f32[4,8,128]{2,1,0:T(8,128)S(1)}, u32[]{:S(2)}, u32[]{:S(2)}) collective-permute-start(f32[4,8,128]{2,1,0:T(8,128)S(1)} %get-tuple-element.34.after.vector.image), channel_id=1, source_target_pairs={{0,112},{16,32},{32,16},{48,64},{64,48},{80,96},{96,80},{112,0},{1... | collective-permute-start | bytes 49160 | tf_op jit(solution)/shard_map/ppermute | solution.py:377
  35.3 2.3 %collective-permute-start.4 = (f32[4,8,128]{2,1,0:T(8,128)S(1)}, f32[4,8,128]{2,1,0:T(8,128)S(1)}, u32[]{:S(2)}, u32[]{:S(2)}) collective-permute-start(f32[4,8,128]{2,1,0:T(8,128)S(1)} %get-tuple-element.34.after.vector.image), channel_id=1, source_target_pairs={{0,16},{16,0},{32,48},{48,32},{64,80},{80,64},{96,112},{112,96},{1... | collective-permute-start | bytes 49160 | tf_op jit(solution)/shard_map/ppermute | solution.py:377
  37.6 6.0 %collective-permute-start.7 = (f32[5,8,128]{2,1,0:T(8,128)S(1)}, f32[5,8,128]{2,1,0:T(8,128)S(1)}, u32[]{:S(2)}, u32[]{:S(2)}) collective-permute-start(f32[5,8,128]{2,1,0:T(8,128)S(1)} %edges.3.vector.after.own), channel_id=1, source_target_pairs={{0,15},{1,2},{2,1},{3,4},{4,3},{5,6},{6,5},{7,8},{8,7},{9,10},{10,... | collective-permute-start | bytes 61448 | tf_op jit(solution)/shard_map/ppermute | solution.py:377
  40.6 3.1 %collective-permute-start.6 = (f32[5,8,128]{2,1,0:T(8,128)S(1)}, f32[5,8,128]{2,1,0:T(8,128)S(1)}, u32[]{:S(2)}, u32[]{:S(2)}) collective-permute-start(f32[5,8,128]{2,1,0:T(8,128)S(1)} %edges.3.vector.after.own), channel_id=1, source_target_pairs={{0,1},{1,0},{2,3},{3,2},{4,5},{5,4},{6,7},{7,6},{8,9},{9,8},{10,11... | collective-permute-start | bytes 61448 | tf_op jit(solution)/shard_map/ppermute | solution.py:377
  43.7 17.8 %all-to-all-start.1 = ((f32[128,4,128]{2,1,0:T(4,128)}), f32[128,4,128]{2,1,0:T(4,128)S(1)}, u32[]{:S(2)}, u32[]{:S(2)}) async-start(f32[128,4,128]{2,1,0:T(4,128)} %second_expand.1), calls=%async_computation.1 | async-start | bytes 524288 | tf_op jit(solution)/shard_map/all_to_all | solution.py:371
  50.1 0.7 copy-start.2

commit v6 on v5

--- a/solution.py
+++ b/solution.py
@@ -51,6 +51,11 @@
     return two_sum(s, e + (x[1] + y[1]))
 
 
+def loose_add(x, y):
+    s, e = two_sum(x[0], y[0])
+    return s, e + (x[1] + y[1])
+
+
 def pair_mul(x, y):
     p, e = two_prod(x[0], y[0])
     return two_sum(p, e + (x[0] * y[1] + x[1] * y[0]))
@@ -71,9 +76,10 @@
     for k, (a, b) in enumerate(pairs):
         s, e = two_prod(a[0], b[0])
         for c in range(1, 4):
-            s, e = pair_add((s, e), two_prod(a[c], b[c]))
+            s, e = loose_add((s, e), two_prod(a[c], b[c]))
         for step in (4, 2, 1):
-            s, e = pair_add((s, e), (pltpu.roll(s, step, 0), pltpu.roll(e, step, 0)))
+            s, e = loose_add((s, e), (pltpu.roll(s, step, 0), pltpu.roll(e, step, 0)))
+        s, e = two_sum(s, e)
         high = jnp.where(sub == k, s, high)
         low = jnp.where(sub == k, e, low)
     pad = jnp.zeros((LEN - 16, LEN), F32)
@@ -85,11 +91,12 @@
 def column_sums(x):
     parts = [(x[8 * i : 8 * i + 8], jnp.zeros((8, LEN), F32)) for i in range(16)]
     while len(parts) > 1:
-        parts = [pair_add(parts[i], parts[i + 1]) for i in range(0, len(parts), 2)]
+        parts = [loose_add(parts[i], parts[i + 1]) for i in range(0, len(parts), 2)]
     s, e = parts[0]
     for step in (4, 2, 1):
-        s, e = pair_add((s, e), (pltpu.roll(s, step, 0), pltpu.roll(e, step, 0)))
-    return s[0:1], e[0:1]
+        s, e = loose_add((s, e), (pltpu.roll(s, step, 0), pltpu.roll(e, step, 0)))
+    s, e = two_sum(s[0:1], e[0:1])
+    return s, e
 
 
 def totals(rows, count):
@@ -263,16 +270,23 @@
     expand(1, coefficients, left, out, payload, sems)
 
 
-def second_expand(row, after, coefficients, left, out, payload, sems):
-    payload[:, 3, :] = jnp.broadcast_to(row[...], (DEVICES, LEN))
+def second_expand(vector, image, coefficients, left, out, payload, sems):
+    start = [vector[c] for c in range(4)]
+    own = [image[c] for c in range(4)]
+    row = dot_row([(start, start), (start, own), (own, own)])
+    payload[:, 3, :] = jnp.broadcast_to(row, (DEVICES, LEN))
     expand(3, coefficients, left, out, payload, sems)
 
 
 def edges(vector, swap_a, swap_b, after, out):
     strip, _ = place()
     even = lax.rem(strip, 2) == 0
-    above = jnp.where(even, swap_b[:, ROWS - 1, :], swap_a[:, ROWS - 1, :])
-    below = jnp.where(even, swap_a[:, 0, :], swap_b[:, 0, :])
+    if len(swap_a.shape) == 3:
+        above = jnp.where(even, swap_b[:, ROWS - 1, :], swap_a[:, ROWS - 1, :])
+        below = jnp.where(even, swap_a[:, 0, :], swap_b[:, 0, :])
+    else:
+        above = jnp.where(even, swap_b[...], swap_a[...])
+        below = jnp.where(even, swap_a[...], swap_b[...])
     out[0:4] = vector[...]
     out[4, 0:4, :] = jnp.where(strip > 0, above, 0.0)
     out[4, 4:8, :] = jnp.where(strip < STRIPS - 1, below, 0.0)
@@ -298,7 +312,7 @@
         full[a] = near_full[:, a * LEN : (a + 1) * LEN]
 
 
-def first_image(vector, local, received, image, far_part, row):
+def first_image(vector, local, received, image, far_part, to_even, to_odd):
     arrived = far_sum(received, lambda g: received[g, 3:4, :])
     for a in range(3):
         far_part[a] = arrived[a]
@@ -306,7 +320,10 @@
     result = image_of(own, local, arrived)
     for c in range(4):
         image[c] = result[c]
-    row[...] = dot_row([(own, own), (own, result), (result, result)])
+    strip, _ = place()
+    even = lax.rem(strip, 2) == 0
+    to_even[...] = jnp.where(even, image[:, ROWS - 1, :], image[:, 0, :])
+    to_odd[...] = jnp.where(even, image[:, 0, :], image[:, ROWS - 1, :])
 
 
 def second_image(vector, image, local_one, local_two, target, received, far_one, first, image_two, scalars, rows):
@@ -457,15 +474,15 @@
     payload, *sides = lax.optimization_barrier((payload, *sides))
     received_one = exchange(payload)
     rounded_one, local_one = local_call()(near_pair, conductivity, start, *sides, near_kernel)
-    image, far_one, row = pl.pallas_call(
+    image, far_one, to_even, to_odd = pl.pallas_call(
         first_image,
-        out_shape=(block, shape(3, ROWS, LEN), line),
+        out_shape=(block, shape(3, ROWS, LEN), shape(4, LEN), shape(4, LEN)),
         in_specs=[VMEM] * 3,
-        out_specs=(VMEM,) * 3,
+        out_specs=(VMEM,) * 4,
         compiler_params=limit(4),
         name="first_image",
     )(start, rounded_one, received_one)
-    swapped = swaps(image, "strip", STRIPS)
+    swapped = swaps(to_even, "strip", STRIPS)[0], swaps(to_odd, "strip", STRIPS)[1]
     right_vmem = pl.pallas_call(
         bring_right,
         out_shape=factors,
@@ -489,7 +506,7 @@
         cost_estimate=cost,
         name="second_project",
     )(source_row, own, right_vmem)
-    payload = expand_call(second_expand, name="second_expand")(row, own, coefficients, left)
+    payload = expand_call(second_expand, in_specs=[VMEM] * 4, name="second_expand")(start, own, coefficients, left)
     payload, *sides = lax.optimization_barrier((payload, *sides))
     received_two = exchange(payload)
     _, local_two = local_call()(near_pair, conductivity, own, *sides, near_kernel)

time: 80.6 us -> 80.1 us (level)
  starting transfers between devices: 27.5 us -> 25 us
  waiting for transfers between devices: 7.88 us -> 10.3 us
    ppermute x8, waiting for transfers between devices: 0.56 us -> 2.94 us  [swaps(): return (lax.ppermute(x, axis, even), lax.ppermute(x, axis, odd))]
    ppermute x8, starting transfers between devices: 14.3 us -> 12.4 us  [swaps(): return (lax.ppermute(x, axis, even), lax.ppermute(x, axis, odd))]
  transfers between devices with their start and end apart: 10 -> 10, of which waited for: 3 -> 4; matrix products, arithmetic and copies ran while one was open for 0% -> 0% of each run, Pallas kernels for 30% -> 30%
where the time goes in v6:
time: 80.1 us; the launch traced here: 79.8 us
  Pallas kernels  26.8 us (33%)
  starting transfers between devices  25 us (31%)
  blocking collectives  16.1 us (20%)
  waiting for transfers between devices  10.3 us (13%)
  between operations  0.81 us (1%)
    all_to_all x1, blocking collectives, exchange(): return lax.all_to_all(x, ('strip', 'blk'), 0, 0, tiled=True)  16.1 us
    all_to_all x2, starting transfers between devices, exchange(): return lax.all_to_all(x, ('strip', 'blk'), 0, 0, tiled=True)  12.6 us
    ppermute x8, starting transfers between devices, swaps(): return (lax.ppermute(x, axis, even), lax.ppermute(x, axis, odd))  12.4 us
    pallas_call x1, Pallas kernels, local(): local_call()(near_pair, conductivity, own, *sides, near_kernel)  7.57 us
    all_to_all x2, waiting for transfers between devices, exchange(): return lax.all_to_all(x, ('strip', 'blk'), 0, 0, tiled=True)  7.37 us
    pallas_call x1, Pallas kernels, local(): local_call()(near_pair, conductivity, start, *sides, near_kernel)  6.97 us
    ppermute x8, waiting for transfers between devices, swaps(): return (lax.ppermute(x, axis, even), lax.ppermute(x, axis, odd))  2.94 us
    pallas_call x1, Pallas kernels, local(): pl.pallas_call(bring, out_shape=(block, integers, integers, factors), in_...  1.97 us
  transfers between devices with their start and end apart: 10, of which 4 were waited for; matrix products, arithmetic and copies ran while one was open for 0% of the time, Pallas kernels for 30%

profile of v6, /device:TPU:1, one launch (start us, length us, event | category | flops | bytes accessed | tf_op | source)
XLA Modules:
  0.0 79.8 jit_solution(3882743286121220184)
XLA Ops:
  0.6 2.7 %collective-permute-start.1 = (f32[4,8,128]{2,1,0:T(8,128)}, f32[4,8,128]{2,1,0:T(8,128)S(1)}, u32[]{:S(2)}, u32[]{:S(2)}) collective-permute-start(f32[4,8,128]{2,1,0:T(8,128)} %vector_hbm.1), channel_id=1, source_target_pairs={{0,112},{16,32},{32,16},{48,64},{64,48},{80,96},{96,80},{112,0},{1... | collective-permute-start | bytes 49160 | tf_op jit(solution)/shard_map/ppermute | solution.py:394
  3.3 1.1 %collective-permute-start = (f32[4,8,128]{2,1,0:T(8,128)}, f32[4,8,128]{2,1,0:T(8,128)S(1)}, u32[]{:S(2)}, u32[]{:S(2)}) collective-permute-start(f32[4,8,128]{2,1,0:T(8,128)} %vector_hbm.1), channel_id=1, source_target_pairs={{0,16},{16,0},{32,48},{48,32},{64,80},{80,64},{96,112},{112,96},{1... | collective-permute-start | bytes 49160 | tf_op jit(solution)/shard_map/ppermute | solution.py:394
  4.4 2.0 %bring.1 = (f32[4,8,128]{2,1,0:T(8,128)S(1)}, s32[1,128]{1,0:T(1,128)S(1)}, s32[1,128]{1,0:T(1,128)S(1)}, bf16[128,3,32,128]{3,2,1,0:T(8,128)(2,1)S(1)}) custom-call(s32[1,128]{1,0:T(1,128)} %source_hbm.1, s32[1,128]{1,0:T(1,128)} %target_hbm.1, f32[4,8,128]{2,1,0:T(8,128)} %vector_hbm.1, bf16[128,3,32,128]{3,2,1,0:T(8,128)(2,1)} %bitcast.12), custom_call_target="tpu_custom_call" | custom-call | flops 200000000 | bytes 10000000 | tf_op jit(solution)/shard_map/bring/pallas_call | solution.py:450
  6.4 0.0 collective-permute-done.1.swap_b
  6.4 0.0 collective-permute-done.swap_a
  6.4 6.3 %collective-permute-start.3 = (f32[5,8,128]{2,1,0:T(8,128)S(1)}, f32[5,8,128]{2,1,0:T(8,128)S(1)}, u32[]{:S(2)}, u32[]{:S(2)}) collective-permute-start(f32[5,8,128]{2,1,0:T(8,128)S(1)} %edges.2.vector.after.own), channel_id=1, source_target_pairs={{0,15},{1,2},{2,1},{3,4},{4,3},{5,6},{6,5},{7,8},{8,7},{9,10},{10,... | collective-permute-start | bytes 61448 | tf_op jit(solution)/shard_map/ppermute | solution.py:394
  12.7 0.0 collective-permute-start.2
  12.7 1.9 %first_project.1 = (bf16[8,16,512]{2,1,0:T(8,128)(2,1)S(1)}, bf16[128,3,32,128]{3,2,1,0:T(8,128)(2,1)S(1)}) custom-call(s32[1,128]{1,0:T(1,128)S(1)} %get-tuple-element.26.after.source_row, f32[5,8,128]{2,1,0:T(8,128)S(1)} %edges.2.vector.after.own, bf16[128,3,32,128]{3,2,1,0:T(8,128)(2,1)S(1)} %get-tuple-element.28.right, bf16[128,3,32,128]{3,2,1,0:T(8,128)(2,1)} %bitcast.14), custom_call_target="tpu_custom_call" | custom-call | flops 200000000 | bytes 10000000 | tf_op jit(solution)/shard_map/first_project/pallas_call | solution.py:463
  14.6 0.0 copy-start
  14.7 0.0 copy-start.1
  14.7 1.2 %first_expand.1 = f32[128,4,128]{2,1,0:T(4,128)} custom-call(s32[1,128]{1,0:T(1,128)S(1)} %get-tuple-element.27.target_row, f32[5,8,128]{2,1,0:T(8,128)S(1)} %edges.2.vector.after.own, bf16[8,16,512]{2,1,0:T(8,128)(2,1)S(1)} %get-tuple-element.29.coefficients, bf16[128,3,32,128]{3,2,1,0:T(8,128)(2,1)S(1)} %get-tuple-element.30.left), custom_call_target="tpu_custom_call" | custom-call | flops 200000000 | bytes 10000000 | tf_op jit(solution)/shard_map/first_expand/pallas_call | solution.py:473
  15.9 0.0 collective-permute-done.2.swap_a
  15.9 6.7 %all-to-all-start = ((f32[128,4,128]{2,1,0:T(4,128)}), f32[128,4,128]{2,1,0:T(4,128)S(1)}, u32[]{:S(2)}, u32[]{:S(2)}) async-start(f32[128,4,128]{2,1,0:T(4,128)} %first_expand.1), calls=%async_computation | async-start | bytes 524288 | tf_op jit(solution)/shard_map/all_to_all | solution.py:388
  22.6 7.0 %local_part.2 = (f32[4,8,128]{2,1,0:T(8,128)S(1)}, f32[4,8,128]{2,1,0:T(8,128)S(1)}) custom-call(s32[48]{0:T(128)S(1)} %copy-done.1, f32[4,8,128]{2,1,0:T(8,128)S(1)} %copy-done, f32[5,8,128]{2,1,0:T(8,128)S(1)} %edges.2.vector.after.own, f32[5,8,128]{2,1,0:T(8,128)S(1)} %collective-permute-done.2.swap_a, f32[5,8,128]{2,1,0:T(8,128)S(1)} %collective-permute-done.3.swap_b, ...), custom_call_target="tpu_custom_call" | custom-call | flops 400000000 | bytes 20000000 | tf_op jit(solution)/shard_map/local_part/pallas_call | solution.py:476
  29.6 4.2 %all-to-all-done.received.target = f32[128,4,128]{2,1,0:T(4,128)S(1)} async-done(((f32[128,4,128]{2,1,0:T(4,128)}), f32[128,4,128]{2,1,0:T(4,128)S(1)}, u32[]{:S(2)}, u32[]{:S(2)}) %all-to-all-start) | async-done | bytes 262176 | tf_op jit(solution)/shard_map/all_to_all | solution.py:388
  33.9 0.2 first_image.1
  34.1 0.8 collective-permute-start.4
  34.9 0.3 collective-permute-start.5
  35.2 1.9 %bring_right.1.after.right = bf16[128,3,32,128]{3,2,1,0:T(8,128)(2,1)S(1)} custom-call(f32[4,8,128]{2,1,0:T(8,128)S(1)} %get-tuple-element.35.after.vector.image, bf16[128,3,32,128]{3,2,1,0:T(8,128)(2,1)} %bitcast.13), custom_call_target="tpu_custom_call" | custom-call | flops 200000000 | bytes 10000000 | tf_op jit(solution)/shard_map/bring_right/pallas_call | solution.py:486
  37.1 0.8 collective-permute-done.5.swap_b
  37.9 1.2 %collective-permute-start.7 = (f32[5,8,128]{2,1,0:T(8,128)S(1)}, f32[5,8,128]{2,1,0:T(8,128)S(1)}, u32[]{:S(2)}, u32[]{:S(2)}) collective-permute-start(f32[5,8,128]{2,1,0:T(8,128)S(1)} %edges.3.vector.image.own), channel_id=1, source_target_pairs={{0,15},{1,2},{2,1},{3,4},{4,3},{5,6},{6,5},{7,8},{8,7},{9,10},{10,... | collective-permute-start | bytes 61448 | tf_op jit(solution)/shard_map/ppermute | solution.py:394
  39.1 1.2 %second_project.1.coefficients = bf16[8,48,512]{2,1,0:T(8,128)(2,1)S(1)} custom-call(s32[1,128]{1,0:T(1,128)S(1)} %get-tuple-element.26.after.source_row, f32[5,8,128]{2,1,0:T(8,128)S(1)} %edges.3.vector.image.own, bf16[128,3,32,128]{3,2,1,0:T(8,128)(2,1)S(1)} %bring_right.1.after.right), custom_call_target="tpu_custom_call" | custom-call | flops 200000000 | bytes 10000000 | tf_op jit(solution)/shard_map/second_project/pallas_call | solution.py:499
  40.3 1.4 %second_expand.1 = f32[128,4,128]{2,1,0:T(4,128)} custom-call(f32[5,8,128]{2,1,0:T(8,128)S(1)} %edges.2.vector.after.own, f32[5,8,128]{2,1,0:T(8,128)S(1)} %edges.3.vector.image.own, bf16[8,48,512]{2,1,0:T(8,128)(2,1)S(1)} %second_project.1.coefficients, bf16[128,3,32,128]{3,2,1,0:T(8,128)(2,1)S(1)} %get-tuple-element.30.left), custom_call_target="tpu_custom_call" | custom-call | flops 200000000 | bytes 10000000 | tf_op jit(solution)/shard_map/second_expand/pallas_call | solution.py:509
  41.7 2.1 %collective-permute-done.7.swap_b = f32[5,8,128]{2,1,0:T(8,128)S(1)} collective-permute-done((f32[5,8,128]{2,1,0:T(8,128)S(1)}, f32[5,8,128]{2,1,0:T(8,128)S(1)}, u32[]{:S(2)}, u32[]{:S(2)}) %collective-permute-start.7) | collective-permute-done | bytes 20512 | tf_op jit(solution)/shard_map/ppermute | solution.py:394
  43.8 5.9 %all-to-all-start.1 = ((f32[128,4,128]{2,1,0:T(4,128)}), f32[128,4,128]{2,1,0:T(4,128)S(1)}, u32[]{:S(2)}, u32[]{:S(2)}) async-start(f32[128,4,128]{2,1,0:T(4,128)} %second_expand.1), calls=%async_computation.1 | async-start | bytes 524288 | tf_op jit(solution)/shard_map/all_to_all | solution.py:388
  49.7 0.0 copy-start.2
  49.7 0.6 copy-done.2
  50.4 7.6 %local_part.3 = (f32[4,8,128]{2,1,0:T(8,128)}, f32[4,8,128]{2,1,0:T(8,128)S(1)}) custom-call(s32[48]{0:T(128)S(1)} %copy-done.2, f32[4,8,128]{2,1,0:T(8,128)S(1)} %copy-done, f32[5,8,128]{2,1,0:T(8,128)S(1)} %edges.3.vector.image.own, f32[5,8,128]{2,1,0:T(8,128)S(1)} %collective-permute-done.6.swap_a, f32[5,8,128]{2,1,0:T(8,128)S(1)} %collective-permute-done.7.swap_b, ...), custom_call_target="tpu_custom_call" | custom-call | flops 400000000 | bytes 20000000 | tf_op jit(solution)/shard_map/local_part/pallas_call | solution.py:512
  58.0 3.1 %all-to-all-done.1.received = f32[128,4,128]{2,1,0:T(4,128)S(1)} async-done(((f32[128,4,128]{2,1,0:T(4,128)}), f32[128,4,128]{2,1,0:T(4,128)S(1)}, u32[]{:S(2)}, u32[]{:S(2)}) %all-to-all-start.1) | async-done | bytes 262176 | tf_op jit(solution)/shard_map/all_to_all | solution.py:388
  61.1 1.1 %second_image.1 = (f32[4,8,128]{2,1,0:T(8,128)S(1)}, f32[4,8,128]{2,1,0:T(8,128)S(1)}, f32[1,128]{1,0:T(1,128)S(1)}, f32[128,128]{1,0:T(8,128)S(1)}) custom-call(f32[5,8,128]{2,1,0:T(8,128)S(1)} %edges.2.vector.after.own, f32[4,8,128]{2,1,0:T(8,128)S(1)} %get-tuple-element.35.after.vector.image, f32[4,8,128]{2,1,0:T(8,128)S(1)} %get-tuple-element.36.local_one, ...), custom_call_target="tpu_custom_call" | custom-call | tf_op jit(solution)/shard_map/second_image/pallas_call | solution.py:513
  62.2 16.1 %all_to_all.21 = f32[128,1,128]{2,1,0:T(1,128)S(1)} all-to-all(f32[128,1,128]{2,1,0:T(1,128)S(1)} %bitcast.11), channel_id=1, replica_groups=mesh['strip'=8,'blk'=16] {'strip','blk'}, dimensions={0} | all-to-all | bytes 131072 | tf_op jit(solution)/shard_map/all_to_all | solution.py:388
  78.3 1.4 %finish.1 = (f32[2,4,8,128]{3,2,1,0:T(8,128)}, f32[5]{0:T(128)}) custom-call(f32[5,8,128]{2,1,0:T(8,128)S(1)} %edges.2.vector.after.own, f32[4,8,128]{2,1,0:T(8,128)S(1)} %get-tuple-element.44.first, f32[4,8,128]{2,1,0:T(8,128)S(1)} %get-tuple-element.45.image, f32[1,128]{1,0:T(1,128)S(1)} %get-tuple-element.46.scalars, f32[128,128]{1,0:T(8,128)S(1)} %bitcast.10), custom_call_target="tpu_custom_call" | custom-call | tf_op jit(solution)/shard_map/finish/pallas_call | solution.py:522
  (8 shorter events, 0.0 us)
Async XLA Ops:
  0.6 5.8 %collective-permute-start.1 = (f32[4,8,128]{2,1,0:T(8,128)}, f32[4,8,128]{2,1,0:T(8,128)S(1)}, u32[]{:S(2)}, u32[]{:S(2)}) collective-permute-start(f32[4,8,128]{2,1,0:T(8,128)} %vector_hbm.1), channel_id=1, source_target_pairs={{0,112},{16,32},{32,16},{48,64},{64,48},{80,96},{96,80},{112,0},{1... | collective-permute-start | bytes 49160 | tf_op jit(solution)/shard_map/ppermute | solution.py:394
  3.3 3.1 %collective-permute-start = (f32[4,8,128]{2,1,0:T(8,128)}, f32[4,8,128]{2,1,0:T(8,128)S(1)}, u32[]{:S(2)}, u32[]{:S(2)}) collective-permute-start(f32[4,8,128]{2,1,0:T(8,128)} %vector_hbm.1), channel_id=1, source_target_pairs={{0,16},{16,0},{32,48},{48,32},{64,80},{80,64},{96,112},{112,96},{1... | collective-permute-start | bytes 49160 | tf_op jit(solution)/shard_map/ppermute | solution.py:394
  6.4 9.5 %collective-permute-start.3 = (f32[5,8,128]{2,1,0:T(8,128)S(1)}, f32[5,8,128]{2,1,0:T(8,128)S(1)}, u32[]{:S(2)}, u32[]{:S(2)}) collective-permute-start(f32[5,8,128]{2,1,0:T(8,128)S(1)} %edges.2.vector.after.own), channel_id=1, source_target_pairs={{0,15},{1,2},{2,1},{3,4},{4,3},{5,6},{6,5},{7,8},{8,7},{9,10},{10,... | collective-permute-start | bytes 61448 | tf_op jit(solution)/shard_map/ppermute | solution.py:394
  12.7 3.2 %collective-permute-start.2 = (f32[5,8,128]{2,1,0:T(8,128)S(1)}, f32[5,8,128]{2,1,0:T(8,128)S(1)}, u32[]{:S(2)}, u32[]{:S(2)}) collective-permute-start(f32[5,8,128]{2,1,0:T(8,128)S(1)} %edges.2.vector.after.own), channel_id=1, source_target_pairs={{0,1},{1,0},{2,3},{3,2},{4,5},{5,4},{6,7},{7,6},{8,9},{9,8},{10,11... | collective-permute-start | bytes 61448 | tf_op jit(solution)/shard_map/ppermute | solution.py:394
  14.6 8.0 %copy-start = (f32[4,8,128]{2,1,0:T(8,128)S(1)}, f32[4,8,128]{2,1,0:T(8,128)}, u32[]{:S(2)}) copy-start(f32[4,8,128]{2,1,0:T(8,128)} %conductivity.3) | copy-start | bytes 49156
  14.7 8.0 %copy-start.1 = (s32[48]{0:T(128)S(1)}, s32[48]{0:T(128)}, u32[]{:S(2)}) copy-start(s32[48]{0:T(128)} %near_pair.3) | copy-start | bytes 580
  15.9 17.9 %all-to-all-start = ((f32[128,4,128]{2,1,0:T(4,128)}), f32[128,4,128]{2,1,0:T(4,128)S(1)}, u32[]{:S(2)}, u32[]{:S(2)}) async-start(f32[128,4,128]{2,1,0:T(4,128)} %first_expand.1), calls=%async_computation | async-start | bytes 524288 | tf_op jit(solution)/shard_map/all_to_all | solution.py:388
  34.1 3.0 %collective-permute-start.4 = (f32[4,128]{1,0:T(4,128)S(1)}, f32[4,128]{1,0:T(4,128)S(1)}, u32[]{:S(2)}, u32[]{:S(2)}) collective-permute-start(f32[4,128]{1,0:T(4,128)S(1)} %get-tuple-element.37), channel_id=1, source_target_pairs={{0,16},{16,0},{32,48},{48,32},{64,80},{80,64},{96,112},{112,96},{1... | collective-permute-start | bytes 6152 | tf_op jit(solution)/shard_map/ppermute | solution.py:394
  34.9 3.0 %collective-permute-start.5 = (f32[4,128]{1,0:T(4,128)S(1)}, f32[4,128]{1,0:T(4,128)S(1)}, u32[]{:S(2)}, u32[]{:S(2)}) collective-permute-start(f32[4,128]{1,0:T(4,128)S(1)} %get-tuple-element.38), channel_id=1, source_target_pairs={{0,112},{16,32},{32,16},{48,64},{64,48},{80,96},{96,80},{112,0},{1... | collective-permute-start | bytes 6152 | tf_op jit(solution)/shard_map/ppermute | solution.py:394
  37.9 6.0 %collective-permute-start.7 = (f32[5,8,128]{2,1,0:T(8,128)S(1)}, f32[5,8,128]{2,1,0:T(8,128)S(1)}, u32[]{:S(2)}, u32[]{:S(2)}) collective-permute-start(f32[5,8,128]{2,1,0:T(8,128)S(1)} %edges.3.vector.image.own), channel_id=1, source_target_pairs={{0,15},{1,2},{2,1},{3,4},{4,3},{5,6},{6,5},{7,8},{8,7},{9,10},{10,... | collective-permute-start | bytes 61448 | tf_op jit(solution)/shard_map/ppermute | solution.py:394
  39.1 4.7 %collective-permute-start.6 = (f32[5,8,128]{2,1,0:T(8,128)S(1)}, f32[5,8,128]{2,1,0:T(8,128)S(1)}, u32[]{:S(2)}, u32[]{:S(2)}) collective-permute-start(f32[5,8,128]{2,1,0:T(8,128)S(1)} %edges.3.vector.image.own), channel_id=1, source_target_pairs={{0,1},{1,0},{2,3},{3,2},{4,5},{5,4},{6,7},{7,6},{8,9},{9,8},{10,11... | collective-permute-start | bytes 61448 | tf_op jit(solution)/shard_map/ppermute | solution.py:394
  43.8 17.2 %all-to-all-start.1 = ((f32[128,4,128]{2,1,0:T(4,128)}), f32[128,4,128]{2,1,0:T(4,128)S(1)}, u32[]{:S(2)}, u32[]{:S(2)}) async-start(f32[128,4,128]{2,1,0:T(4,128)} %second_expand.1), calls=%async_computation.1 | async-start | bytes 524288 | tf_op jit(solution)/shard_map/all_to_all | solution.py:388
  49.7 0.7 copy-start.2

commit v7 on v6

--- a/solution.py
+++ b/solution.py
@@ -14,6 +14,8 @@
 HALO = 32
 NEAR_CHUNK = 8
 NEAR_CHUNKS = PAIRS // NEAR_CHUNK
+SMALL_CHUNK = 4
+SMALL_CHUNKS = PAIRS // SMALL_CHUNK
 FAR_CHUNK = 16
 FAR_CHUNKS = DEVICES // FAR_CHUNK
 FAR_PER_COPY = 2
@@ -139,9 +141,39 @@
     return total[0:8], total[0:8] + (total[8:16] + total[16:24])
 
 
-def near_copy(kernel_hbm, kernels, sems, n):
-    part = pl.ds(n * NEAR_CHUNK, NEAR_CHUNK)
+def near_copy(kernel_hbm, kernels, sems, n, size=NEAR_CHUNK):
+    part = pl.ds(n * size, size)
     return pltpu.make_async_copy(kernel_hbm.at[part], kernels.at[part], sems.at[n])
+
+
+def near_tiles(around, near_pair, kernel_hbm, kernels, sems, tiles):
+    def pair(p, carry):
+        @pl.when(lax.rem(p, SMALL_CHUNK) == 0)
+        def _():
+            near_copy(kernel_hbm, kernels, sems, p // SMALL_CHUNK, SMALL_CHUNK).wait()
+
+        code = near_pair[p]
+        t = code // 9
+        k = code - 9 * t
+        up = k // 3
+        source = (k - 3 * up) * 10 + t + up
+        rows = [around[b, pl.ds(source, 1), :] for b in range(3)]
+        for a in range(3):
+            for i in range(0, LEN, 16):
+                part = pl.ds(i, 16)
+                products = [kernels[p, a, b, part, :].astype(F32) * rows[b] for b in range(3)]
+                tiles[t, a, part, :] += products[0] + products[1] + products[2]
+        return carry
+
+    lax.fori_loop(0, PAIRS, pair, 0)
+
+
+def lane_sums(tiles, a):
+    ones = jnp.ones((8, LEN), BF16)
+    pieces = split3(tiles[:, a].reshape(ROWS * LEN, LEN))
+    low, mid, high = (lax.dot_general(ones, x, TRANS_B, preferred_element_type=F32) for x in reversed(pieces))
+    total = (low + mid) + high
+    return jnp.concatenate([total[0:1, t * LEN : (t + 1) * LEN] for t in range(ROWS)], axis=0)
 
 
 def far_copy(hbm, buffer, sems, n):
@@ -292,8 +324,7 @@
     out[4, 4:8, :] = jnp.where(strip < STRIPS - 1, below, 0.0)
 
 
-def local_part(near_pair, conductivity, own, swap_a, swap_b, kernel_hbm, rounded, full, around, kernels, sems):
-    start_near(kernel_hbm, kernels, sems)
+def gather_around(around, own, swap_a, swap_b):
     _, blk = place()
     even = lax.rem(blk, 2) == 0
     left = jnp.where(blk > 0, jnp.where(even, swap_b[...], swap_a[...]), 0.0)
@@ -303,6 +334,11 @@
         around[:, base + 1 : base + 9, :] = blocks[0:4]
         around[:, base, :] = blocks[4, 0:4]
         around[:, base + 9, :] = blocks[4, 4:8]
+
+
+def local_part(near_pair, conductivity, own, swap_a, swap_b, kernel_hbm, rounded, full, around, kernels, sems):
+    start_near(kernel_hbm, kernels, sems)
+    gather_around(around, own, swap_a, swap_b)
     flux_sum = flux(around, conductivity)
     rounded[3] = flux_sum
     full[3] = flux_sum
@@ -310,6 +346,23 @@
     for a in range(3):
         rounded[a] = near_rounded[:, a * LEN : (a + 1) * LEN]
         full[a] = near_full[:, a * LEN : (a + 1) * LEN]
+
+
+def second_local(
+    pair_hbm, conductivity, own, swap_a, swap_b, kernel_hbm, full, around, kernels, sems, near_pair, pair_sem, tiles
+):
+    pair_copy = pltpu.make_async_copy(pair_hbm, near_pair, pair_sem)
+    pair_copy.start()
+    for n in range(SMALL_CHUNKS):
+        near_copy(kernel_hbm, kernels, sems, n, SMALL_CHUNK).start()
+    gather_around(around, own, swap_a, swap_b)
+    full[3] = flux(around, conductivity)
+    for t in range(ROWS):
+        tiles[t] = jnp.zeros((3, LEN, LEN), F32)
+    pair_copy.wait()
+    near_tiles(around, near_pair, kernel_hbm, kernels, sems, tiles)
+    for a in range(3):
+        full[a] = lane_sums(tiles, a)
 
 
 def first_image(vector, local, received, image, far_part, to_even, to_odd):
@@ -509,7 +562,23 @@
     payload = expand_call(second_expand, in_specs=[VMEM] * 4, name="second_expand")(start, own, coefficients, left)
     payload, *sides = lax.optimization_barrier((payload, *sides))
     received_two = exchange(payload)
-    _, local_two = local_call()(near_pair, conductivity, own, *sides, near_kernel)
+    local_two = pl.pallas_call(
+        second_local,
+        out_shape=block,
+        in_specs=[HBM, VMEM, VMEM, VMEM, VMEM, HBM],
+        out_specs=VMEM,
+        scratch_shapes=[
+            pltpu.VMEM((4, HALO, LEN), F32),
+            pltpu.VMEM((PAIRS, 3, 3, LEN, LEN), BF16),
+            pltpu.SemaphoreType.DMA((SMALL_CHUNKS,)),
+            pltpu.SMEM((PAIRS,), jnp.int32),
+            pltpu.SemaphoreType.DMA,
+            pltpu.VMEM((ROWS, 3, LEN, LEN), F32),
+        ],
+        compiler_params=limit(24),
+        cost_estimate=pl.CostEstimate(flops=4 * 10**8, bytes_accessed=2 * 10**7, transcendentals=0),
+        name="second_local",
+    )(in_hbm(near_pair), conductivity, own, *sides, near_kernel)
     first, image_two, scalars, rows = pl.pallas_call(
         second_image,
         out_shape=(block, block, line, shape(DEVICES, LEN)),

time: 80.1 us -> 78 us (0.974)
  blocking collectives: 16.1 us -> 14.1 us
  waiting for transfers between devices: 10.3 us -> 12.3 us
  Pallas kernels: 26.8 us -> 25.5 us
    all_to_all x2, waiting for transfers between devices: 7.37 us -> 9.39 us  [exchange(): return lax.all_to_all(x, ('strip', 'blk'), 0, 0, tiled=True)]
    all_to_all x1, blocking collectives: 16.1 us -> 14.1 us  [exchange(): return lax.all_to_all(x, ('strip', 'blk'), 0, 0, tiled=True)]
    pallas_call x1, Pallas kernels: 7.57 us -> 6.22 us  [local(): pl.pallas_call(second_local, out_shape=block, in_specs=[HBM, VMEM, VMEM,...]
  transfers between devices with their start and end apart: 10 -> 10, of which waited for: 4 -> 4; matrix products, arithmetic and copies ran while one was open for 0% -> 0% of each run, Pallas kernels for 30% -> 29%
where the time goes in v7:
time: 78 us; the launch traced here: 77.7 us
  Pallas kernels  25.5 us (33%)
  starting transfers between devices  25 us (32%)
  blocking collectives  14.1 us (18%)
  waiting for transfers between devices  12.3 us (16%)
  between operations  0.8 us (1%)
    all_to_all x1, blocking collectives, exchange(): return lax.all_to_all(x, ('strip', 'blk'), 0, 0, tiled=True)  14.1 us
    all_to_all x2, starting transfers between devices, exchange(): return lax.all_to_all(x, ('strip', 'blk'), 0, 0, tiled=True)  12.6 us
    ppermute x8, starting transfers between devices, swaps(): return (lax.ppermute(x, axis, even), lax.ppermute(x, axis, odd))  12.4 us
    all_to_all x2, waiting for transfers between devices, exchange(): return lax.all_to_all(x, ('strip', 'blk'), 0, 0, tiled=True)  9.39 us
    pallas_call x1, Pallas kernels, local(): local_call()(near_pair, conductivity, start, *sides, near_kernel)  6.97 us
    pallas_call x1, Pallas kernels, local(): pl.pallas_call(second_local, out_shape=block, in_specs=[HBM, VMEM, VMEM,...  6.22 us
    ppermute x8, waiting for transfers between devices, swaps(): return (lax.ppermute(x, axis, even), lax.ppermute(x, axis, odd))  2.96 us
    pallas_call x1, Pallas kernels, local(): pl.pallas_call(bring, out_shape=(block, integers, integers, factors), in_...  1.97 us
  transfers between devices with their start and end apart: 10, of which 4 were waited for; matrix products, arithmetic and copies ran while one was open for 0% of the time, Pallas kernels for 29%

profile of v7, /device:TPU:1, one launch (start us, length us, event | category | flops | bytes accessed | tf_op | source)
XLA Modules:
  0.0 77.7 jit_solution(3599709515094063657)
XLA Ops:
  0.6 2.7 %collective-permute-start.1 = (f32[4,8,128]{2,1,0:T(8,128)}, f32[4,8,128]{2,1,0:T(8,128)S(1)}, u32[]{:S(2)}, u32[]{:S(2)}) collective-permute-start(f32[4,8,128]{2,1,0:T(8,128)} %vector_hbm.1), channel_id=1, source_target_pairs={{0,112},{16,32},{32,16},{48,64},{64,48},{80,96},{96,80},{112,0},{1... | collective-permute-start | bytes 49160 | tf_op jit(solution)/shard_map/ppermute | solution.py:447
  3.3 1.1 %collective-permute-start = (f32[4,8,128]{2,1,0:T(8,128)}, f32[4,8,128]{2,1,0:T(8,128)S(1)}, u32[]{:S(2)}, u32[]{:S(2)}) collective-permute-start(f32[4,8,128]{2,1,0:T(8,128)} %vector_hbm.1), channel_id=1, source_target_pairs={{0,16},{16,0},{32,48},{48,32},{64,80},{80,64},{96,112},{112,96},{1... | collective-permute-start | bytes 49160 | tf_op jit(solution)/shard_map/ppermute | solution.py:447
  4.4 2.0 %bring.1 = (f32[4,8,128]{2,1,0:T(8,128)S(1)}, s32[1,128]{1,0:T(1,128)S(1)}, s32[1,128]{1,0:T(1,128)S(1)}, bf16[128,3,32,128]{3,2,1,0:T(8,128)(2,1)S(1)}) custom-call(s32[1,128]{1,0:T(1,128)} %source_hbm.1, s32[1,128]{1,0:T(1,128)} %target_hbm.1, f32[4,8,128]{2,1,0:T(8,128)} %vector_hbm.1, bf16[128,3,32,128]{3,2,1,0:T(8,128)(2,1)} %bitcast.12), custom_call_target="tpu_custom_call" | custom-call | flops 200000000 | bytes 10000000 | tf_op jit(solution)/shard_map/bring/pallas_call | solution.py:503
  6.4 0.0 collective-permute-done.1.swap_b
  6.4 0.0 collective-permute-done.swap_a
  6.4 6.3 %collective-permute-start.3 = (f32[5,8,128]{2,1,0:T(8,128)S(1)}, f32[5,8,128]{2,1,0:T(8,128)S(1)}, u32[]{:S(2)}, u32[]{:S(2)}) collective-permute-start(f32[5,8,128]{2,1,0:T(8,128)S(1)} %edges.2.vector.after.own), channel_id=1, source_target_pairs={{0,15},{1,2},{2,1},{3,4},{4,3},{5,6},{6,5},{7,8},{8,7},{9,10},{10,... | collective-permute-start | bytes 61448 | tf_op jit(solution)/shard_map/ppermute | solution.py:447
  12.7 0.0 collective-permute-start.2
  12.7 1.9 %first_project.1 = (bf16[8,16,512]{2,1,0:T(8,128)(2,1)S(1)}, bf16[128,3,32,128]{3,2,1,0:T(8,128)(2,1)S(1)}) custom-call(s32[1,128]{1,0:T(1,128)S(1)} %get-tuple-element.25.after.source_row, f32[5,8,128]{2,1,0:T(8,128)S(1)} %edges.2.vector.after.own, bf16[128,3,32,128]{3,2,1,0:T(8,128)(2,1)S(1)} %get-tuple-element.27.right, bf16[128,3,32,128]{3,2,1,0:T(8,128)(2,1)} %bitcast.14), custom_call_target="tpu_custom_call" | custom-call | flops 200000000 | bytes 10000000 | tf_op jit(solution)/shard_map/first_project/pallas_call | solution.py:516
  14.6 0.0 copy-start
  14.7 0.0 copy-start.1
  14.7 1.2 %first_expand.1 = f32[128,4,128]{2,1,0:T(4,128)} custom-call(s32[1,128]{1,0:T(1,128)S(1)} %get-tuple-element.26.target_row, f32[5,8,128]{2,1,0:T(8,128)S(1)} %edges.2.vector.after.own, bf16[8,16,512]{2,1,0:T(8,128)(2,1)S(1)} %get-tuple-element.28.coefficients, bf16[128,3,32,128]{3,2,1,0:T(8,128)(2,1)S(1)} %get-tuple-element.29.left), custom_call_target="tpu_custom_call" | custom-call | flops 200000000 | bytes 10000000 | tf_op jit(solution)/shard_map/first_expand/pallas_call | solution.py:526
  15.9 0.0 collective-permute-done.3.swap_b
  15.9 0.0 collective-permute-done.2.swap_a
  15.9 6.7 %all-to-all-start = ((f32[128,4,128]{2,1,0:T(4,128)}), f32[128,4,128]{2,1,0:T(4,128)S(1)}, u32[]{:S(2)}, u32[]{:S(2)}) async-start(f32[128,4,128]{2,1,0:T(4,128)} %first_expand.1), calls=%async_computation | async-start | bytes 524288 | tf_op jit(solution)/shard_map/all_to_all | solution.py:441
  22.6 7.0 %local_part.1 = (f32[4,8,128]{2,1,0:T(8,128)S(1)}, f32[4,8,128]{2,1,0:T(8,128)S(1)}) custom-call(s32[48]{0:T(128)S(1)} %copy-done.1, f32[4,8,128]{2,1,0:T(8,128)S(1)} %copy-done, f32[5,8,128]{2,1,0:T(8,128)S(1)} %edges.2.vector.after.own, f32[5,8,128]{2,1,0:T(8,128)S(1)} %collective-permute-done.2.swap_a, f32[5,8,128]{2,1,0:T(8,128)S(1)} %collective-permute-done.3.swap_b, ...), custom_call_target="tpu_custom_call" | custom-call | flops 400000000 | bytes 20000000 | tf_op jit(solution)/shard_map/local_part/pallas_call | solution.py:529
  29.6 4.2 %all-to-all-done.received.target = f32[128,4,128]{2,1,0:T(4,128)S(1)} async-done(((f32[128,4,128]{2,1,0:T(4,128)}), f32[128,4,128]{2,1,0:T(4,128)S(1)}, u32[]{:S(2)}, u32[]{:S(2)}) %all-to-all-start) | async-done | bytes 262176 | tf_op jit(solution)/shard_map/all_to_all | solution.py:441
  33.9 0.2 first_image.1
  34.1 0.8 %collective-permute-start.4 = (f32[4,128]{1,0:T(4,128)S(1)}, f32[4,128]{1,0:T(4,128)S(1)}, u32[]{:S(2)}, u32[]{:S(2)}) collective-permute-start(f32[4,128]{1,0:T(4,128)S(1)} %get-tuple-element.36), channel_id=1, source_target_pairs={{0,16},{16,0},{32,48},{48,32},{64,80},{80,64},{96,112},{112,96},{1... | collective-permute-start | bytes 6152 | tf_op jit(solution)/shard_map/ppermute | solution.py:447
  34.9 0.3 collective-permute-start.5
  35.2 1.9 %bring_right.1.after.right = bf16[128,3,32,128]{3,2,1,0:T(8,128)(2,1)S(1)} custom-call(f32[4,8,128]{2,1,0:T(8,128)S(1)} %get-tuple-element.34.after.vector.image, bf16[128,3,32,128]{3,2,1,0:T(8,128)(2,1)} %bitcast.13), custom_call_target="tpu_custom_call" | custom-call | flops 200000000 | bytes 10000000 | tf_op jit(solution)/shard_map/bring_right/pallas_call | solution.py:539
  37.1 0.0 collective-permute-done.4.swap_a
  37.1 0.8 %collective-permute-done.5.swap_b = f32[4,128]{1,0:T(4,128)S(1)} collective-permute-done((f32[4,128]{1,0:T(4,128)S(1)}, f32[4,128]{1,0:T(4,128)S(1)}, u32[]{:S(2)}, u32[]{:S(2)}) %collective-permute-start.5) | collective-permute-done | bytes 2080 | tf_op jit(solution)/shard_map/ppermute | solution.py:447
  37.9 1.2 %collective-permute-start.7 = (f32[5,8,128]{2,1,0:T(8,128)S(1)}, f32[5,8,128]{2,1,0:T(8,128)S(1)}, u32[]{:S(2)}, u32[]{:S(2)}) collective-permute-start(f32[5,8,128]{2,1,0:T(8,128)S(1)} %edges.3.vector.image.own), channel_id=1, source_target_pairs={{0,15},{1,2},{2,1},{3,4},{4,3},{5,6},{6,5},{7,8},{8,7},{9,10},{10,... | collective-permute-start | bytes 61448 | tf_op jit(solution)/shard_map/ppermute | solution.py:447
  39.1 1.2 %second_project.1.coefficients = bf16[8,48,512]{2,1,0:T(8,128)(2,1)S(1)} custom-call(s32[1,128]{1,0:T(1,128)S(1)} %get-tuple-element.25.after.source_row, f32[5,8,128]{2,1,0:T(8,128)S(1)} %edges.3.vector.image.own, bf16[128,3,32,128]{3,2,1,0:T(8,128)(2,1)S(1)} %bring_right.1.after.right), custom_call_target="tpu_custom_call" | custom-call | flops 200000000 | bytes 10000000 | tf_op jit(solution)/shard_map/second_project/pallas_call | solution.py:552
  40.3 1.3 %second_expand.1 = f32[128,4,128]{2,1,0:T(4,128)} custom-call(f32[5,8,128]{2,1,0:T(8,128)S(1)} %edges.2.vector.after.own, f32[5,8,128]{2,1,0:T(8,128)S(1)} %edges.3.vector.image.own, bf16[8,48,512]{2,1,0:T(8,128)(2,1)S(1)} %second_project.1.coefficients, bf16[128,3,32,128]{3,2,1,0:T(8,128)(2,1)S(1)} %get-tuple-element.29.left), custom_call_target="tpu_custom_call" | custom-call | flops 200000000 | bytes 10000000 | tf_op jit(solution)/shard_map/second_expand/pallas_call | solution.py:562
  41.7 2.1 %collective-permute-done.7.swap_b = f32[5,8,128]{2,1,0:T(8,128)S(1)} collective-permute-done((f32[5,8,128]{2,1,0:T(8,128)S(1)}, f32[5,8,128]{2,1,0:T(8,128)S(1)}, u32[]{:S(2)}, u32[]{:S(2)}) %collective-permute-start.7) | collective-permute-done | bytes 20512 | tf_op jit(solution)/shard_map/ppermute | solution.py:447
  43.8 5.9 %all-to-all-start.1 = ((f32[128,4,128]{2,1,0:T(4,128)}), f32[128,4,128]{2,1,0:T(4,128)S(1)}, u32[]{:S(2)}, u32[]{:S(2)}) async-start(f32[128,4,128]{2,1,0:T(4,128)} %second_expand.1), calls=%async_computation.1 | async-start | bytes 524288 | tf_op jit(solution)/shard_map/all_to_all | solution.py:441
  49.7 6.2 %second_local.1.local_two = f32[4,8,128]{2,1,0:T(8,128)S(1)} custom-call(s32[48]{0:T(128)} %pair_hbm.1, f32[4,8,128]{2,1,0:T(8,128)S(1)} %copy-done, f32[5,8,128]{2,1,0:T(8,128)S(1)} %edges.3.vector.image.own, f32[5,8,128]{2,1,0:T(8,128)S(1)} %collective-permute-done.6.swap_a, f32[5,8,128]{2,1,0:T(8,128)S(1)} %collective-permute-done.7.swap_b, ...), custom_call_target="tpu_custom_call" | custom-call | flops 400000000 | bytes 20000000 | tf_op jit(solution)/shard_map/second_local/pallas_call | solution.py:565
  55.9 5.1 %all-to-all-done.1.received = f32[128,4,128]{2,1,0:T(4,128)S(1)} async-done(((f32[128,4,128]{2,1,0:T(4,128)}), f32[128,4,128]{2,1,0:T(4,128)S(1)}, u32[]{:S(2)}, u32[]{:S(2)}) %all-to-all-start.1) | async-done | bytes 262176 | tf_op jit(solution)/shard_map/all_to_all | solution.py:441
  61.1 1.1 %second_image.1 = (f32[4,8,128]{2,1,0:T(8,128)S(1)}, f32[4,8,128]{2,1,0:T(8,128)S(1)}, f32[1,128]{1,0:T(1,128)S(1)}, f32[128,128]{1,0:T(8,128)S(1)}) custom-call(f32[5,8,128]{2,1,0:T(8,128)S(1)} %edges.2.vector.after.own, f32[4,8,128]{2,1,0:T(8,128)S(1)} %get-tuple-element.34.after.vector.image, f32[4,8,128]{2,1,0:T(8,128)S(1)} %get-tuple-element.35.local_one, ...), custom_call_target="tpu_custom_call" | custom-call | tf_op jit(solution)/shard_map/second_image/pallas_call | solution.py:582
  62.2 14.1 %all_to_all.21 = f32[128,1,128]{2,1,0:T(1,128)S(1)} all-to-all(f32[128,1,128]{2,1,0:T(1,128)S(1)} %bitcast.11), channel_id=1, replica_groups=mesh['strip'=8,'blk'=16] {'strip','blk'}, dimensions={0} | all-to-all | bytes 131072 | tf_op jit(solution)/shard_map/all_to_all | solution.py:441
  76.3 1.4 %finish.1 = (f32[2,4,8,128]{3,2,1,0:T(8,128)}, f32[5]{0:T(128)}) custom-call(f32[5,8,128]{2,1,0:T(8,128)S(1)} %edges.2.vector.after.own, f32[4,8,128]{2,1,0:T(8,128)S(1)} %get-tuple-element.42.first, f32[4,8,128]{2,1,0:T(8,128)S(1)} %get-tuple-element.43.image, f32[1,128]{1,0:T(1,128)S(1)} %get-tuple-element.44.scalars, f32[128,128]{1,0:T(8,128)S(1)} %bitcast.10), custom_call_target="tpu_custom_call" | custom-call | tf_op jit(solution)/shard_map/finish/pallas_call | solution.py:591
  (6 shorter events, 0.0 us)
Async XLA Ops:
  0.6 5.8 %collective-permute-start.1 = (f32[4,8,128]{2,1,0:T(8,128)}, f32[4,8,128]{2,1,0:T(8,128)S(1)}, u32[]{:S(2)}, u32[]{:S(2)}) collective-permute-start(f32[4,8,128]{2,1,0:T(8,128)} %vector_hbm.1), channel_id=1, source_target_pairs={{0,112},{16,32},{32,16},{48,64},{64,48},{80,96},{96,80},{112,0},{1... | collective-permute-start | bytes 49160 | tf_op jit(solution)/shard_map/ppermute | solution.py:447
  3.3 3.1 %collective-permute-start = (f32[4,8,128]{2,1,0:T(8,128)}, f32[4,8,128]{2,1,0:T(8,128)S(1)}, u32[]{:S(2)}, u32[]{:S(2)}) collective-permute-start(f32[4,8,128]{2,1,0:T(8,128)} %vector_hbm.1), channel_id=1, source_target_pairs={{0,16},{16,0},{32,48},{48,32},{64,80},{80,64},{96,112},{112,96},{1... | collective-permute-start | bytes 49160 | tf_op jit(solution)/shard_map/ppermute | solution.py:447
  6.4 9.5 %collective-permute-start.3 = (f32[5,8,128]{2,1,0:T(8,128)S(1)}, f32[5,8,128]{2,1,0:T(8,128)S(1)}, u32[]{:S(2)}, u32[]{:S(2)}) collective-permute-start(f32[5,8,128]{2,1,0:T(8,128)S(1)} %edges.2.vector.after.own), channel_id=1, source_target_pairs={{0,15},{1,2},{2,1},{3,4},{4,3},{5,6},{6,5},{7,8},{8,7},{9,10},{10,... | collective-permute-start | bytes 61448 | tf_op jit(solution)/shard_map/ppermute | solution.py:447
  12.7 3.2 %collective-permute-start.2 = (f32[5,8,128]{2,1,0:T(8,128)S(1)}, f32[5,8,128]{2,1,0:T(8,128)S(1)}, u32[]{:S(2)}, u32[]{:S(2)}) collective-permute-start(f32[5,8,128]{2,1,0:T(8,128)S(1)} %edges.2.vector.after.own), channel_id=1, source_target_pairs={{0,1},{1,0},{2,3},{3,2},{4,5},{5,4},{6,7},{7,6},{8,9},{9,8},{10,11... | collective-permute-start | bytes 61448 | tf_op jit(solution)/shard_map/ppermute | solution.py:447
  14.6 8.0 %copy-start = (f32[4,8,128]{2,1,0:T(8,128)S(1)}, f32[4,8,128]{2,1,0:T(8,128)}, u32[]{:S(2)}) copy-start(f32[4,8,128]{2,1,0:T(8,128)} %conductivity.3) | copy-start | bytes 49156
  14.7 8.0 %copy-start.1 = (s32[48]{0:T(128)S(1)}, s32[48]{0:T(128)}, u32[]{:S(2)}) copy-start(s32[48]{0:T(128)} %pair_hbm.1) | copy-start | bytes 580
  15.9 17.9 %all-to-all-start = ((f32[128,4,128]{2,1,0:T(4,128)}), f32[128,4,128]{2,1,0:T(4,128)S(1)}, u32[]{:S(2)}, u32[]{:S(2)}) async-start(f32[128,4,128]{2,1,0:T(4,128)} %first_expand.1), calls=%async_computation | async-start | bytes 524288 | tf_op jit(solution)/shard_map/all_to_all | solution.py:441
  34.1 3.0 %collective-permute-start.4 = (f32[4,128]{1,0:T(4,128)S(1)}, f32[4,128]{1,0:T(4,128)S(1)}, u32[]{:S(2)}, u32[]{:S(2)}) collective-permute-start(f32[4,128]{1,0:T(4,128)S(1)} %get-tuple-element.36), channel_id=1, source_target_pairs={{0,16},{16,0},{32,48},{48,32},{64,80},{80,64},{96,112},{112,96},{1... | collective-permute-start | bytes 6152 | tf_op jit(solution)/shard_map/ppermute | solution.py:447
  34.9 3.0 %collective-permute-start.5 = (f32[4,128]{1,0:T(4,128)S(1)}, f32[4,128]{1,0:T(4,128)S(1)}, u32[]{:S(2)}, u32[]{:S(2)}) collective-permute-start(f32[4,128]{1,0:T(4,128)S(1)} %get-tuple-element.37), channel_id=1, source_target_pairs={{0,112},{16,32},{32,16},{48,64},{64,48},{80,96},{96,80},{112,0},{1... | collective-permute-start | bytes 6152 | tf_op jit(solution)/shard_map/ppermute | solution.py:447
  37.9 6.0 %collective-permute-start.7 = (f32[5,8,128]{2,1,0:T(8,128)S(1)}, f32[5,8,128]{2,1,0:T(8,128)S(1)}, u32[]{:S(2)}, u32[]{:S(2)}) collective-permute-start(f32[5,8,128]{2,1,0:T(8,128)S(1)} %edges.3.vector.image.own), channel_id=1, source_target_pairs={{0,15},{1,2},{2,1},{3,4},{4,3},{5,6},{6,5},{7,8},{8,7},{9,10},{10,... | collective-permute-start | bytes 61448 | tf_op jit(solution)/shard_map/ppermute | solution.py:447
  39.1 4.7 %collective-permute-start.6 = (f32[5,8,128]{2,1,0:T(8,128)S(1)}, f32[5,8,128]{2,1,0:T(8,128)S(1)}, u32[]{:S(2)}, u32[]{:S(2)}) collective-permute-start(f32[5,8,128]{2,1,0:T(8,128)S(1)} %edges.3.vector.image.own), channel_id=1, source_target_pairs={{0,1},{1,0},{2,3},{3,2},{4,5},{5,4},{6,7},{7,6},{8,9},{9,8},{10,11... | collective-permute-start | bytes 61448 | tf_op jit(solution)/shard_map/ppermute | solution.py:447
  43.8 17.2 %all-to-all-start.1 = ((f32[128,4,128]{2,1,0:T(4,128)}), f32[128,4,128]{2,1,0:T(4,128)S(1)}, u32[]{:S(2)}, u32[]{:S(2)}) async-start(f32[128,4,128]{2,1,0:T(4,128)} %second_expand.1), calls=%async_computation.1 | async-start | bytes 524288 | tf_op jit(solution)/shard_map/all_to_all | solution.py:441

commit v8 on v7

--- a/solution.py
+++ b/solution.py
@@ -133,12 +133,12 @@
             for b in range(3):
                 rows.append(jnp.where(sub == t, around[b, pl.ds(source, 1), :], 0.0))
                 matrices.append(kernels[p, :, b].reshape(3 * LEN, LEN))
-        left = jnp.concatenate(split3(jnp.concatenate(rows, axis=1)), axis=0)
+        left = jnp.concatenate(split3(jnp.concatenate(rows, axis=1))[:2], axis=0)
         matrix = jnp.concatenate(matrices, axis=1)
         return total + lax.dot_general(left, matrix, TRANS_B, preferred_element_type=F32)
 
-    total = lax.fori_loop(0, NEAR_CHUNKS, chunk, jnp.zeros((24, 3 * LEN), F32))
-    return total[0:8], total[0:8] + (total[8:16] + total[16:24])
+    total = lax.fori_loop(0, NEAR_CHUNKS, chunk, jnp.zeros((16, 3 * LEN), F32))
+    return total[0:8], total[0:8] + total[8:16]
 
 
 def near_copy(kernel_hbm, kernels, sems, n, size=NEAR_CHUNK):

time: 78 us -> 78 us (level)
  no operation moved by 1% of the time
where the time goes in v8:
time: 78 us; the launch traced here: 77.7 us
  Pallas kernels  25.2 us (32%)
  starting transfers between devices  24.7 us (32%)
  blocking collectives  14.1 us (18%)
  waiting for transfers between devices  12.9 us (17%)
  between operations  0.8 us (1%)
    all_to_all x1, blocking collectives, exchange(): return lax.all_to_all(x, ('strip', 'blk'), 0, 0, tiled=True)  14.1 us
    all_to_all x2, starting transfers between devices, exchange(): return lax.all_to_all(x, ('strip', 'blk'), 0, 0, tiled=True)  12.6 us
    ppermute x8, starting transfers between devices, swaps(): return (lax.ppermute(x, axis, even), lax.ppermute(x, axis, odd))  12.1 us
    all_to_all x2, waiting for transfers between devices, exchange(): return lax.all_to_all(x, ('strip', 'blk'), 0, 0, tiled=True)  9.68 us
    pallas_call x1, Pallas kernels, local(): local_call()(near_pair, conductivity, start, *sides, near_kernel)  6.7 us
    pallas_call x1, Pallas kernels, local(): pl.pallas_call(second_local, out_shape=block, in_specs=[HBM, VMEM, VMEM,...  6.22 us
    ppermute x8, waiting for transfers between devices, swaps(): return (lax.ppermute(x, axis, even), lax.ppermute(x, axis, odd))  3.23 us
    pallas_call x1, Pallas kernels, local(): pl.pallas_call(bring, out_shape=(block, integers, integers, factors), in_...  1.97 us
  transfers between devices with their start and end apart: 10, of which 4 were waited for; matrix products, arithmetic and copies ran while one was open for 0% of the time, Pallas kernels for 29%

profile of v8, /device:TPU:1, one launch (start us, length us, event | category | flops | bytes accessed | tf_op | source)
XLA Modules:
  0.0 77.7 jit_solution(14776650901605382414)
XLA Ops:
  0.6 2.7 %collective-permute-start.1 = (f32[4,8,128]{2,1,0:T(8,128)}, f32[4,8,128]{2,1,0:T(8,128)S(1)}, u32[]{:S(2)}, u32[]{:S(2)}) collective-permute-start(f32[4,8,128]{2,1,0:T(8,128)} %vector_hbm.1), channel_id=1, source_target_pairs={{0,112},{16,32},{32,16},{48,64},{64,48},{80,96},{96,80},{112,0},{1... | collective-permute-start | bytes 49160 | tf_op jit(solution)/shard_map/ppermute | solution.py:447
  3.3 1.1 %collective-permute-start = (f32[4,8,128]{2,1,0:T(8,128)}, f32[4,8,128]{2,1,0:T(8,128)S(1)}, u32[]{:S(2)}, u32[]{:S(2)}) collective-permute-start(f32[4,8,128]{2,1,0:T(8,128)} %vector_hbm.1), channel_id=1, source_target_pairs={{0,16},{16,0},{32,48},{48,32},{64,80},{80,64},{96,112},{112,96},{1... | collective-permute-start | bytes 49160 | tf_op jit(solution)/shard_map/ppermute | solution.py:447
  4.4 2.0 %bring.1 = (f32[4,8,128]{2,1,0:T(8,128)S(1)}, s32[1,128]{1,0:T(1,128)S(1)}, s32[1,128]{1,0:T(1,128)S(1)}, bf16[128,3,32,128]{3,2,1,0:T(8,128)(2,1)S(1)}) custom-call(s32[1,128]{1,0:T(1,128)} %source_hbm.1, s32[1,128]{1,0:T(1,128)} %target_hbm.1, f32[4,8,128]{2,1,0:T(8,128)} %vector_hbm.1, bf16[128,3,32,128]{3,2,1,0:T(8,128)(2,1)} %bitcast.12), custom_call_target="tpu_custom_call" | custom-call | flops 200000000 | bytes 10000000 | tf_op jit(solution)/shard_map/bring/pallas_call | solution.py:503
  6.4 0.0 collective-permute-done.1.swap_b
  6.4 0.0 collective-permute-done.swap_a
  6.4 6.3 %collective-permute-start.3 = (f32[5,8,128]{2,1,0:T(8,128)S(1)}, f32[5,8,128]{2,1,0:T(8,128)S(1)}, u32[]{:S(2)}, u32[]{:S(2)}) collective-permute-start(f32[5,8,128]{2,1,0:T(8,128)S(1)} %edges.2.vector.after.own), channel_id=1, source_target_pairs={{0,15},{1,2},{2,1},{3,4},{4,3},{5,6},{6,5},{7,8},{8,7},{9,10},{10,... | collective-permute-start | bytes 61448 | tf_op jit(solution)/shard_map/ppermute | solution.py:447
  12.7 0.0 collective-permute-start.2
  12.7 1.9 %first_project.1 = (bf16[8,16,512]{2,1,0:T(8,128)(2,1)S(1)}, bf16[128,3,32,128]{3,2,1,0:T(8,128)(2,1)S(1)}) custom-call(s32[1,128]{1,0:T(1,128)S(1)} %get-tuple-element.25.after.source_row, f32[5,8,128]{2,1,0:T(8,128)S(1)} %edges.2.vector.after.own, bf16[128,3,32,128]{3,2,1,0:T(8,128)(2,1)S(1)} %get-tuple-element.27.right, bf16[128,3,32,128]{3,2,1,0:T(8,128)(2,1)} %bitcast.14), custom_call_target="tpu_custom_call" | custom-call | flops 200000000 | bytes 10000000 | tf_op jit(solution)/shard_map/first_project/pallas_call | solution.py:516
  14.6 0.0 copy-start
  14.7 0.0 copy-start.1
  14.7 1.2 %first_expand.1 = f32[128,4,128]{2,1,0:T(4,128)} custom-call(s32[1,128]{1,0:T(1,128)S(1)} %get-tuple-element.26.target_row, f32[5,8,128]{2,1,0:T(8,128)S(1)} %edges.2.vector.after.own, bf16[8,16,512]{2,1,0:T(8,128)(2,1)S(1)} %get-tuple-element.28.coefficients, bf16[128,3,32,128]{3,2,1,0:T(8,128)(2,1)S(1)} %get-tuple-element.29.left), custom_call_target="tpu_custom_call" | custom-call | flops 200000000 | bytes 10000000 | tf_op jit(solution)/shard_map/first_expand/pallas_call | solution.py:526
  15.9 0.0 collective-permute-done.3.swap_b
  15.9 0.0 collective-permute-done.2.swap_a
  15.9 6.7 %all-to-all-start = ((f32[128,4,128]{2,1,0:T(4,128)}), f32[128,4,128]{2,1,0:T(4,128)S(1)}, u32[]{:S(2)}, u32[]{:S(2)}) async-start(f32[128,4,128]{2,1,0:T(4,128)} %first_expand.1), calls=%async_computation | async-start | bytes 524288 | tf_op jit(solution)/shard_map/all_to_all | solution.py:441
  22.6 6.7 %local_part.1 = (f32[4,8,128]{2,1,0:T(8,128)S(1)}, f32[4,8,128]{2,1,0:T(8,128)S(1)}) custom-call(s32[48]{0:T(128)S(1)} %copy-done.1, f32[4,8,128]{2,1,0:T(8,128)S(1)} %copy-done, f32[5,8,128]{2,1,0:T(8,128)S(1)} %edges.2.vector.after.own, f32[5,8,128]{2,1,0:T(8,128)S(1)} %collective-permute-done.2.swap_a, f32[5,8,128]{2,1,0:T(8,128)S(1)} %collective-permute-done.3.swap_b, ...), custom_call_target="tpu_custom_call" | custom-call | flops 400000000 | bytes 20000000 | tf_op jit(solution)/shard_map/local_part/pallas_call | solution.py:529
  29.3 4.5 %all-to-all-done.received.target = f32[128,4,128]{2,1,0:T(4,128)S(1)} async-done(((f32[128,4,128]{2,1,0:T(4,128)}), f32[128,4,128]{2,1,0:T(4,128)S(1)}, u32[]{:S(2)}, u32[]{:S(2)}) %all-to-all-start) | async-done | bytes 262176 | tf_op jit(solution)/shard_map/all_to_all | solution.py:441
  33.9 0.2 first_image.1
  34.1 0.8 %collective-permute-start.4 = (f32[4,128]{1,0:T(4,128)S(1)}, f32[4,128]{1,0:T(4,128)S(1)}, u32[]{:S(2)}, u32[]{:S(2)}) collective-permute-start(f32[4,128]{1,0:T(4,128)S(1)} %get-tuple-element.36), channel_id=1, source_target_pairs={{0,16},{16,0},{32,48},{48,32},{64,80},{80,64},{96,112},{112,96},{1... | collective-permute-start | bytes 6152 | tf_op jit(solution)/shard_map/ppermute | solution.py:447
  34.9 0.3 collective-permute-start.5
  35.2 1.9 %bring_right.1.after.right = bf16[128,3,32,128]{3,2,1,0:T(8,128)(2,1)S(1)} custom-call(f32[4,8,128]{2,1,0:T(8,128)S(1)} %get-tuple-element.34.after.vector.image, bf16[128,3,32,128]{3,2,1,0:T(8,128)(2,1)} %bitcast.13), custom_call_target="tpu_custom_call" | custom-call | flops 200000000 | bytes 10000000 | tf_op jit(solution)/shard_map/bring_right/pallas_call | solution.py:539
  37.1 0.0 collective-permute-done.4.swap_a
  37.1 0.8 %collective-permute-done.5.swap_b = f32[4,128]{1,0:T(4,128)S(1)} collective-permute-done((f32[4,128]{1,0:T(4,128)S(1)}, f32[4,128]{1,0:T(4,128)S(1)}, u32[]{:S(2)}, u32[]{:S(2)}) %collective-permute-start.5) | collective-permute-done | bytes 2080 | tf_op jit(solution)/shard_map/ppermute | solution.py:447
  37.9 1.0 %collective-permute-start.7 = (f32[5,8,128]{2,1,0:T(8,128)S(1)}, f32[5,8,128]{2,1,0:T(8,128)S(1)}, u32[]{:S(2)}, u32[]{:S(2)}) collective-permute-start(f32[5,8,128]{2,1,0:T(8,128)S(1)} %edges.3.vector.image.own), channel_id=1, source_target_pairs={{0,15},{1,2},{2,1},{3,4},{4,3},{5,6},{6,5},{7,8},{8,7},{9,10},{10,... | collective-permute-start | bytes 61448 | tf_op jit(solution)/shard_map/ppermute | solution.py:447
  38.9 1.2 %second_project.1.coefficients = bf16[8,48,512]{2,1,0:T(8,128)(2,1)S(1)} custom-call(s32[1,128]{1,0:T(1,128)S(1)} %get-tuple-element.25.after.source_row, f32[5,8,128]{2,1,0:T(8,128)S(1)} %edges.3.vector.image.own, bf16[128,3,32,128]{3,2,1,0:T(8,128)(2,1)S(1)} %bring_right.1.after.right), custom_call_target="tpu_custom_call" | custom-call | flops 200000000 | bytes 10000000 | tf_op jit(solution)/shard_map/second_project/pallas_call | solution.py:552
  40.1 1.3 %second_expand.1 = f32[128,4,128]{2,1,0:T(4,128)} custom-call(f32[5,8,128]{2,1,0:T(8,128)S(1)} %edges.2.vector.after.own, f32[5,8,128]{2,1,0:T(8,128)S(1)} %edges.3.vector.image.own, bf16[8,48,512]{2,1,0:T(8,128)(2,1)S(1)} %second_project.1.coefficients, bf16[128,3,32,128]{3,2,1,0:T(8,128)(2,1)S(1)} %get-tuple-element.29.left), custom_call_target="tpu_custom_call" | custom-call | flops 200000000 | bytes 10000000 | tf_op jit(solution)/shard_map/second_expand/pallas_call | solution.py:562
  41.4 2.4 %collective-permute-done.7.swap_b = f32[5,8,128]{2,1,0:T(8,128)S(1)} collective-permute-done((f32[5,8,128]{2,1,0:T(8,128)S(1)}, f32[5,8,128]{2,1,0:T(8,128)S(1)}, u32[]{:S(2)}, u32[]{:S(2)}) %collective-permute-start.7) | collective-permute-done | bytes 20512 | tf_op jit(solution)/shard_map/ppermute | solution.py:447
  43.8 5.9 %all-to-all-start.1 = ((f32[128,4,128]{2,1,0:T(4,128)}), f32[128,4,128]{2,1,0:T(4,128)S(1)}, u32[]{:S(2)}, u32[]{:S(2)}) async-start(f32[128,4,128]{2,1,0:T(4,128)} %second_expand.1), calls=%async_computation.1 | async-start | bytes 524288 | tf_op jit(solution)/shard_map/all_to_all | solution.py:441
  49.7 6.2 %second_local.1.local_two = f32[4,8,128]{2,1,0:T(8,128)S(1)} custom-call(s32[48]{0:T(128)} %pair_hbm.1, f32[4,8,128]{2,1,0:T(8,128)S(1)} %copy-done, f32[5,8,128]{2,1,0:T(8,128)S(1)} %edges.3.vector.image.own, f32[5,8,128]{2,1,0:T(8,128)S(1)} %collective-permute-done.6.swap_a, f32[5,8,128]{2,1,0:T(8,128)S(1)} %collective-permute-done.7.swap_b, ...), custom_call_target="tpu_custom_call" | custom-call | flops 400000000 | bytes 20000000 | tf_op jit(solution)/shard_map/second_local/pallas_call | solution.py:565
  55.9 5.2 %all-to-all-done.1.received = f32[128,4,128]{2,1,0:T(4,128)S(1)} async-done(((f32[128,4,128]{2,1,0:T(4,128)}), f32[128,4,128]{2,1,0:T(4,128)S(1)}, u32[]{:S(2)}, u32[]{:S(2)}) %all-to-all-start.1) | async-done | bytes 262176 | tf_op jit(solution)/shard_map/all_to_all | solution.py:441
  61.1 1.1 %second_image.1 = (f32[4,8,128]{2,1,0:T(8,128)S(1)}, f32[4,8,128]{2,1,0:T(8,128)S(1)}, f32[1,128]{1,0:T(1,128)S(1)}, f32[128,128]{1,0:T(8,128)S(1)}) custom-call(f32[5,8,128]{2,1,0:T(8,128)S(1)} %edges.2.vector.after.own, f32[4,8,128]{2,1,0:T(8,128)S(1)} %get-tuple-element.34.after.vector.image, f32[4,8,128]{2,1,0:T(8,128)S(1)} %get-tuple-element.35.local_one, ...), custom_call_target="tpu_custom_call" | custom-call | tf_op jit(solution)/shard_map/second_image/pallas_call | solution.py:582
  62.2 14.1 %all_to_all.21 = f32[128,1,128]{2,1,0:T(1,128)S(1)} all-to-all(f32[128,1,128]{2,1,0:T(1,128)S(1)} %bitcast.11), channel_id=1, replica_groups=mesh['strip'=8,'blk'=16] {'strip','blk'}, dimensions={0} | all-to-all | bytes 131072 | tf_op jit(solution)/shard_map/all_to_all | solution.py:441
  76.3 1.4 %finish.1 = (f32[2,4,8,128]{3,2,1,0:T(8,128)}, f32[5]{0:T(128)}) custom-call(f32[5,8,128]{2,1,0:T(8,128)S(1)} %edges.2.vector.after.own, f32[4,8,128]{2,1,0:T(8,128)S(1)} %get-tuple-element.42.first, f32[4,8,128]{2,1,0:T(8,128)S(1)} %get-tuple-element.43.image, f32[1,128]{1,0:T(1,128)S(1)} %get-tuple-element.44.scalars, f32[128,128]{1,0:T(8,128)S(1)} %bitcast.10), custom_call_target="tpu_custom_call" | custom-call | tf_op jit(solution)/shard_map/finish/pallas_call | solution.py:591
  (6 shorter events, 0.0 us)
Async XLA Ops:
  0.6 5.8 %collective-permute-start.1 = (f32[4,8,128]{2,1,0:T(8,128)}, f32[4,8,128]{2,1,0:T(8,128)S(1)}, u32[]{:S(2)}, u32[]{:S(2)}) collective-permute-start(f32[4,8,128]{2,1,0:T(8,128)} %vector_hbm.1), channel_id=1, source_target_pairs={{0,112},{16,32},{32,16},{48,64},{64,48},{80,96},{96,80},{112,0},{1... | collective-permute-start | bytes 49160 | tf_op jit(solution)/shard_map/ppermute | solution.py:447
  3.3 3.1 %collective-permute-start = (f32[4,8,128]{2,1,0:T(8,128)}, f32[4,8,128]{2,1,0:T(8,128)S(1)}, u32[]{:S(2)}, u32[]{:S(2)}) collective-permute-start(f32[4,8,128]{2,1,0:T(8,128)} %vector_hbm.1), channel_id=1, source_target_pairs={{0,16},{16,0},{32,48},{48,32},{64,80},{80,64},{96,112},{112,96},{1... | collective-permute-start | bytes 49160 | tf_op jit(solution)/shard_map/ppermute | solution.py:447
  6.4 9.5 %collective-permute-start.3 = (f32[5,8,128]{2,1,0:T(8,128)S(1)}, f32[5,8,128]{2,1,0:T(8,128)S(1)}, u32[]{:S(2)}, u32[]{:S(2)}) collective-permute-start(f32[5,8,128]{2,1,0:T(8,128)S(1)} %edges.2.vector.after.own), channel_id=1, source_target_pairs={{0,15},{1,2},{2,1},{3,4},{4,3},{5,6},{6,5},{7,8},{8,7},{9,10},{10,... | collective-permute-start | bytes 61448 | tf_op jit(solution)/shard_map/ppermute | solution.py:447
  12.7 3.2 %collective-permute-start.2 = (f32[5,8,128]{2,1,0:T(8,128)S(1)}, f32[5,8,128]{2,1,0:T(8,128)S(1)}, u32[]{:S(2)}, u32[]{:S(2)}) collective-permute-start(f32[5,8,128]{2,1,0:T(8,128)S(1)} %edges.2.vector.after.own), channel_id=1, source_target_pairs={{0,1},{1,0},{2,3},{3,2},{4,5},{5,4},{6,7},{7,6},{8,9},{9,8},{10,11... | collective-permute-start | bytes 61448 | tf_op jit(solution)/shard_map/ppermute | solution.py:447
  14.6 8.0 %copy-start = (f32[4,8,128]{2,1,0:T(8,128)S(1)}, f32[4,8,128]{2,1,0:T(8,128)}, u32[]{:S(2)}) copy-start(f32[4,8,128]{2,1,0:T(8,128)} %conductivity.3) | copy-start | bytes 49156
  14.7 8.0 %copy-start.1 = (s32[48]{0:T(128)S(1)}, s32[48]{0:T(128)}, u32[]{:S(2)}) copy-start(s32[48]{0:T(128)} %pair_hbm.1) | copy-start | bytes 580
  15.9 17.9 %all-to-all-start = ((f32[128,4,128]{2,1,0:T(4,128)}), f32[128,4,128]{2,1,0:T(4,128)S(1)}, u32[]{:S(2)}, u32[]{:S(2)}) async-start(f32[128,4,128]{2,1,0:T(4,128)} %first_expand.1), calls=%async_computation | async-start | bytes 524288 | tf_op jit(solution)/shard_map/all_to_all | solution.py:441
  34.1 3.0 %collective-permute-start.4 = (f32[4,128]{1,0:T(4,128)S(1)}, f32[4,128]{1,0:T(4,128)S(1)}, u32[]{:S(2)}, u32[]{:S(2)}) collective-permute-start(f32[4,128]{1,0:T(4,128)S(1)} %get-tuple-element.36), channel_id=1, source_target_pairs={{0,16},{16,0},{32,48},{48,32},{64,80},{80,64},{96,112},{112,96},{1... | collective-permute-start | bytes 6152 | tf_op jit(solution)/shard_map/ppermute | solution.py:447
  34.9 3.0 %collective-permute-start.5 = (f32[4,128]{1,0:T(4,128)S(1)}, f32[4,128]{1,0:T(4,128)S(1)}, u32[]{:S(2)}, u32[]{:S(2)}) collective-permute-start(f32[4,128]{1,0:T(4,128)S(1)} %get-tuple-element.37), channel_id=1, source_target_pairs={{0,112},{16,32},{32,16},{48,64},{64,48},{80,96},{96,80},{112,0},{1... | collective-permute-start | bytes 6152 | tf_op jit(solution)/shard_map/ppermute | solution.py:447
  37.9 6.0 %collective-permute-start.7 = (f32[5,8,128]{2,1,0:T(8,128)S(1)}, f32[5,8,128]{2,1,0:T(8,128)S(1)}, u32[]{:S(2)}, u32[]{:S(2)}) collective-permute-start(f32[5,8,128]{2,1,0:T(8,128)S(1)} %edges.3.vector.image.own), channel_id=1, source_target_pairs={{0,15},{1,2},{2,1},{3,4},{4,3},{5,6},{6,5},{7,8},{8,7},{9,10},{10,... | collective-permute-start | bytes 61448 | tf_op jit(solution)/shard_map/ppermute | solution.py:447
  38.8 5.0 %collective-permute-start.6 = (f32[5,8,128]{2,1,0:T(8,128)S(1)}, f32[5,8,128]{2,1,0:T(8,128)S(1)}, u32[]{:S(2)}, u32[]{:S(2)}) collective-permute-start(f32[5,8,128]{2,1,0:T(8,128)S(1)} %edges.3.vector.image.own), channel_id=1, source_target_pairs={{0,1},{1,0},{2,3},{3,2},{4,5},{5,4},{6,7},{7,6},{8,9},{9,8},{10,11... | collective-permute-start | bytes 61448 | tf_op jit(solution)/shard_map/ppermute | solution.py:447
  43.8 17.2 %all-to-all-start.1 = ((f32[128,4,128]{2,1,0:T(4,128)}), f32[128,4,128]{2,1,0:T(4,128)S(1)}, u32[]{:S(2)}, u32[]{:S(2)}) async-start(f32[128,4,128]{2,1,0:T(4,128)} %second_expand.1), calls=%async_computation.1 | async-start | bytes 524288 | tf_op jit(solution)/shard_map/all_to_all | solution.py:441
